TPU v7x, 32 devices: a whole 2x2x4 slice. The times are simulated.
32 devices in a mesh: af: 4 (over z), row: 8 (over y, x, core).
Axes of the slice: x: 2, y: 2, z: 4, core: 2. Of those that a mesh axis runs over, the one named last changes fastest.
Arguments:
- image_in: bfloat16 [10, 2, 20, 256, 256], P(None, None, 'af', 'row'), may hold values from -6 to 6
- measured: float32 [10, 20, 256, 512], P(None, None, ('af', 'row')), may hold values from -6 to 6
- target: float32 [10, 20, 256, 512], P(None, None, ('af', 'row')), may hold values from -6 to 6
- line_mask: int32 [20, 256], P(None, ('af', 'row')), may hold values from 0 to 1, as said below
- window_half: int32 [20], replicated, may hold values from 0 to 2
- in_kernel: float32 [64, 54], replicated, may hold values from -0.875 to 0.875
- out_kernel: float32 [27, 2, 64], replicated, may hold values from -0.15625 to 0.15625
- biases: float32 [66], replicated, may hold values from -1 to 1
- in_moment: float32 [64, 54], replicated, may hold values from -0.00012207031 to 0.00012207031
- out_moment: float32 [27, 2, 64], replicated, may hold values from -0.00061035156 to 0.00061035156
- bias_moment: float32 [66], replicated, may hold values from -0.0004272461 to 0.0004272461
- in_square: float32 [64, 54], replicated, may hold values from 6.866455e-11 to 2.746582e-10
- out_square: float32 [27, 2, 64], replicated, may hold values from 1.7166137e-09 to 6.866455e-09
- bias_square: float32 [66], replicated, may hold values from 7.6293943e-10 to 3.0517577e-09
- in_smooth: float32 [64, 54], replicated, may hold values from -0.875 to 0.875
- out_smooth: float32 [27, 2, 64], replicated, may hold values from -0.15625 to 0.15625
- bias_smooth: float32 [66], replicated, may hold values from -1 to 1
Outputs:
- loss_total: float32 [], replicated
- unsampled_count: float32 [], replicated
- in_first: float32 [64, 54], replicated
- out_first: float32 [27, 2, 64], replicated
- bias_first: float32 [66], replicated
- in_second: float32 [64, 54], replicated
- out_second: float32 [27, 2, 64], replicated
- bias_second: float32 [66], replicated
- in_master: float32 [64, 54], replicated
- out_master: float32 [27, 2, 64], replicated
- bias_master: float32 [66], replicated
- in_average: float32 [64, 54], replicated
- out_average: float32 [27, 2, 64], replicated
- bias_average: float32 [66], replicated
- in_copy: bfloat16 [64, 54], replicated
- out_copy: bfloat16 [27, 2, 64], replicated
- bias_copy: bfloat16 [66], replicated
Inputs may be any that keep to these rules, and one draw needn't show every extreme that they name: `line_mask`: 1 where line ky of frame t is sampled; line 256 - 1 is unsampled in every frame.
All inputs are finite; a program needn't handle non-finite values.
Results may differ from a plain program's by a relative error of at most 0.004.
The roundings to bfloat16 on the way count: a program that leaves them out, or rounds other values in their place, can miss the bound.
Values may be sent and summed in bfloat16 or wider, within the bound.
No kernel may reach another device: no remote copies, remote signals or barrier semaphores. Data moves between devices by JAX's collectives and lax.ppermute only.
A program may use at most 128 MiB of HBM per device.

v0:
```python
import functools
import math

import jax
import jax.numpy as jnp
import numpy as np
from jax import lax
from jax.experimental import pallas as pl
from jax.experimental.pallas import tpu as pltpu
from jax.sharding import PartitionSpec as P

STEP = 5
AXES = ("af", "row")
BLOCK = 4
WIN = 8
SIDE = 16
DEPTH = 9 * SIDE
ONES_ROW = BLOCK + 2
PACKED = 128
EDGES = 6
BIAS_LANE = WIN - 1
VMEM = 60 * 2**20
GELU = math.sqrt(2.0 / math.pi)
CUBE = 0.044715

beta_first = 0.5
beta_second = 0.5
rate_in = 0.2
rate_out = 0.04
rate_bias = 0.3
decay_weight = 0.01
average_keep = 0.9
epsilon = 1e-08

NT = (((1,), (1,)), ((), ()))
TN = (((0,), (0,)), ((), ()))


def dft_table(length):
    index = np.arange(length)
    phase = (index[:, None] * index[None, :] % length) * (2.0 * math.pi / length)
    cosine = np.cos(phase) / math.sqrt(length)
    sine = np.sin(phase) / math.sqrt(length)
    upper = np.concatenate([cosine, -sine], axis=1)
    lower = np.concatenate([sine, cosine], axis=1)
    return np.concatenate([upper, lower], axis=0).astype(np.float32)


def share_matrix(window_half, frames):
    index = jnp.arange(frames, dtype=jnp.int32)
    inside = (jnp.abs(index[None, :] - index[:, None]) <= window_half[:, None]).astype(jnp.float32)
    return inside / jnp.sum(inside, axis=1, keepdims=True)


def adam_step(master, grad, first, second, rate):
    first_new = beta_first * first + (1.0 - beta_first) * grad
    second_new = beta_second * second + (1.0 - beta_second) * grad * grad
    first_hat = first_new / (1.0 - beta_first**STEP)
    second_hat = second_new / (1.0 - beta_second**STEP)
    master_new = master - rate * (
        first_hat / (jnp.sqrt(second_hat) + epsilon) + decay_weight * master
    )
    return (first_new, second_new, master_new)


def conv_in_weights(kernel, bias):
    width = kernel.shape[0]
    taps = kernel.astype(jnp.bfloat16).astype(jnp.float32).reshape(width, 2, 3, 3, 3)
    rows = []
    for j in range(BLOCK):
        row = jnp.pad(taps, ((0, 0), (0, 0), (0, 0), (j, WIN - 3 - j), (0, 0)))
        rows.append(row.transpose(0, 2, 4, 1, 3))
    spread = jnp.stack(rows)
    high = lax.reduce_precision(bias, 8, 7)
    rest = bias - high
    middle = lax.reduce_precision(rest, 8, 7)
    parts = jnp.stack([high, middle, rest - middle], axis=1)
    spread = spread.at[:, :, :, 0, 0, ONES_ROW].set(jnp.broadcast_to(parts, (BLOCK, width, 3)))
    return 0.5 * spread.reshape(BLOCK * width, DEPTH)


def conv_out_weights(kernel):
    width = kernel.shape[2]
    taps = kernel.astype(jnp.bfloat16).reshape(3, 3, 3, 2, width)[:, ::-1]
    columns = []
    for j in range(BLOCK):
        column = jnp.pad(taps, ((0, 0), (j, WIN - 3 - j), (0, 0), (0, 0), (0, 0)))
        columns.append(column.transpose(0, 2, 3, 1, 4))
    return jnp.stack(columns, axis=4).reshape(DEPTH, BLOCK * width)


def conv_back_weights(kernel):
    width = kernel.shape[2]
    taps = kernel.astype(jnp.bfloat16).reshape(3, 3, 3, 2, width)[::-1, ::-1, ::-1]
    rows = []
    for j in range(BLOCK):
        row = jnp.pad(taps, ((0, 0), (j, WIN - 3 - j), (0, 0), (0, 0), (0, 0)))
        rows.append(row.transpose(0, 2, 3, 1, 4))
    return 0.5 * jnp.stack(rows, axis=4).reshape(DEPTH, BLOCK * width)


def pick_table():
    table = np.zeros((2, 256, PACKED), np.float32)
    for a, b, e, c in np.ndindex(3, 3, 3, 2):
        lane = ((a * 3 + e) * 2 + c) * WIN + b
        table[0, lane, 27 * c + 9 * a + 3 * b + e] = 1.0
        tap = 9 * (2 - a) + 3 * (2 - b) + 2 - e
        table[1, lane, PACKED // 2 + 2 * tap + c] = 1.0
    table[0, BIAS_LANE, 54] = 1.0
    return jnp.asarray(table, jnp.bfloat16)


def load_volume(volume, own, below, above, left, right, corner_below, corner_above):
    _, channels, frames, rows, columns = own.shape
    lanes = (frames + 2) * columns
    for c in range(channels):
        volume[c, rows + 8 : rows + 16, :] = jnp.zeros((8, lanes), jnp.float32)
        for t in range(frames + 2):
            if t == 0:
                piece = below[0, c]
            elif t == frames + 1:
                piece = above[0, c]
            else:
                piece = own[0, c, t - 1]
            volume[c, 8 : 8 + rows, t * columns : (t + 1) * columns] = piece.astype(jnp.float32)
    low = corner_below[0].astype(jnp.float32)
    high = corner_above[0].astype(jnp.float32)
    for side, at, line in ((0, 7, left), (1, rows + 8, right)):
        middle = line[0].astype(jnp.float32)
        for c in range(channels):
            k = 2 * side + c
            volume[c, at : at + 1, 0:columns] = low[k : k + 1]
            volume[c, at : at + 1, columns : lanes - columns] = middle[c : c + 1]
            volume[c, at : at + 1, lanes - columns :] = high[k : k + 1]


def build_windows(volume, windows, columns, ones):
    blocks, _, lanes = windows.shape
    column = lax.broadcasted_iota(jnp.int32, (SIDE, columns), 1)
    row = lax.broadcasted_iota(jnp.int32, (SIDE, columns), 0)
    zero = jnp.zeros((SIDE, columns), jnp.bfloat16)
    for block in range(blocks):
        for t in range(lanes // columns):
            here = slice(t * columns, (t + 1) * columns)
            start = 7 + BLOCK * block
            window = jnp.concatenate(
                [volume[c, start : start + WIN, here] for c in range(2)], axis=0
            ).astype(jnp.bfloat16)
            for e in range(3):
                shifted = window
                if e != 1:
                    shifted = pltpu.roll(window, (1 - e) % columns, axis=1)
                    shifted = jnp.where(column == (0 if e == 0 else columns - 1), zero, shifted)
                if ones and e == 0:
                    shifted = jnp.where(row == ONES_ROW, zero + 1.0, shifted)
                windows[block, e * SIDE : (e + 1) * SIDE, here] = shifted


def forward_kernel(
    own, *refs,
):
    edges, refs = refs[:EDGES], refs[EDGES:]
    (
    w_in, w_out, bias_out,
    main, part_below, part_above, part_left, part_right,
    volume, windows, total, hidden, mixed, spread,
    ) = refs
    _, _, frames, rows, columns = own.shape
    blocks = windows.shape[0]
    load_volume(volume, own, *edges)
    build_windows(volume, windows, columns, True)
    column = lax.broadcasted_iota(jnp.int32, (SIDE, columns), 1)

    def step(block, carry):
        for f in range(frames):
            here = slice(f * columns, (f + 1) * columns)
            patch = jnp.concatenate(
                [windows[block, :, (f + a) * columns : (f + a + 1) * columns] for a in range(3)],
                axis=0,
            )
            half = jnp.dot(w_in[...], patch, preferred_element_type=jnp.float32)
            t = jnp.tanh(half * (2.0 * GELU + (8.0 * GELU * CUBE) * (half * half)))
            hidden[:, here] = (half + half * t).astype(jnp.bfloat16)
        for f in range(frames):
            here = slice(f * columns, (f + 1) * columns)
            mixed[f] = jnp.dot(w_out[...], hidden[:, here], preferred_element_type=jnp.float32)
        for t in range(frames + 2):
            window = None
            for e in range(3):
                summed = None
                for a in range(3):
                    f = t - 2 + a
                    if 0 <= f < frames:
                        start = (a * 3 + e) * SIDE
                        piece = mixed[f, start : start + SIDE, :]
                        summed = piece if summed is None else summed + piece
                if e != 1:
                    summed = pltpu.roll(summed, (1 - e) % columns, axis=1)
                    summed = jnp.where(column == (0 if e == 0 else columns - 1), 0.0, summed)
                window = summed if window is None else window + summed
            spread[block, :, t * columns : (t + 1) * columns] = window
        return carry

    lax.fori_loop(0, blocks, step, 0, unroll=True)
    total[...] = jnp.zeros_like(total)
    for block in range(blocks):
        for o in range(2):
            start = 7 + BLOCK * block
            total[o, start : start + WIN, :] = (
                total[o, start : start + WIN, :] + spread[block, o * WIN : (o + 1) * WIN, :]
            )
    for o in range(2):
        for t in range(frames + 2):
            here = total[o, 8 : 8 + rows, t * columns : (t + 1) * columns]
            if t == 0:
                part_below[0, o] = here.astype(jnp.bfloat16)
            elif t == frames + 1:
                part_above[0, o] = here.astype(jnp.bfloat16)
            else:
                base = volume[o, 8 : 8 + rows, t * columns : (t + 1) * columns] + bias_out[o]
                main[0, t - 1, :, o * columns : (o + 1) * columns] = base + here
    for at, out in ((7, part_left), (8 + rows, part_right)):
        both = [total[o, at : at + 1, :] for o in range(2)]
        out[0] = jnp.concatenate(both, axis=0).astype(jnp.bfloat16)


def patches(source, block, frames, columns):
    return jnp.concatenate(
        [source[block, :, a * columns : (a + frames) * columns] for a in range(3)], axis=0
    )


def hidden_kernel(own, *refs):
    edges, (w_in, *_, hidden, slopes, volume, windows) = refs[:EDGES], refs[EDGES:]
    _, _, frames, rows, columns = own.shape
    load_volume(volume, own, *edges)
    build_windows(volume, windows, columns, True)

    def step(block, carry):
        patch = patches(windows, block, frames, columns)
        for f in range(frames):
            here = slice(f * columns, (f + 1) * columns)
            half = lax.dot_general(
                patch[:, here], w_in[...], TN, preferred_element_type=jnp.float32
            )
            u = half * half
            t = jnp.tanh(half * (2.0 * GELU + (8.0 * GELU * CUBE) * u))
            up = 1.0 + t
            hidden[0, block, here, :] = (half * up).astype(jnp.bfloat16)
            slope = half * (2.0 * GELU + (24.0 * GELU * CUBE) * u)
            slopes[0, block, here, :] = (up + (up * (1.0 - t)) * slope).astype(jnp.bfloat16)
        return carry

    lax.fori_loop(0, windows.shape[0], step, 0, unroll=True)


def backward_kernel(
    own, *refs,
):
    edges, grad, grad_edges = refs[:EDGES], refs[EDGES], refs[EDGES + 1 : 2 * EDGES + 1]
    (
        hidden, slopes, w_back, pick, extras, out,
        volume, windows, grad_windows, grads, sum_in, sum_out,
    ) = refs[2 * EDGES + 1 :]
    _, _, frames, rows, columns = own.shape

    part = pl.program_id(1)

    @pl.when((pl.program_id(0) == 0) & (part == 0))
    def _():
        sum_in[...] = jnp.zeros_like(sum_in)
        sum_out[...] = jnp.zeros_like(sum_out)

    @pl.when(part == 0)
    def _():
        load_volume(volume, own, *edges)
        build_windows(volume, windows, columns, True)
        load_volume(volume, grad, *grad_edges)
        build_windows(volume, grad_windows, columns, False)

    blocks = hidden.shape[1]

    def step(at):
        block = part * blocks + at
        patch = patches(windows, block, frames, columns)
        grad_patch = patches(grad_windows, block, frames, columns)
        for f in range(frames):
            here = slice(f * columns, (f + 1) * columns)
            gh = lax.dot_general(
                grad_patch[:, here], w_back[...], TN, preferred_element_type=jnp.float32
            )
            grads[here, :] = (slopes[0, at, here, :].astype(jnp.float32) * gh).astype(
                jnp.bfloat16
            )
        sum_in[:DEPTH, :] += jnp.dot(patch, grads[...], preferred_element_type=jnp.float32)
        sum_out[:DEPTH, :] += jnp.dot(
            grad_patch, hidden[0, at], preferred_element_type=jnp.float32
        )

    for at in range(blocks):
        step(at)

    @pl.when((pl.program_id(0) == pl.num_programs(0) - 1) & (part == pl.num_programs(1) - 1))
    def _():
        width = sum_in.shape[1] // BLOCK
        lanes = sum_in.shape[0]
        lane = lax.broadcasted_iota(jnp.int32, (width, lanes), 1)
        picked = jnp.zeros((width, pick.shape[2]), jnp.float32)
        for index, source in enumerate((sum_in[...].T, sum_out[...].T)):
            folded = source[0:width, :]
            bias = folded
            for j in range(1, BLOCK):
                piece = source[j * width : (j + 1) * width, :]
                folded = folded + pltpu.roll(piece, lanes - j, axis=1)
                bias = bias + piece
            if index == 0:
                moved = pltpu.roll(bias, BIAS_LANE - ONES_ROW, axis=1)
                folded = jnp.where(lane == BIAS_LANE, moved, folded)
            for _ in range(3):
                piece = folded.astype(jnp.bfloat16)
                folded = folded - piece.astype(jnp.float32)
                picked = picked + jnp.dot(piece, pick[index], preferred_element_type=jnp.float32)
        out[0:width, :] = picked + extras[0:width, :]
        out[width:, :] = extras[width:, :]


def whole(shape):
    return pl.BlockSpec(tuple(shape), lambda s: (0,) * len(shape))


def a_slice(shape, first=0):
    rest = (0,) * (len(shape) - 1)
    return pl.BlockSpec((1,) + tuple(shape[1:]), lambda s: (s + first,) + rest)


def expected(microseconds):
    return pl.CostEstimate(
        flops=int(microseconds * 1.15e9), bytes_accessed=0, transcendentals=0
    )


def conv_scratch(frames, rows, columns):
    lanes = (frames + 2) * columns
    return (
        pltpu.VMEM((2, rows + 16, lanes), jnp.float32),
        pltpu.VMEM((rows // BLOCK, 3 * SIDE, lanes), jnp.bfloat16),
    )


def conv_forward(own, edges, group, w_in, w_out, bias_out):
    _, _, frames, rows, columns = own.shape
    first, slices = group
    lanes = (frames + 2) * columns
    span = w_in.shape[0]
    volume, windows = conv_scratch(frames, rows, columns)
    out_shape = [
        jax.ShapeDtypeStruct((slices, frames, rows, 2 * columns), jnp.float32),
        jax.ShapeDtypeStruct((slices, 2, rows, columns), jnp.bfloat16),
        jax.ShapeDtypeStruct((slices, 2, rows, columns), jnp.bfloat16),
        jax.ShapeDtypeStruct((slices, 2, lanes), jnp.bfloat16),
        jax.ShapeDtypeStruct((slices, 2, lanes), jnp.bfloat16),
    ]
    return pl.pallas_call(
        forward_kernel,
        grid=(slices,),
        in_specs=[a_slice(own.shape, first)]
        + [a_slice(one.shape) for one in edges]
        + [whole(w_in.shape), whole(w_out.shape), pl.BlockSpec(memory_space=pltpu.SMEM)],
        out_specs=[a_slice(one.shape) for one in out_shape],
        out_shape=out_shape,
        scratch_shapes=[
            volume,
            windows,
            volume,
            pltpu.VMEM((span, frames * columns), jnp.bfloat16),
            pltpu.VMEM((frames, DEPTH, columns), jnp.float32),
            pltpu.VMEM((rows // BLOCK, SIDE, lanes), jnp.float32),
        ],
        compiler_params=pltpu.CompilerParams(vmem_limit_bytes=VMEM),
        cost_estimate=expected(6 * slices),
        name="conv_forward",
    )(own, *edges, w_in, w_out, bias_out)


def hidden_again(own, edges, group, w_in, kept=()):
    _, _, frames, rows, columns = own.shape
    first, slices = group
    volume, windows = conv_scratch(frames, rows, columns)
    shape = (own.shape[0], rows // BLOCK, frames * columns, w_in.shape[1])
    return pl.pallas_call(
        hidden_kernel,
        grid=(slices,),
        in_specs=[a_slice(own.shape, first)]
        + [a_slice(one.shape, first) for one in edges]
        + [whole(w_in.shape)]
        + [pl.BlockSpec(memory_space=pl.ANY)] * len(kept),
        out_specs=[a_slice(shape, first)] * 2,
        out_shape=[jax.ShapeDtypeStruct(shape, jnp.bfloat16)] * 2,
        input_output_aliases={2 + EDGES + k: k for k in range(len(kept))},
        scratch_shapes=[volume, windows],
        compiler_params=pltpu.CompilerParams(vmem_limit_bytes=VMEM),
        cost_estimate=expected(5 * slices),
        name="hidden_again",
    )(own, *edges, w_in, *kept)


def conv_backward(own, edges, grad, grad_edges, hidden, slopes, w_back, extras):
    slices, _, frames, rows, columns = own.shape
    span = w_back.shape[1]
    volume, windows = conv_scratch(frames, rows, columns)
    total = pltpu.VMEM((2 * 128, span), jnp.float32)
    fixed = (w_back, pick_table(), extras)
    here = (own, *edges, grad, *grad_edges)
    blocks = rows // BLOCK
    parts = 1

    def of_slice(shape):
        rest = (0,) * (len(shape) - 1)
        return pl.BlockSpec((1,) + tuple(shape[1:]), lambda s, part: (s,) + rest)

    def part_of_slice(shape):
        size = (1, blocks // parts) + tuple(shape[2:])
        return pl.BlockSpec(size, lambda s, part: (s, part, 0, 0))

    def all_of(shape):
        return pl.BlockSpec(tuple(shape), lambda s, part: (0,) * len(shape))

    return pl.pallas_call(
        backward_kernel,
        grid=(slices, parts),
        in_specs=[of_slice(one.shape) for one in here]
        + [part_of_slice(one.shape) for one in (hidden, slopes)]
        + [all_of(one.shape) for one in fixed],
        out_specs=all_of(extras.shape),
        out_shape=jax.ShapeDtypeStruct(extras.shape, jnp.float32),
        scratch_shapes=[
            volume,
            windows,
            windows,
            pltpu.VMEM((frames * columns, span), jnp.bfloat16),
            total,
            total,
        ],
        compiler_params=pltpu.CompilerParams(vmem_limit_bytes=VMEM),
        cost_estimate=expected(5 * slices),
        name="conv_backward",
    )(*here, hidden, slopes, *fixed)


def along(axis, step):
    count = lax.axis_size(axis)
    return [(i, i + step) for i in range(count) if 0 <= i + step < count]


def sum_over(array, axis):
    size = lax.axis_size(axis)
    if size & (size - 1):
        return lax.psum(array, axis)

    def other(values, bits):
        return lax.ppermute(values, axis, [(i, i ^ bits) for i in range(size)])

    bit = 1
    if size.bit_length() % 2 == 0:
        array = array + other(array, bit)
        bit = 2
    while bit < size:
        one, two, three = (other(array, bit * k) for k in (1, 2, 3))
        array = (array + one) + (two + three)
        bit *= 4
    return array


def corners_along(left, right, columns):
    both = jnp.concatenate([left, right], axis=1)
    lanes = both.shape[2]
    below = lax.ppermute(both[:, :, lanes - columns :], "af", along("af", 1))
    above = lax.ppermute(both[:, :, :columns], "af", along("af", -1))
    return below, above


def share_edges(low, high, first, last):
    left = lax.ppermute(last, "row", along("row", 1))
    right = lax.ppermute(first, "row", along("row", -1))
    below = lax.ppermute(high, "af", along("af", 1))
    above = lax.ppermute(low, "af", along("af", -1))
    return below, above, left, right, *corners_along(left, right, low.shape[3])


def image_edges(image, group):
    start, slices = group
    part = image[start : start + slices]
    _, _, frames, rows, columns = part.shape
    flat = (slices, 2, frames * columns)
    return share_edges(
        part[:, :, 0], part[:, :, frames - 1],
        part[:, :, :, 0].reshape(flat), part[:, :, :, rows - 1].reshape(flat),
    )


def return_edges(part_below, part_above, part_left, part_right, columns):
    lower = lax.ppermute(part_left, "row", along("row", -1))
    upper = lax.ppermute(part_right, "row", along("row", 1))
    from_above = lax.ppermute(part_below, "af", along("af", -1))
    from_below = lax.ppermute(part_above, "af", along("af", 1))
    corner_below, corner_above = corners_along(upper, lower, columns)
    return from_below, from_above, upper, lower, corner_below, corner_above


def image_kernel(
    main, from_below, from_above, upper, lower, corner_below, corner_above,
    table, note, out, image,
):
    slices, frames, rows, twice = main.shape
    columns = twice // 2
    row = lax.broadcasted_iota(jnp.int32, (rows, columns), 0)
    for s in range(slices):
        tops = upper[s].astype(jnp.float32)
        ends = lower[s].astype(jnp.float32)
        corners = {
            0: corner_below[s].astype(jnp.float32),
            frames - 1: corner_above[s].astype(jnp.float32),
        }
        for f in range(frames):
            at = slice((f + 1) * columns, (f + 2) * columns)
            for o in range(2):
                here = slice(o * columns, (o + 1) * columns)
                value = main[s, f, :, here]
                if f == 0:
                    value = value + from_below[s, o].astype(jnp.float32)
                if f == frames - 1:
                    value = value + from_above[s, o].astype(jnp.float32)
                top, end = tops[o : o + 1, at], ends[o : o + 1, at]
                if f in corners:
                    top = top + corners[f][o : o + 1]
                    end = end + corners[f][2 + o : 3 + o]
                value = value + jnp.where(row == 0, top, 0.0)
                value = value + jnp.where(row == rows - 1, end, 0.0)
                start = (s * frames + f) * rows
                image[start : start + rows, here] = value.astype(jnp.bfloat16)
    size = slices * frames * rows
    for start in range(0, size, 512):
        stop = min(start + 512, size)
        out[:, start:stop] = lax.dot_general(
            table[...], image[start:stop, :], NT, preferred_element_type=jnp.float32
        ).astype(jnp.bfloat16)
    rest = out.shape[1] - size
    if rest:
        lane = lax.broadcasted_iota(jnp.int32, (out.shape[0], rest), 1)
        out[:, size:] = jnp.where(lane == 0, note[0, 0], 0.0).astype(jnp.bfloat16)


def image_to_hybrid(main, added, table, note, lanes):
    slices, frames, rows, twice = main.shape
    return pl.pallas_call(
        image_kernel,
        in_specs=[pl.BlockSpec(memory_space=pltpu.VMEM)] * (2 + EDGES)
        + [pl.BlockSpec(memory_space=pltpu.SMEM)],
        out_shape=jax.ShapeDtypeStruct((twice, lanes), jnp.bfloat16),
        scratch_shapes=[pltpu.VMEM((slices * frames * rows, twice), jnp.bfloat16)],
        compiler_params=pltpu.CompilerParams(vmem_limit_bytes=VMEM),
        cost_estimate=expected(slices / 2),
        name="image_to_hybrid",
    )(main, *added, table, note)


def grad_image_kernel(hybrid, table, out, low, high, first, last, sums):
    slices, _, frames, rows, columns = out.shape
    sums[...] = jnp.zeros_like(sums)
    for s in range(slices):
        size = frames * rows
        start = s * size // 128 * 128
        stop = -(-(s + 1) * size // 128) * 128
        value = lax.dot_general(
            hybrid[:, start:stop], table[...], TN, preferred_element_type=jnp.float32
        ).astype(jnp.bfloat16)
        for c in range(2):
            tops, ends = [], []
            for f in range(frames):
                at = s * size + f * rows - start
                piece = value[at : at + rows, c * columns : (c + 1) * columns]
                out[s, c, f] = piece
                if f == 0:
                    low[s, c] = piece
                if f == frames - 1:
                    high[s, c] = piece
                wide = piece.astype(jnp.float32)
                sums[c : c + 1, :] += jnp.sum(wide, axis=0, keepdims=True)
                tops.append(wide[0:1])
                ends.append(wide[rows - 1 :])
            first[s, c : c + 1, :] = jnp.concatenate(tops, axis=1)
            last[s, c : c + 1, :] = jnp.concatenate(ends, axis=1)


def hybrid_to_grad(hybrid, table, shape):
    slices, channels, frames, rows, columns = shape
    edge_frame = jax.ShapeDtypeStruct((slices, channels, rows, columns), jnp.bfloat16)
    edge_row = jax.ShapeDtypeStruct((slices, channels, frames * columns), jnp.float32)
    return pl.pallas_call(
        grad_image_kernel,
        out_shape=[
            jax.ShapeDtypeStruct(shape, jnp.bfloat16),
            edge_frame,
            edge_frame,
            edge_row,
            edge_row,
            jax.ShapeDtypeStruct((2, columns), jnp.float32),
        ],
        compiler_params=pltpu.CompilerParams(vmem_limit_bytes=VMEM),
        cost_estimate=expected(slices / 2),
        name="hybrid_to_grad",
    )(hybrid, table)


def chunk_transpose(pieces, low_half, even):
    a, c, b, d = pieces
    a, b = (
        jnp.where(low_half, a, pltpu.roll(b, 64, axis=1)),
        jnp.where(low_half, pltpu.roll(a, 64, axis=1), b),
    )
    c, d = (
        jnp.where(low_half, c, pltpu.roll(d, 64, axis=1)),
        jnp.where(low_half, pltpu.roll(c, 64, axis=1), d),
    )
    return (
        jnp.where(even, a, pltpu.roll(c, 32, axis=1)),
        jnp.where(even, pltpu.roll(a, 96, axis=1), c),
        jnp.where(even, b, pltpu.roll(d, 32, axis=1)),
        jnp.where(even, pltpu.roll(b, 96, axis=1), d),
    )


def kspace_slice(
    k, index, frames_here, n_af, measured, target, sampled, share, scale, table,
    spectrum, grads, loss_lanes,
):
    frames = n_af * frames_here
    twice = table.shape[0]
    first = index * frames_here
    size = frames * 8
    here = spectrum[pl.ds(first, frames_here)].reshape(size, twice).astype(jnp.bfloat16)
    kspace = jnp.dot(here, table[...], preferred_element_type=jnp.float32)

    def place(t):
        return (t % frames_here) * n_af + t // frames_here

    filled = []
    for t in range(frames):
        mask = sampled[t]
        filled.append(mask * measured[k, t] + (1.0 - mask) * kspace[place(t) * 8 : place(t) * 8 + 8])
    slopes = []
    for t in range(frames):
        mask = sampled[t]
        near = range(max(t - 2, 0), min(t + 3, frames))
        shared = sum(share[t, s] * filled[s] for s in near)
        differ = mask * measured[k, t] + (1.0 - mask) * shared - target[k, t]
        square = differ * differ + 1.0
        inverse = lax.rsqrt(square)
        loss_lanes[...] += (1.0 - mask) * (square * inverse - 1.0)
        slopes.append((1.0 - mask) * differ * inverse * scale[0, 0])
    for s in range(frames):
        near = range(max(s - 2, 0), min(s + 3, frames))
        grad = sum(share[t, s] * slopes[t] for t in near)
        grads[k, place(s) * 8 : place(s) * 8 + 8, :] = (1.0 - sampled[s]) * grad
    grad = grads[k]
    high = grad.astype(jnp.bfloat16)
    low = (grad - high.astype(jnp.float32)).astype(jnp.bfloat16)
    back = lax.dot_general(high, table[...], NT, preferred_element_type=jnp.float32)
    back += lax.dot_general(low, table[...], NT, preferred_element_type=jnp.float32)
    spectrum[pl.ds(first, frames_here)] = back.reshape(frames_here, n_af, 8, twice)


def kspace_kernel(
    frames_here, received, measured, target, sampled, share, scale, table, out, loss,
    spectrum, grads, loss_lanes,
):
    groups, _, lanes = received.shape
    pairs, n_af, _, twice = spectrum.shape
    rows = twice // 2
    n_row = groups // n_af
    step = pl.program_id(0)
    lane = lax.broadcasted_iota(jnp.int32, (SIDE, 128), 1)
    low_half = lane < 64
    even = lane % 64 < 32

    @pl.when(step == 0)
    def _():
        loss_lanes[...] = jnp.zeros_like(loss_lanes)
        def gather(af, carry):
            for tile in range(lanes // 128):
                for h in range(n_row // 4):
                    source = [
                        received[af * n_row + h * 4 + m, :, tile * 128 : (tile + 1) * 128]
                        for m in range(4)
                    ]
                    moved = chunk_transpose(source, low_half, even)
                    for k in range(4):
                        if tile * 4 + k < pairs:
                            wide = moved[k].astype(jnp.float32)
                            for c in range(2):
                                at = c * rows + h * 128
                                spectrum[tile * 4 + k, af, :, at : at + 128] = wide[
                                    c * 8 : (c + 1) * 8
                                ]
            return carry

        lax.fori_loop(0, n_af, gather, 0)

    each = measured.shape[0]
    for k in range(each):
        kspace_slice(
            k, step * each + k, frames_here, n_af, measured, target, sampled, share, scale, table,
            spectrum, grads, loss_lanes,
        )

    @pl.when(step == pl.num_programs(0) - 1)
    def _():
        loss[...] = loss_lanes[...]

        def scatter(af, carry):
            for tile in range(lanes // 128):
                for h in range(n_row // 4):
                    source = []
                    for k in range(4):
                        pair = min(tile * 4 + k, pairs - 1)
                        both = [
                            spectrum[pair, af, :, c * rows + h * 128 : c * rows + h * 128 + 128]
                            for c in range(2)
                        ]
                        source.append(jnp.concatenate(both, axis=0).astype(jnp.bfloat16))
                    moved = chunk_transpose(source, low_half, even)
                    for m in range(4):
                        out[af * n_row + h * 4 + m, :, tile * 128 : (tile + 1) * 128] = moved[m]
            return carry

        lax.fori_loop(0, n_af, scatter, 0)


def kspace_step(received, measured, target, sampled, share, scale, table, frames_here, group):
    _, frames, lines, twice = measured.shape
    first, slices = group
    n_af = frames // frames_here
    each = 2 if slices % 2 == 0 and first % 2 == 0 else 1

    def some(shape):
        start = first // each
        return pl.BlockSpec((each,) + tuple(shape[1:]), lambda s: (s + start, 0, 0, 0))

    smem = pl.BlockSpec(memory_space=pltpu.SMEM)
    return pl.pallas_call(
        functools.partial(kspace_kernel, frames_here),
        grid=(slices // each,),
        in_specs=[
            whole(received.shape),
            some(measured.shape),
            some(target.shape),
            whole(sampled.shape),
            smem,
            smem,
            whole(table.shape),
        ],
        out_specs=[whole(received.shape), whole((lines, twice))],
        out_shape=[
            jax.ShapeDtypeStruct(received.shape, jnp.bfloat16),
            jax.ShapeDtypeStruct((lines, twice), jnp.float32),
        ],
        scratch_shapes=[
            pltpu.VMEM((slices * frames_here, n_af, lines, twice), jnp.float32),
            pltpu.VMEM((each, frames * lines, twice), jnp.float32),
            pltpu.VMEM((lines, twice), jnp.float32),
        ],
        compiler_params=pltpu.CompilerParams(vmem_limit_bytes=VMEM),
        cost_estimate=expected(3 * slices),
        name="kspace",
    )(received, measured, target, sampled, share, scale, table)


def middle_plain(main, added, measured, target, sampled, share, table_y, table_x):
    highest = lax.Precision.HIGHEST
    slices, frames_here, rows_here, twice = main.shape
    count = lax.psum(jnp.sum(1.0 - sampled) * (2.0 * slices * measured.shape[3] / 2), AXES)
    columns = twice // 2
    frames, lines = measured.shape[1:3]
    rows = measured.shape[3] // 2
    table_y = jnp.asarray(table_y, jnp.bfloat16)
    table_x = jnp.asarray(table_x, jnp.bfloat16)
    image = main.reshape(slices, frames_here, rows_here, 2, columns)
    below, above, upper, lower, *corners = (one.astype(jnp.float32) for one in added)
    image = image.at[:, 0].add(below.transpose(0, 2, 1, 3))
    image = image.at[:, frames_here - 1].add(above.transpose(0, 2, 1, 3))
    for at, line in ((0, upper), (rows_here - 1, lower)):
        line = line[:, :, columns:-columns].reshape(slices, 2, frames_here, columns)
        image = image.at[:, :, at].add(line.transpose(0, 2, 1, 3))
    for f, corner in ((0, corners[0]), (frames_here - 1, corners[1])):
        image = image.at[:, f, 0].add(corner[:, 0:2])
        image = image.at[:, f, rows_here - 1].add(corner[:, 2:4])
    flat = image.reshape(slices, frames_here, rows_here, twice).astype(jnp.bfloat16)
    hybrid = jnp.dot(flat, table_y, preferred_element_type=jnp.float32).astype(jnp.bfloat16)
    hybrid = hybrid.reshape(slices, frames_here, rows_here, 2, columns)
    part = lax.all_to_all(hybrid, "af", split_axis=4, concat_axis=1, tiled=True)
    spread = lax.all_to_all(part, "row", split_axis=4, concat_axis=2, tiled=True)
    spectrum = jnp.transpose(spread, (0, 1, 4, 3, 2)).reshape(slices, frames, lines, 2 * rows)
    kspace = jnp.dot(spectrum, table_x, preferred_element_type=jnp.float32)
    mask = sampled[None, :, :, None]
    filled = mask * measured + (1.0 - mask) * kspace
    shared = jnp.einsum("ts,bslk->btlk", share, filled, precision=highest)
    differ = mask * measured + (1.0 - mask) * shared - target
    root = jnp.sqrt(differ * differ + 1.0)
    loss = jnp.sum((1.0 - mask) * (root - 1.0))
    slope = (1.0 - mask) * differ / root / count
    grad = (1.0 - mask) * jnp.einsum("ts,btlk->bslk", share, slope, precision=highest)
    back = jnp.dot(grad, table_x.T.astype(jnp.float32), precision=highest).astype(jnp.bfloat16)
    back = jnp.transpose(back.reshape(slices, frames, lines, 2, rows), (0, 1, 4, 3, 2))
    part = lax.all_to_all(back, "row", split_axis=2, concat_axis=4, tiled=True)
    whole_rows = lax.all_to_all(part, "af", split_axis=1, concat_axis=4, tiled=True)
    grad = jnp.dot(
        whole_rows.reshape(slices, frames_here, rows_here, twice),
        table_y.T,
        preferred_element_type=jnp.float32,
    ).reshape(slices, frames_here, rows_here, 2, columns)
    grad = jnp.transpose(grad, (0, 3, 1, 2, 4)).astype(jnp.bfloat16)
    return loss, count, grad, jnp.sum(grad.astype(jnp.float32), axis=(0, 2, 3, 4))


def update_kernel(total, *refs):
    ins, outs = refs[:12], refs[12:]
    taps, width = ins[0].shape
    turned = total[0:width, :].T

    def step(kind, at, grad):
        master, first, second, smooth = (one[at] for one in ins[kind::3])
        rate = (rate_in, rate_out, rate_bias)[kind]
        first, second, master = adam_step(master, grad, first, second, rate)
        average = average_keep * smooth + (1.0 - average_keep) * master
        for out, value in zip(outs[kind::3], (first, second, master, average, master)):
            out[at] = value.astype(out.dtype)

    step(0, ..., turned[0:taps, :])
    for tap in range(ins[1].shape[0]):
        start = PACKED // 2 + 2 * tap
        step(1, tap, turned[start : start + 2, :])
    step(2, (slice(0, 1), slice(0, width)), turned[54:55, :])
    step(2, (slice(0, 1), slice(width, width + 2)), total[width : width + 1, 1:3])


def update(total, weights, firsts, seconds, smooths):
    arrays = [*weights, *firsts, *seconds, *smooths]
    turn = {1: lambda one: one.reshape(1, -1), 2: jnp.transpose, 3: lambda one: one}
    arrays = [turn[one.ndim](one) for one in arrays]
    kinds = [jnp.float32] * 4 + [jnp.bfloat16]
    outs = pl.pallas_call(
        update_kernel,
        out_shape=[jax.ShapeDtypeStruct(one.shape, kind) for kind in kinds for one in arrays[:3]],
        name="update",
    )(total, *arrays)
    back = (jnp.transpose, lambda one: one, lambda one: one.reshape(-1))
    return [back[k % 3](one) for k, one in enumerate(outs)]


def packed_extras(width, loss, sums):
    row = jnp.concatenate([loss.reshape(1), sums])
    return jnp.pad(row.reshape(1, 3), ((width, 7), (0, PACKED - 3)))


def middle_fast(
    main, added, measured, target, sampled, share, table_y, table_x, between, after
):
    devices = lax.axis_size("af") * lax.axis_size("row")
    slices, frames_here, rows, twice = main.shape
    lines, readout = measured.shape[2:]
    size = slices * frames_here * rows
    order = np.arange(twice).reshape(2, devices, lines).transpose(1, 0, 2).reshape(-1)
    permuted = jnp.asarray(np.ascontiguousarray(table_y[:, order].T), jnp.bfloat16)
    mask = jnp.broadcast_to(sampled[:, :, None], sampled.shape + (readout,))
    note = jnp.sum(1.0 - sampled).reshape(1, 1)
    lanes = (size // 128 + 1) * 128
    hybrid = image_to_hybrid(main, added, permuted, note, lanes)
    received = lax.all_to_all(
        hybrid.reshape(devices, 2 * lines, lanes), AXES, 0, 0, tiled=True
    )
    first = between(hybrid)
    received, first = lax.optimization_barrier((received, first))
    notes = received[:, 0, size].astype(jnp.float32)
    count = jnp.sum(notes) * (1.0 * slices * readout)
    back, loss = kspace_step(
        received, measured, target, mask, share, (1.0 / count).reshape(1, 1),
        jnp.asarray(table_x, jnp.bfloat16), frames_here, (0, slices),
    )
    returned = lax.all_to_all(back, AXES, 0, 0, tiled=True)
    second = after(back, first)
    returned, second = lax.optimization_barrier((returned, second))
    shape = (slices, 2, frames_here, rows, twice // 2)
    grad, *grad_edge, sums = hybrid_to_grad(returned.reshape(twice, lanes), permuted, shape)
    return jnp.sum(loss), count, grad, grad_edge, jnp.sum(sums, axis=1), second


def train_step(
    image_in, measured, target, sampled, share, table_y, table_x, w_in, w_out, w_back, bias_out
):
    slices, _, frames_here, rows, columns = image_in.shape
    frames, lines = measured.shape[1:3]
    cut = (slices + 1) // 2
    groups = [(0, cut), (cut, slices - cut)]
    edges = image_edges(image_in, (0, slices))
    main, *part = conv_forward(image_in, edges, (0, slices), w_in, w_out, bias_out)
    added = return_edges(*part, columns)

    def again(group, after, kept=()):
        held, _ = lax.optimization_barrier((w_in.T, after))
        return hidden_again(image_in, edges, group, held, kept)

    fits = rows == 32 and lines == 8 and lax.axis_size("row") % 4 == 0
    fits = fits and frames * lines <= 256
    if fits:
        loss, count, grad, grad_edge, sums, kept = middle_fast(
            main, added, measured, target, sampled, share, table_y, table_x,
            functools.partial(again, groups[0]), functools.partial(again, groups[1]),
        )
    else:
        loss, count, grad, sums = middle_plain(
            main, added, measured, target, sampled, share, table_y, table_x
        )
        flat = (slices, 2, frames_here * columns)
        grad_edge = (
            grad[:, :, 0], grad[:, :, frames_here - 1],
            grad[:, :, :, 0].reshape(flat), grad[:, :, :, rows - 1].reshape(flat),
        )
        kept = None
    around = share_edges(*grad_edge)
    total = packed_extras(w_in.shape[0] // BLOCK, loss, sums)
    if kept is not None:
        return count, conv_backward(image_in, edges, grad, around, *kept, w_back, total)
    for first, size in groups:
        own, *sides = (one[first : first + size] for one in (image_in, *edges, grad, *around))
        held, _ = lax.optimization_barrier((w_in.T, total))
        kept = hidden_again(own, sides[:EDGES], (0, size), held)
        total = conv_backward(
            own, sides[:EDGES], sides[EDGES], sides[EDGES + 1 :], *kept, w_back, total
        )
    return count, total


def on_device(
    image_in, measured, target, line_mask, window_half, in_kernel, out_kernel, biases,
    in_moment, out_moment, bias_moment, in_square, out_square, bias_square,
    in_smooth, out_smooth, bias_smooth,
):
    slices, _, frames_here, rows_here, columns = image_in.shape
    frames = measured.shape[1]
    width = in_kernel.shape[0]
    rows = rows_here * lax.axis_size("row")
    table_y = dft_table(columns)
    table_x = dft_table(rows)
    share = share_matrix(window_half, frames)
    sampled = line_mask.astype(jnp.float32)
    w_in = conv_in_weights(in_kernel, biases[:width])
    w_out = conv_out_weights(out_kernel)
    w_back = conv_back_weights(out_kernel)

    count, total = train_step(
        image_in, measured, target, sampled, share, table_y, table_x,
        w_in, w_out, w_back, biases[width:],
    )
    total = sum_over(sum_over(total, "row"), "af")
    outs = update(
        total,
        (in_kernel, out_kernel, biases),
        (in_moment, out_moment, bias_moment),
        (in_square, out_square, bias_square),
        (in_smooth, out_smooth, bias_smooth),
    )
    return (total[width, 0], count, *outs)


def solution(mesh):
    in_specs = (
        P(None, None, "af", "row", None),
        P(None, None, ("af", "row"), None),
        P(None, None, ("af", "row"), None),
        P(None, ("af", "row")),
    ) + (P(),) * 13
    return jax.shard_map(
        on_device, mesh=mesh, in_specs=in_specs, out_specs=(P(),) * 17, check_vma=False
    )
```

profile of v0, /device:TPU:0, one launch (start us, length us, event | category | flops | bytes accessed | tf_op | source)
XLA Modules:
  0.0 303.9 jit_solution(16939475865474063917)
XLA Ops:
  2.3 2.4 collective-permute-start.2
  7.2 4.3 %collective-permute-start = (bf16[10,2,32,256]{3,2,1,0:T(8,128)(2,1)S(1)}, bf16[10,2,32,256]{3,2,1,0:T(8,128)(2,1)S(1)}, u32[]{:S(2)}, u32[]{:S(2)}) collective-permute-start(bf16[10,2,32,256]{3,2,1,0:T(8,128)(2,1)S(1)} %get-tuple-element.112), channel_id=1, source_target_pairs={{0,8},{8,16},{16,24},{1,9},{9,17},{17,25},{2,10},{10,18},{18,26},{... | collective-permute-start | bytes 983048 | tf_op jit(solution)/shard_map/ppermute | solution.py:485
  13.3 4.5 %collective-permute-start.4 = (bf16[10,4,256]{2,1,0:T(4,128)(2,1)S(1)}, bf16[10,4,256]{2,1,0:T(4,128)(2,1)S(1)}, u32[]{:S(2)}, u32[]{:S(2)}) collective-permute-start(bf16[10,4,256]{2,1,0:T(4,128)(2,1)S(1)} %get-tuple-element.118), channel_id=1, source_target_pairs={{0,8},{8,16},{16,24},{1,9},{9,17},{17,25},{2,10},{10,18},{18,26},{... | collective-permute-start | bytes 61448 | tf_op jit(solution)/shard_map/ppermute | solution.py:477
  25.3 40.7 %conv_forward.1 = (f32[10,5,32,512]{3,2,1,0:T(8,128)}, bf16[10,2,32,256]{3,2,1,0:T(8,128)(2,1)}, bf16[10,2,32,256]{3,2,1,0:T(8,128)(2,1)}, bf16[10,2,1792]{2,1,0:T(2,128)(2,1)}, bf16[10,2,1792]{2,1,0:T(2,128)(2,1)}) custom-call(bf16[10,2,5,32,256]{4,3,2,1,0:T(8,128)(2,1)} %own.7, bf16[10,2,32,256]{3,2,1,0:T(8,128)(2,1)} %copy-done.3, ...), custom_call_target="tpu_custom_call" | custom-call | flops 69000003584 | tf_op jit(solution)/shard_map/conv_forward/pallas_call | solution.py:363
  66.0 3.5 %collective-permute-start.6 = (bf16[10,2,32,256]{3,2,1,0:T(8,128)(2,1)}, bf16[10,2,32,256]{3,2,1,0:T(8,128)(2,1)S(1)}, u32[]{:S(2)}, u32[]{:S(2)}) collective-permute-start(bf16[10,2,32,256]{3,2,1,0:T(8,128)(2,1)} %get-tuple-element.70), channel_id=1, source_target_pairs={{0,8},{8,16},{16,24},{1,9},{9,17},{17,25},{2,10},{10,18},{18,26},{... | collective-permute-start | bytes 983048 | tf_op jit(solution)/shard_map/ppermute | solution.py:505
  70.8 2.3 collective-permute-start.8
  74.4 5.0 %collective-permute-done.9.lower = bf16[10,2,1792]{2,1,0:T(2,128)(2,1)S(1)} collective-permute-done((bf16[10,2,1792]{2,1,0:T(2,128)(2,1)}, bf16[10,2,1792]{2,1,0:T(2,128)(2,1)S(1)}, u32[]{:S(2)}, u32[]{:S(2)}) %collective-permute-start.9) | collective-permute-done | bytes 71712 | tf_op jit(solution)/shard_map/ppermute | solution.py:502
  79.5 4.5 %collective-permute-start.10 = (bf16[10,4,256]{2,1,0:T(4,128)(2,1)S(1)}, bf16[10,4,256]{2,1,0:T(4,128)(2,1)S(1)}, u32[]{:S(2)}, u32[]{:S(2)}) collective-permute-start(bf16[10,4,256]{2,1,0:T(4,128)(2,1)S(1)} %get-tuple-element.116), channel_id=1, source_target_pairs={{0,8},{8,16},{16,24},{1,9},{9,17},{17,25},{2,10},{10,18},{18,26},{... | collective-permute-start | bytes 61448 | tf_op jit(solution)/shard_map/ppermute | solution.py:477
  86.0 3.8 %collective-permute-done.11.corner_above = bf16[10,4,256]{2,1,0:T(4,128)(2,1)S(1)} collective-permute-done((bf16[10,4,256]{2,1,0:T(4,128)(2,1)S(1)}, bf16[10,4,256]{2,1,0:T(4,128)(2,1)S(1)}, u32[]{:S(2)}, u32[]{:S(2)}) %collective-permute-start.11) | collective-permute-done | bytes 20512 | tf_op jit(solution)/shard_map/ppermute | solution.py:478
  90.6 5.3 %image_to_hybrid.1 = bf16[512,1664]{1,0:T(8,128)(2,1)} custom-call(f32[10,5,32,512]{3,2,1,0:T(8,128)} %get-tuple-element.69.main, bf16[10,2,32,256]{3,2,1,0:T(8,128)(2,1)} %copy-done.22, bf16[10,2,32,256]{3,2,1,0:T(8,128)(2,1)} %copy-done.23, bf16[10,2,1792]{2,1,0:T(2,128)(2,1)} %copy-done.12, bf16[10,2,1792]{2,1,0:T(2,128)(2,1)} %copy-done.13, ...), custom_call_target="tpu_custom_call" | custom-call | flops 5750000128 | tf_op jit(solution)/shard_map/image_to_hybrid/pallas_call | solution.py:555
  95.9 7.0 %all-to-all-start = ((bf16[32,16,1664]{2,1,0:T(8,128)(2,1)}), bf16[32,16,1664]{2,1,0:T(8,128)(2,1)S(1)}, u32[]{:S(2)}, u32[]{:S(2)}) async-start(bf16[32,16,1664]{2,1,0:T(8,128)(2,1)} %bitcast.95), calls=%async_computation | async-start | bytes 3407872 | tf_op jit(solution)/shard_map/all_to_all | solution.py:878
  103.9 34.9 %hidden_again.2 = (bf16[10,8,1280,256]{3,2,1,0:T(8,128)(2,1)}, bf16[10,8,1280,256]{3,2,1,0:T(8,128)(2,1)}) custom-call(bf16[10,2,5,32,256]{4,3,2,1,0:T(8,128)(2,1)} %own.7, bf16[10,2,32,256]{3,2,1,0:T(8,128)(2,1)} %copy-done.3, bf16[10,2,32,256]{3,2,1,0:T(8,128)(2,1)} %copy-done.4, bf16[10,2,1280]{2,1,0:T(2,128)(2,1)} %copy-done.5, ...), custom_call_target="tpu_custom_call" | custom-call | flops 28750000128 | tf_op jit(solution)/shard_map/hidden_again/pallas_call | solution.py:390
  138.8 4.4 %all-to-all-done.received = bf16[32,16,1664]{2,1,0:T(8,128)(2,1)S(1)} async-done(((bf16[32,16,1664]{2,1,0:T(8,128)(2,1)}), bf16[32,16,1664]{2,1,0:T(8,128)(2,1)S(1)}, u32[]{:S(2)}, u32[]{:S(2)}) %all-to-all-start) | async-done | bytes 1703968 | tf_op jit(solution)/shard_map/all_to_all | solution.py:878
  145.6 18.8 %kspace.1 = (bf16[32,16,1664]{2,1,0:T(8,128)(2,1)}, f32[8,512]{1,0:T(8,128)}) custom-call(bf16[32,16,1664]{2,1,0:T(8,128)(2,1)} %copy-done, f32[10,20,8,512]{3,2,1,0:T(8,128)} %measured.1, f32[10,20,8,512]{3,2,1,0:T(8,128)} %target.1, f32[20,8,512]{2,1,0:T(8,128)} %broadcast_in_dim.2.sampled, f32[20,20]{1,0:T(8,128)} %convert_divide_fusion.share, ...), custom_call_target="tpu_custom_call" | custom-call | flops 34500001792 | tf_op jit(solution)/shard_map/kspace/pallas_call | solution.py:750
  164.4 4.1 %all-to-all-start.1 = ((bf16[32,16,1664]{2,1,0:T(8,128)(2,1)}), bf16[32,16,1664]{2,1,0:T(8,128)(2,1)S(1)}, u32[]{:S(2)}, u32[]{:S(2)}) async-start(bf16[32,16,1664]{2,1,0:T(8,128)(2,1)} %get-tuple-element.78), calls=%async_computation.1 | async-start | bytes 3407872 | tf_op jit(solution)/shard_map/all_to_all | solution.py:889
  168.6 35.1 %hidden_again.3 = (bf16[10,8,1280,256]{3,2,1,0:T(8,128)(2,1)}, bf16[10,8,1280,256]{3,2,1,0:T(8,128)(2,1)}) custom-call(bf16[10,2,5,32,256]{4,3,2,1,0:T(8,128)(2,1)} %own.7, bf16[10,2,32,256]{3,2,1,0:T(8,128)(2,1)} %copy-done.3, bf16[10,2,32,256]{3,2,1,0:T(8,128)(2,1)} %copy-done.4, ...), custom_call_target="tpu_custom_call", output_to_operand_aliasing={{0}: (8, {}), {1}: (9, {})} | custom-call | flops 28750000128 | tf_op jit(solution)/shard_map/hidden_again/pallas_call | solution.py:390
  203.7 5.1 %all-to-all-done.1 = bf16[32,16,1664]{2,1,0:T(8,128)(2,1)S(1)} async-done(((bf16[32,16,1664]{2,1,0:T(8,128)(2,1)}), bf16[32,16,1664]{2,1,0:T(8,128)(2,1)S(1)}, u32[]{:S(2)}, u32[]{:S(2)}) %all-to-all-start.1) | async-done | bytes 1703968 | tf_op jit(solution)/shard_map/all_to_all | solution.py:889
  210.0 4.6 %hybrid_to_grad.1 = (bf16[10,2,5,32,256]{4,3,2,1,0:T(8,128)(2,1)}, bf16[10,2,32,256]{3,2,1,0:T(8,128)(2,1)}, bf16[10,2,32,256]{3,2,1,0:T(8,128)(2,1)}, f32[10,2,...) custom-call(bf16[512,1664]{1,0:T(8,128)(2,1)} %bitcast.94, bf16[512,512]{1,0:T(8,128)(2,1)} %constant.56.clone.table), custom_call_target="tpu_custom_call" | custom-call | flops 5750000128 | tf_op jit(solution)/shard_map/hybrid_to_grad/pallas_call | solution.py:599
  217.5 2.7 collective-permute-start.12
  224.1 4.5 %collective-permute-start.16 = (f32[10,4,256]{2,1,0:T(4,128)S(1)}, f32[10,4,256]{2,1,0:T(4,128)S(1)}, u32[]{:S(2)}, u32[]{:S(2)}) collective-permute-start(f32[10,4,256]{2,1,0:T(4,128)S(1)} %get-tuple-element.114), channel_id=1, source_target_pairs={{0,8},{8,16},{16,24},{1,9},{9,17},{17,25},{2,10},{10,18},{18,26},{... | collective-permute-start | bytes 122888 | tf_op jit(solution)/shard_map/ppermute | solution.py:477
  231.6 3.0 collective-permute-done.17.refs_12_
  235.5 44.8 %conv_backward.1 = f32[72,128]{1,0:T(8,128)} custom-call(bf16[10,2,5,32,256]{4,3,2,1,0:T(8,128)(2,1)} %own.7, bf16[10,2,32,256]{3,2,1,0:T(8,128)(2,1)} %copy-done.3, bf16[10,2,32,256]{3,2,1,0:T(8,128)(2,1)} %copy-done.4, bf16[10,2,1280]{2,1,0:T(2,128)(2,1)} %copy-done.5, bf16[10,2,1280]{2,1,0:T(2,128)(2,1)} %copy-done.6, bf16[10,4,256]{2,1,0:T(4,128)(2,1)} %copy-done.14, ...), custom_call_target="tpu_custom_call" | custom-call | flops 57500000256 | tf_op jit(solution)/shard_map/conv_backward/pallas_call | solution.py:428
  282.5 3.0 collective-permute-start.19
  298.0 2.4 collective-permute-done.24
  (141 shorter events, 50.0 us)
Async XLA Ops:
  2.3 10.9 %collective-permute-start.2 = (bf16[10,2,1280]{2,1,0:T(2,128)(2,1)S(1)}, bf16[10,2,1280]{2,1,0:T(2,128)(2,1)S(1)}, u32[]{:S(2)}, u32[]{:S(2)}) collective-permute-start(bf16[10,2,1280]{2,1,0:T(2,128)(2,1)S(1)} %reshape_squeeze.6), channel_id=1, source_target_pairs={{0,1},{1,2},{2,3},{3,4},{4,5},{5,6},{6,7},{8,9},{9,10},{10,11},{11... | collective-permute-start | bytes 153608 | tf_op jit(solution)/shard_map/ppermute | solution.py:483
  4.7 8.5 %collective-permute-start.3 = (bf16[10,2,1280]{2,1,0:T(2,128)(2,1)S(1)}, bf16[10,2,1280]{2,1,0:T(2,128)(2,1)S(1)}, u32[]{:S(2)}, u32[]{:S(2)}) collective-permute-start(bf16[10,2,1280]{2,1,0:T(2,128)(2,1)S(1)} %reshape_squeeze.7), channel_id=1, source_target_pairs={{1,0},{2,1},{3,2},{4,3},{5,4},{6,5},{7,6},{9,8},{10,9},{11,10},{12... | collective-permute-start | bytes 153608 | tf_op jit(solution)/shard_map/ppermute | solution.py:484
  7.2 16.7 %collective-permute-start = (bf16[10,2,32,256]{3,2,1,0:T(8,128)(2,1)S(1)}, bf16[10,2,32,256]{3,2,1,0:T(8,128)(2,1)S(1)}, u32[]{:S(2)}, u32[]{:S(2)}) collective-permute-start(bf16[10,2,32,256]{3,2,1,0:T(8,128)(2,1)S(1)} %get-tuple-element.112), channel_id=1, source_target_pairs={{0,8},{8,16},{16,24},{1,9},{9,17},{17,25},{2,10},{10,18},{18,26},{... | collective-permute-start | bytes 983048 | tf_op jit(solution)/shard_map/ppermute | solution.py:485
  11.5 12.3 %collective-permute-start.1 = (bf16[10,2,32,256]{3,2,1,0:T(8,128)(2,1)S(1)}, bf16[10,2,32,256]{3,2,1,0:T(8,128)(2,1)S(1)}, u32[]{:S(2)}, u32[]{:S(2)}) collective-permute-start(bf16[10,2,32,256]{3,2,1,0:T(8,128)(2,1)S(1)} %get-tuple-element.111), channel_id=1, source_target_pairs={{8,0},{16,8},{24,16},{9,1},{17,9},{25,17},{10,2},{18,10},{26,18},{... | collective-permute-start | bytes 983048 | tf_op jit(solution)/shard_map/ppermute | solution.py:486
  13.3 8.8 %collective-permute-start.4 = (bf16[10,4,256]{2,1,0:T(4,128)(2,1)S(1)}, bf16[10,4,256]{2,1,0:T(4,128)(2,1)S(1)}, u32[]{:S(2)}, u32[]{:S(2)}) collective-permute-start(bf16[10,4,256]{2,1,0:T(4,128)(2,1)S(1)} %get-tuple-element.118), channel_id=1, source_target_pairs={{0,8},{8,16},{16,24},{1,9},{9,17},{17,25},{2,10},{10,18},{18,26},{... | collective-permute-start | bytes 61448 | tf_op jit(solution)/shard_map/ppermute | solution.py:477
  17.9 6.0 %collective-permute-start.5 = (bf16[10,4,256]{2,1,0:T(4,128)(2,1)S(1)}, bf16[10,4,256]{2,1,0:T(4,128)(2,1)S(1)}, u32[]{:S(2)}, u32[]{:S(2)}) collective-permute-start(bf16[10,4,256]{2,1,0:T(4,128)(2,1)S(1)} %get-tuple-element.117), channel_id=1, source_target_pairs={{8,0},{16,8},{24,16},{9,1},{17,9},{25,17},{10,2},{18,10},{26,18},{... | collective-permute-start | bytes 61448 | tf_op jit(solution)/shard_map/ppermute | solution.py:478
  66.0 23.7 %collective-permute-start.6 = (bf16[10,2,32,256]{3,2,1,0:T(8,128)(2,1)}, bf16[10,2,32,256]{3,2,1,0:T(8,128)(2,1)S(1)}, u32[]{:S(2)}, u32[]{:S(2)}) collective-permute-start(bf16[10,2,32,256]{3,2,1,0:T(8,128)(2,1)} %get-tuple-element.70), channel_id=1, source_target_pairs={{0,8},{8,16},{16,24},{1,9},{9,17},{17,25},{2,10},{10,18},{18,26},{... | collective-permute-start | bytes 983048 | tf_op jit(solution)/shard_map/ppermute | solution.py:505
  69.5 20.2 %collective-permute-start.7 = (bf16[10,2,32,256]{3,2,1,0:T(8,128)(2,1)}, bf16[10,2,32,256]{3,2,1,0:T(8,128)(2,1)S(1)}, u32[]{:S(2)}, u32[]{:S(2)}) collective-permute-start(bf16[10,2,32,256]{3,2,1,0:T(8,128)(2,1)} %get-tuple-element.71), channel_id=1, source_target_pairs={{8,0},{16,8},{24,16},{9,1},{17,9},{25,17},{10,2},{18,10},{26,18},{... | collective-permute-start | bytes 983048 | tf_op jit(solution)/shard_map/ppermute | solution.py:504
  73.1 6.3 %collective-permute-start.9 = (bf16[10,2,1792]{2,1,0:T(2,128)(2,1)}, bf16[10,2,1792]{2,1,0:T(2,128)(2,1)S(1)}, u32[]{:S(2)}, u32[]{:S(2)}) collective-permute-start(bf16[10,2,1792]{2,1,0:T(2,128)(2,1)} %get-tuple-element.73), channel_id=1, source_target_pairs={{1,0},{2,1},{3,2},{4,3},{5,4},{6,5},{7,6},{9,8},{10,9},{11,10},{12... | collective-permute-start | bytes 215048 | tf_op jit(solution)/shard_map/ppermute | solution.py:502
  79.5 6.5 %collective-permute-start.10 = (bf16[10,4,256]{2,1,0:T(4,128)(2,1)S(1)}, bf16[10,4,256]{2,1,0:T(4,128)(2,1)S(1)}, u32[]{:S(2)}, u32[]{:S(2)}) collective-permute-start(bf16[10,4,256]{2,1,0:T(4,128)(2,1)S(1)} %get-tuple-element.116), channel_id=1, source_target_pairs={{0,8},{8,16},{16,24},{1,9},{9,17},{17,25},{2,10},{10,18},{18,26},{... | collective-permute-start | bytes 61448 | tf_op jit(solution)/shard_map/ppermute | solution.py:477
  84.1 5.7 %collective-permute-start.11 = (bf16[10,4,256]{2,1,0:T(4,128)(2,1)S(1)}, bf16[10,4,256]{2,1,0:T(4,128)(2,1)S(1)}, u32[]{:S(2)}, u32[]{:S(2)}) collective-permute-start(bf16[10,4,256]{2,1,0:T(4,128)(2,1)S(1)} %get-tuple-element.115), channel_id=1, source_target_pairs={{8,0},{16,8},{24,16},{9,1},{17,9},{25,17},{10,2},{18,10},{26,18},{... | collective-permute-start | bytes 61448 | tf_op jit(solution)/shard_map/ppermute | solution.py:478
  95.9 47.3 %all-to-all-start = ((bf16[32,16,1664]{2,1,0:T(8,128)(2,1)}), bf16[32,16,1664]{2,1,0:T(8,128)(2,1)S(1)}, u32[]{:S(2)}, u32[]{:S(2)}) async-start(bf16[32,16,1664]{2,1,0:T(8,128)(2,1)} %bitcast.95), calls=%async_computation | async-start | bytes 3407872 | tf_op jit(solution)/shard_map/all_to_all | solution.py:878
  164.4 44.4 %all-to-all-start.1 = ((bf16[32,16,1664]{2,1,0:T(8,128)(2,1)}), bf16[32,16,1664]{2,1,0:T(8,128)(2,1)S(1)}, u32[]{:S(2)}, u32[]{:S(2)}) async-start(bf16[32,16,1664]{2,1,0:T(8,128)(2,1)} %get-tuple-element.78), calls=%async_computation.1 | async-start | bytes 3407872 | tf_op jit(solution)/shard_map/all_to_all | solution.py:889
  214.6 9.4 %collective-permute-start.14 = (f32[10,2,1280]{2,1,0:T(2,128)}, f32[10,2,1280]{2,1,0:T(2,128)S(1)}, u32[]{:S(2)}, u32[]{:S(2)}) collective-permute-start(f32[10,2,1280]{2,1,0:T(2,128)} %get-tuple-element.88), channel_id=1, source_target_pairs={{0,1},{1,2},{2,3},{3,4},{4,5},{5,6},{6,7},{8,9},{9,10},{10,11},{11... | collective-permute-start | bytes 307208 | tf_op jit(solution)/shard_map/ppermute | solution.py:483
  216.2 7.8 %collective-permute-start.15 = (f32[10,2,1280]{2,1,0:T(2,128)}, f32[10,2,1280]{2,1,0:T(2,128)S(1)}, u32[]{:S(2)}, u32[]{:S(2)}) collective-permute-start(f32[10,2,1280]{2,1,0:T(2,128)} %get-tuple-element.89), channel_id=1, source_target_pairs={{1,0},{2,1},{3,2},{4,3},{5,4},{6,5},{7,6},{9,8},{10,9},{11,10},{12... | collective-permute-start | bytes 307208 | tf_op jit(solution)/shard_map/ppermute | solution.py:484
  217.5 17.1 %collective-permute-start.12 = (bf16[10,2,32,256]{3,2,1,0:T(8,128)(2,1)}, bf16[10,2,32,256]{3,2,1,0:T(8,128)(2,1)S(1)}, u32[]{:S(2)}, u32[]{:S(2)}) collective-permute-start(bf16[10,2,32,256]{3,2,1,0:T(8,128)(2,1)} %get-tuple-element.86), channel_id=1, source_target_pairs={{0,8},{8,16},{16,24},{1,9},{9,17},{17,25},{2,10},{10,18},{18,26},{... | collective-permute-start | bytes 983048 | tf_op jit(solution)/shard_map/ppermute | solution.py:485
  220.1 14.5 %collective-permute-start.13 = (bf16[10,2,32,256]{3,2,1,0:T(8,128)(2,1)}, bf16[10,2,32,256]{3,2,1,0:T(8,128)(2,1)S(1)}, u32[]{:S(2)}, u32[]{:S(2)}) collective-permute-start(bf16[10,2,32,256]{3,2,1,0:T(8,128)(2,1)} %get-tuple-element.87), channel_id=1, source_target_pairs={{8,0},{16,8},{24,16},{9,1},{17,9},{25,17},{10,2},{18,10},{26,18},{... | collective-permute-start | bytes 983048 | tf_op jit(solution)/shard_map/ppermute | solution.py:486
  224.1 7.5 %collective-permute-start.16 = (f32[10,4,256]{2,1,0:T(4,128)S(1)}, f32[10,4,256]{2,1,0:T(4,128)S(1)}, u32[]{:S(2)}, u32[]{:S(2)}) collective-permute-start(f32[10,4,256]{2,1,0:T(4,128)S(1)} %get-tuple-element.114), channel_id=1, source_target_pairs={{0,8},{8,16},{16,24},{1,9},{9,17},{17,25},{2,10},{10,18},{18,26},{... | collective-permute-start | bytes 122888 | tf_op jit(solution)/shard_map/ppermute | solution.py:477
  228.6 6.0 %collective-permute-start.17 = (f32[10,4,256]{2,1,0:T(4,128)S(1)}, f32[10,4,256]{2,1,0:T(4,128)S(1)}, u32[]{:S(2)}, u32[]{:S(2)}) collective-permute-start(f32[10,4,256]{2,1,0:T(4,128)S(1)} %get-tuple-element.113), channel_id=1, source_target_pairs={{8,0},{16,8},{24,16},{9,1},{17,9},{25,17},{10,2},{18,10},{26,18},{... | collective-permute-start | bytes 122888 | tf_op jit(solution)/shard_map/ppermute | solution.py:478
  282.5 5.4 %collective-permute-start.19 = (f32[72,128]{1,0:T(8,128)S(1)}, f32[72,128]{1,0:T(8,128)S(1)}, u32[]{:S(2)}, u32[]{:S(2)}) collective-permute-start(f32[72,128]{1,0:T(8,128)S(1)} %add.49), channel_id=1, source_target_pairs={{0,2},{1,3},{2,0},{3,1},{4,6},{5,7},{6,4},{7,5},{8,10},{9,11},{10,... | collective-permute-start | bytes 110600 | tf_op jit(solution)/shard_map/ppermute | solution.py:461
  286.6 4.9 %collective-permute-start.21 = (f32[72,128]{1,0:T(8,128)S(1)}, f32[72,128]{1,0:T(8,128)S(1)}, u32[]{:S(2)}, u32[]{:S(2)}) collective-permute-start(f32[72,128]{1,0:T(8,128)S(1)} %add.49), channel_id=1, source_target_pairs={{0,6},{1,7},{2,4},{3,5},{4,2},{5,3},{6,0},{7,1},{8,14},{9,15},{10,... | collective-permute-start | bytes 110600 | tf_op jit(solution)/shard_map/ppermute | solution.py:461
  291.4 4.6 %collective-permute-start.22 = (f32[72,128]{1,0:T(8,128)S(1)}, f32[72,128]{1,0:T(8,128)S(1)}, u32[]{:S(2)}, u32[]{:S(2)}) collective-permute-start(f32[72,128]{1,0:T(8,128)S(1)} %add_add_fusion.1), channel_id=1, source_target_pairs={{0,8},{8,0},{16,24},{24,16},{1,9},{9,1},{17,25},{25,17},{2,10},{10... | collective-permute-start | bytes 110600 | tf_op jit(solution)/shard_map/ppermute | solution.py:461
  293.1 4.9 %collective-permute-start.23 = (f32[72,128]{1,0:T(8,128)S(1)}, f32[72,128]{1,0:T(8,128)S(1)}, u32[]{:S(2)}, u32[]{:S(2)}) collective-permute-start(f32[72,128]{1,0:T(8,128)S(1)} %add_add_fusion.1), channel_id=1, source_target_pairs={{0,16},{8,24},{16,0},{24,8},{1,17},{9,25},{17,1},{25,9},{2,18},{10... | collective-permute-start | bytes 110600 | tf_op jit(solution)/shard_map/ppermute | solution.py:461
  294.6 5.8 %collective-permute-start.24 = (f32[72,128]{1,0:T(8,128)S(1)}, f32[72,128]{1,0:T(8,128)S(1)}, u32[]{:S(2)}, u32[]{:S(2)}) collective-permute-start(f32[72,128]{1,0:T(8,128)S(1)} %add_add_fusion.1), channel_id=1, source_target_pairs={{0,24},{8,16},{16,8},{24,0},{1,25},{9,17},{17,9},{25,1},{2,26},{10... | collective-permute-start | bytes 110600 | tf_op jit(solution)/shard_map/ppermute | solution.py:461
  (31 other events, 260.3 us)
where the time goes:
time: 305 us; the launch traced here: 304 us
  Pallas kernels  186 us (61%)
  starting transfers between devices  63.3 us (21%)
  waiting for transfers between devices  32.4 us (11%)
  local copies, waits for them, and re-layouts  13 us (4%)
  other arithmetic  6.1 us (2%)
  between operations  3.11 us (1%)
    pallas_call x2, Pallas kernels, hidden_again(): pl.pallas_call(hidden_kernel, grid=(slices,), in_specs=[a_slice(own.shape...  70.1 us
    pallas_call x1, Pallas kernels, conv_backward(): pl.pallas_call(backward_kernel, grid=(slices, parts), in_specs=[of_slice(...  44.8 us
    pallas_call x1, Pallas kernels, conv_forward(): pl.pallas_call(forward_kernel, grid=(slices,), in_specs=[a_slice(own.shap...  40.7 us
    pallas_call x1, Pallas kernels, kspace_step(): pl.pallas_call(functools.partial(kspace_kernel, frames_here), grid=(slice...  18.8 us
    ppermute x3, starting transfers between devices, corners_along(): below = lax.ppermute(both[:, :, lanes - columns:], 'af', along('af', 1))  13.6 us
    ppermute x7, starting transfers between devices, other(): return lax.ppermute(values, axis, [(i, i ^ bits) for i in range(size)])  10 us
    ppermute x7, waiting for transfers between devices, other(): return lax.ppermute(values, axis, [(i, i ^ bits) for i in range(size)])  9.29 us
    ppermute x3, waiting for transfers between devices, corners_along(): above = lax.ppermute(both[:, :, :columns], 'af', along('af', -1))  8.52 us
  transfers between devices with their start and end apart: 27, of which 11 were waited for; matrix products, arithmetic and copies ran while one was open for 3% of the time, Pallas kernels for 23%

commit v1 on v0

--- a/solution.py
+++ b/solution.py
@@ -217,7 +217,7 @@
             elif t == frames + 1:
                 part_above[0, o] = here.astype(jnp.bfloat16)
             else:
-                base = volume[o, 8 : 8 + rows, t * columns : (t + 1) * columns] + bias_out[o]
+                base = volume[o, 8 : 8 + rows, t * columns : (t + 1) * columns] + bias_out[bias_out.shape[0] - 2 + o]
                 main[0, t - 1, :, o * columns : (o + 1) * columns] = base + here
     for at, out in ((7, part_left), (8 + rows, part_right)):
         both = [total[o, at : at + 1, :] for o in range(2)]
@@ -259,7 +259,7 @@
 ):
     edges, grad, grad_edges = refs[:EDGES], refs[EDGES], refs[EDGES + 1 : 2 * EDGES + 1]
     (
-        hidden, slopes, w_back, pick, extras, out,
+        hidden, slopes, w_back, pick, loss, sums, out,
         volume, windows, grad_windows, grads, sum_in, sum_out,
     ) = refs[2 * EDGES + 1 :]
     _, _, frames, rows, columns = own.shape
@@ -320,8 +320,14 @@
                 piece = folded.astype(jnp.bfloat16)
                 folded = folded - piece.astype(jnp.float32)
                 picked = picked + jnp.dot(piece, pick[index], preferred_element_type=jnp.float32)
-        out[0:width, :] = picked + extras[0:width, :]
-        out[width:, :] = extras[width:, :]
+        out[0:width, :] = picked
+        spot = lax.broadcasted_iota(jnp.int32, (8, PACKED), 1)
+        both = jnp.sum(sums[...], axis=1, keepdims=True)
+        values = (jnp.sum(loss[...], axis=(0, 1), keepdims=True), both[0:1], both[1:2])
+        row = jnp.zeros((8, PACKED), jnp.float32)
+        for k, value in enumerate(values):
+            row = jnp.where(spot == k, value, row)
+        out[width:, :] = row
 
 
 def whole(shape):
@@ -404,12 +410,13 @@
     )(own, *edges, w_in, *kept)
 
 
-def conv_backward(own, edges, grad, grad_edges, hidden, slopes, w_back, extras):
+def conv_backward(own, edges, grad, grad_edges, hidden, slopes, w_back, loss, sums):
     slices, _, frames, rows, columns = own.shape
     span = w_back.shape[1]
     volume, windows = conv_scratch(frames, rows, columns)
     total = pltpu.VMEM((2 * 128, span), jnp.float32)
-    fixed = (w_back, pick_table(), extras)
+    fixed = (w_back, pick_table(), loss, sums)
+    out_shape = jax.ShapeDtypeStruct((span // BLOCK + 8, PACKED), jnp.float32)
     here = (own, *edges, grad, *grad_edges)
     blocks = rows // BLOCK
     parts = 1
@@ -431,8 +438,8 @@
         in_specs=[of_slice(one.shape) for one in here]
         + [part_of_slice(one.shape) for one in (hidden, slopes)]
         + [all_of(one.shape) for one in fixed],
-        out_specs=all_of(extras.shape),
-        out_shape=jax.ShapeDtypeStruct(extras.shape, jnp.float32),
+        out_specs=all_of(out_shape.shape),
+        out_shape=out_shape,
         scratch_shapes=[
             volume,
             windows,
@@ -445,6 +452,19 @@
         cost_estimate=expected(5 * slices),
         name="conv_backward",
     )(*here, hidden, slopes, *fixed)
+
+
+def last_parts(array, axis):
+    if lax.axis_size(axis) != 4:
+        return [sum_over(array, axis)]
+    others = [
+        lax.ppermute(array, axis, [(i, i ^ k) for i in range(4)]) for k in (1, 2, 3)
+    ]
+    return [array, *others]
+
+
+def in_vmem(array):
+    return pltpu.with_memory_space_constraint(array, pltpu.VMEM)
 
 
 def along(axis, step):
@@ -561,7 +581,7 @@
         compiler_params=pltpu.CompilerParams(vmem_limit_bytes=VMEM),
         cost_estimate=expected(slices / 2),
         name="image_to_hybrid",
-    )(main, *added, table, note)
+    )(main, *map(in_vmem, added), table, note)
 
 
 def grad_image_kernel(hybrid, table, out, low, high, first, last, sums):
@@ -609,25 +629,16 @@
         compiler_params=pltpu.CompilerParams(vmem_limit_bytes=VMEM),
         cost_estimate=expected(slices / 2),
         name="hybrid_to_grad",
-    )(hybrid, table)
-
-
-def chunk_transpose(pieces, low_half, even):
-    a, c, b, d = pieces
-    a, b = (
-        jnp.where(low_half, a, pltpu.roll(b, 64, axis=1)),
-        jnp.where(low_half, pltpu.roll(a, 64, axis=1), b),
-    )
-    c, d = (
-        jnp.where(low_half, c, pltpu.roll(d, 64, axis=1)),
-        jnp.where(low_half, pltpu.roll(c, 64, axis=1), d),
-    )
-    return (
-        jnp.where(even, a, pltpu.roll(c, 32, axis=1)),
-        jnp.where(even, pltpu.roll(a, 96, axis=1), c),
-        jnp.where(even, b, pltpu.roll(d, 32, axis=1)),
-        jnp.where(even, pltpu.roll(b, 96, axis=1), d),
-    )
+    )(in_vmem(hybrid), table)
+
+
+def chunk_table():
+    index = np.arange(512).reshape(4, 4, 32)
+    return jnp.asarray(np.eye(512)[index.transpose(1, 0, 2).reshape(-1)], jnp.bfloat16)
+
+
+def beside(pieces):
+    return jnp.concatenate(pieces, axis=1)
 
 
 def kspace_slice(
@@ -657,7 +668,7 @@
         square = differ * differ + 1.0
         inverse = lax.rsqrt(square)
         loss_lanes[...] += (1.0 - mask) * (square * inverse - 1.0)
-        slopes.append((1.0 - mask) * differ * inverse * scale[0, 0])
+        slopes.append((1.0 - mask) * differ * inverse * scale[...])
     for s in range(frames):
         near = range(max(s - 2, 0), min(s + 3, frames))
         grad = sum(share[t, s] * slopes[t] for t in near)
@@ -671,40 +682,50 @@
 
 
 def kspace_kernel(
-    frames_here, received, measured, target, sampled, share, scale, table, out, loss,
-    spectrum, grads, loss_lanes,
+    frames_here, factor, received, measured, target, sampled, share, table, chunks,
+    out, loss, count, spectrum, grads, loss_lanes, scale,
 ):
     groups, _, lanes = received.shape
     pairs, n_af, _, twice = spectrum.shape
     rows = twice // 2
     n_row = groups // n_af
     step = pl.program_id(0)
-    lane = lax.broadcasted_iota(jnp.int32, (SIDE, 128), 1)
-    low_half = lane < 64
-    even = lane % 64 < 32
+    tiles = lanes // 128
+    size = out.shape[1]
 
     @pl.when(step == 0)
     def _():
         loss_lanes[...] = jnp.zeros_like(loss_lanes)
-        def gather(af, carry):
-            for tile in range(lanes // 128):
-                for h in range(n_row // 4):
-                    source = [
-                        received[af * n_row + h * 4 + m, :, tile * 128 : (tile + 1) * 128]
-                        for m in range(4)
-                    ]
-                    moved = chunk_transpose(source, low_half, even)
-                    for k in range(4):
-                        if tile * 4 + k < pairs:
-                            wide = moved[k].astype(jnp.float32)
-                            for c in range(2):
-                                at = c * rows + h * 128
-                                spectrum[tile * 4 + k, af, :, at : at + 128] = wide[
-                                    c * 8 : (c + 1) * 8
-                                ]
-            return carry
-
-        lax.fori_loop(0, n_af, gather, 0)
+        last = slice((tiles - 1) * 128, lanes)
+        notes = sum(received[group, 0:size, last].astype(jnp.float32) for group in range(groups))
+        at = pairs * (128 // 4) - (tiles - 1) * 128
+        total = notes[0:1, at : at + 1] * factor
+        count[...] = jnp.broadcast_to(total, count.shape)
+        scale[...] = jnp.broadcast_to(1.0 / total, scale.shape)
+        for h in range(n_row // 4):
+            for af in range(n_af):
+                source = [
+                    beside(
+                        [
+                            received[af * n_row + h * 4 + m, :, tile * 128 : (tile + 1) * 128]
+                            for m in range(4)
+                        ]
+                    )
+                    for tile in range(tiles)
+                ]
+                moved = jnp.dot(
+                    jnp.concatenate(source, axis=0),
+                    chunks[...],
+                    preferred_element_type=jnp.float32,
+                )
+                for pair in range(pairs):
+                    tile, k = pair // 4, pair % 4
+                    for c in range(2):
+                        at = c * rows + h * 128
+                        start = tile * size + c * 8
+                        spectrum[pair, af, :, at : at + 128] = moved[
+                            start : start + 8, k * 128 : (k + 1) * 128
+                        ]
 
     each = measured.shape[0]
     for k in range(each):
@@ -717,62 +738,69 @@
     def _():
         loss[...] = loss_lanes[...]
 
-        def scatter(af, carry):
-            for tile in range(lanes // 128):
-                for h in range(n_row // 4):
-                    source = []
+        for h in range(n_row // 4):
+            for af in range(n_af):
+                source = []
+                for tile in range(tiles):
+                    four = []
                     for k in range(4):
                         pair = min(tile * 4 + k, pairs - 1)
                         both = [
                             spectrum[pair, af, :, c * rows + h * 128 : c * rows + h * 128 + 128]
                             for c in range(2)
                         ]
-                        source.append(jnp.concatenate(both, axis=0).astype(jnp.bfloat16))
-                    moved = chunk_transpose(source, low_half, even)
-                    for m in range(4):
-                        out[af * n_row + h * 4 + m, :, tile * 128 : (tile + 1) * 128] = moved[m]
-            return carry
-
-        lax.fori_loop(0, n_af, scatter, 0)
-
-
-def kspace_step(received, measured, target, sampled, share, scale, table, frames_here, group):
+                        four.append(jnp.concatenate(both, axis=0).astype(jnp.bfloat16))
+                    source.append(beside(four))
+                moved = jnp.dot(
+                    jnp.concatenate(source, axis=0),
+                    chunks[...],
+                    preferred_element_type=jnp.float32,
+                ).astype(jnp.bfloat16)
+                for m in range(4):
+                    for tile in range(tiles):
+                        out[af * n_row + h * 4 + m, :, tile * 128 : (tile + 1) * 128] = moved[
+                            tile * size : (tile + 1) * size, m * 128 : (m + 1) * 128
+                        ]
+
+
+def kspace_step(received, measured, target, sampled, share, table, frames_here, factor):
     _, frames, lines, twice = measured.shape
-    first, slices = group
+    slices = measured.shape[0]
     n_af = frames // frames_here
-    each = 2 if slices % 2 == 0 and first % 2 == 0 else 1
+    each = 2 if slices % 2 == 0 else 1
+    chunks = chunk_table()
 
     def some(shape):
-        start = first // each
-        return pl.BlockSpec((each,) + tuple(shape[1:]), lambda s: (s + start, 0, 0, 0))
-
-    smem = pl.BlockSpec(memory_space=pltpu.SMEM)
+        return pl.BlockSpec((each,) + tuple(shape[1:]), lambda s: (s, 0, 0, 0))
+
     return pl.pallas_call(
-        functools.partial(kspace_kernel, frames_here),
+        functools.partial(kspace_kernel, frames_here, factor),
         grid=(slices // each,),
         in_specs=[
-            whole(received.shape),
+            pl.BlockSpec(memory_space=pltpu.VMEM),
             some(measured.shape),
             some(target.shape),
             whole(sampled.shape),
-            smem,
-            smem,
+            pl.BlockSpec(memory_space=pltpu.SMEM),
             whole(table.shape),
+            whole(chunks.shape),
         ],
-        out_specs=[whole(received.shape), whole((lines, twice))],
+        out_specs=[whole(received.shape), whole((lines, twice)), whole((8, 128))],
         out_shape=[
             jax.ShapeDtypeStruct(received.shape, jnp.bfloat16),
             jax.ShapeDtypeStruct((lines, twice), jnp.float32),
+            jax.ShapeDtypeStruct((8, 128), jnp.float32),
         ],
         scratch_shapes=[
             pltpu.VMEM((slices * frames_here, n_af, lines, twice), jnp.float32),
             pltpu.VMEM((each, frames * lines, twice), jnp.float32),
             pltpu.VMEM((lines, twice), jnp.float32),
+            pltpu.VMEM((lines, twice), jnp.float32),
         ],
         compiler_params=pltpu.CompilerParams(vmem_limit_bytes=VMEM),
         cost_estimate=expected(3 * slices),
         name="kspace",
-    )(received, measured, target, sampled, share, scale, table)
+    )(in_vmem(received), measured, target, sampled, share, table, chunks)
 
 
 def middle_plain(main, added, measured, target, sampled, share, table_y, table_x):
@@ -819,11 +847,16 @@
         preferred_element_type=jnp.float32,
     ).reshape(slices, frames_here, rows_here, 2, columns)
     grad = jnp.transpose(grad, (0, 3, 1, 2, 4)).astype(jnp.bfloat16)
-    return loss, count, grad, jnp.sum(grad.astype(jnp.float32), axis=(0, 2, 3, 4))
-
-
-def update_kernel(total, *refs):
-    ins, outs = refs[:12], refs[12:]
+    return loss, jnp.broadcast_to(count, (8, 128)), grad, jnp.sum(grad.astype(jnp.float32), axis=(0, 2, 3, 4))
+
+
+def update_kernel(parts, *refs):
+    count, *ins = refs[parts : parts + 13]
+    outs = refs[parts + 13 :]
+    total = refs[0][...]
+    if parts == 4:
+        total = (total + refs[1][...]) + (refs[2][...] + refs[3][...])
+    *outs, loss, unsampled = outs
     taps, width = ins[0].shape
     turned = total[0:width, :].T
 
@@ -841,25 +874,23 @@
         step(1, tap, turned[start : start + 2, :])
     step(2, (slice(0, 1), slice(0, width)), turned[54:55, :])
     step(2, (slice(0, 1), slice(width, width + 2)), total[width : width + 1, 1:3])
-
-
-def update(total, weights, firsts, seconds, smooths):
+    loss[...] = total[width : width + 1, 0:1]
+    unsampled[...] = count[0:1, 0:1]
+
+
+def update(parts, count, weights, firsts, seconds, smooths):
     arrays = [*weights, *firsts, *seconds, *smooths]
     turn = {1: lambda one: one.reshape(1, -1), 2: jnp.transpose, 3: lambda one: one}
     arrays = [turn[one.ndim](one) for one in arrays]
     kinds = [jnp.float32] * 4 + [jnp.bfloat16]
-    outs = pl.pallas_call(
-        update_kernel,
-        out_shape=[jax.ShapeDtypeStruct(one.shape, kind) for kind in kinds for one in arrays[:3]],
+    *outs, loss, unsampled = pl.pallas_call(
+        functools.partial(update_kernel, len(parts)),
+        out_shape=[jax.ShapeDtypeStruct(one.shape, kind) for kind in kinds for one in arrays[:3]]
+        + [jax.ShapeDtypeStruct((1, 1), jnp.float32)] * 2,
         name="update",
-    )(total, *arrays)
+    )(*map(in_vmem, parts), count, *arrays)
     back = (jnp.transpose, lambda one: one, lambda one: one.reshape(-1))
-    return [back[k % 3](one) for k, one in enumerate(outs)]
-
-
-def packed_extras(width, loss, sums):
-    row = jnp.concatenate([loss.reshape(1), sums])
-    return jnp.pad(row.reshape(1, 3), ((width, 7), (0, PACKED - 3)))
+    return loss[0, 0], unsampled[0, 0], *[back[k % 3](one) for k, one in enumerate(outs)]
 
 
 def middle_fast(
@@ -873,6 +904,7 @@
     permuted = jnp.asarray(np.ascontiguousarray(table_y[:, order].T), jnp.bfloat16)
     mask = jnp.broadcast_to(sampled[:, :, None], sampled.shape + (readout,))
     note = jnp.sum(1.0 - sampled).reshape(1, 1)
+    mask, share, *added = lax.optimization_barrier((mask, share, *added))
     lanes = (size // 128 + 1) * 128
     hybrid = image_to_hybrid(main, added, permuted, note, lanes)
     received = lax.all_to_all(
@@ -880,18 +912,16 @@
     )
     first = between(hybrid)
     received, first = lax.optimization_barrier((received, first))
-    notes = received[:, 0, size].astype(jnp.float32)
-    count = jnp.sum(notes) * (1.0 * slices * readout)
-    back, loss = kspace_step(
-        received, measured, target, mask, share, (1.0 / count).reshape(1, 1),
-        jnp.asarray(table_x, jnp.bfloat16), frames_here, (0, slices),
+    back, loss, count = kspace_step(
+        received, measured, target, mask, share, jnp.asarray(table_x, jnp.bfloat16),
+        frames_here, 1.0 * slices * readout,
     )
     returned = lax.all_to_all(back, AXES, 0, 0, tiled=True)
     second = after(back, first)
     returned, second = lax.optimization_barrier((returned, second))
     shape = (slices, 2, frames_here, rows, twice // 2)
     grad, *grad_edge, sums = hybrid_to_grad(returned.reshape(twice, lanes), permuted, shape)
-    return jnp.sum(loss), count, grad, grad_edge, jnp.sum(sums, axis=1), second
+    return loss, count, grad, grad_edge, sums, second
 
 
 def train_step(
@@ -927,16 +957,18 @@
         )
         kept = None
     around = share_edges(*grad_edge)
-    total = packed_extras(w_in.shape[0] // BLOCK, loss, sums)
     if kept is not None:
-        return count, conv_backward(image_in, edges, grad, around, *kept, w_back, total)
+        return count, conv_backward(image_in, edges, grad, around, *kept, w_back, loss, sums)
+    total = 0.0
+    loss, sums = loss.reshape(1, 1), sums.reshape(2, 1)
     for first, size in groups:
         own, *sides = (one[first : first + size] for one in (image_in, *edges, grad, *around))
         held, _ = lax.optimization_barrier((w_in.T, total))
         kept = hidden_again(own, sides[:EDGES], (0, size), held)
-        total = conv_backward(
-            own, sides[:EDGES], sides[EDGES], sides[EDGES + 1 :], *kept, w_back, total
+        total += conv_backward(
+            own, sides[:EDGES], sides[EDGES], sides[EDGES + 1 :], *kept, w_back, loss, sums
         )
+        loss, sums = 0.0 * loss, 0.0 * sums
     return count, total
 
 
@@ -959,17 +991,16 @@
 
     count, total = train_step(
         image_in, measured, target, sampled, share, table_y, table_x,
-        w_in, w_out, w_back, biases[width:],
+        w_in, w_out, w_back, biases,
     )
-    total = sum_over(sum_over(total, "row"), "af")
-    outs = update(
-        total,
+    return update(
+        last_parts(sum_over(total, "row"), "af"),
+        count,
         (in_kernel, out_kernel, biases),
         (in_moment, out_moment, bias_moment),
         (in_square, out_square, bias_square),
         (in_smooth, out_smooth, bias_smooth),
     )
-    return (total[width, 0], count, *outs)
 
 
 def solution(mesh):

time: 305 us -> 290 us (0.951)
  Pallas kernels: 186 us -> 180 us
  local copies, waits for them, and re-layouts: 13 us -> 9.2 us
    ppermute x7 -> x4, starting transfers between devices: 10 us -> 4.19 us  [other(): return lax.ppermute(values, axis, [(i, i ^ bits) for i in range(size)])]
    pallas_call x2, Pallas kernels: 20.6 us -> 15.5 us  [the longest x1 13.7 us: kspace_step(): pl.pallas_call(functools.partial(kspace_kernel, frames_here, factor), gri...]
    ppermute x1, waiting for transfers between devices: 5.03 us -> 0.01 us  [return_edges(): lower = lax.ppermute(part_left, 'row', along('row', -1))]
    ppermute x0 -> x3, starting transfers between devices: none -> 4.56 us  [last_parts(): lax.ppermute(array, axis, [(i, i ^ k) for i in range(4)])]
    ppermute x7 -> x4, waiting for transfers between devices: 9.29 us -> 4.79 us  [other(): return lax.ppermute(values, axis, [(i, i ^ bits) for i in range(size)])]
    ppermute x0 -> x3, waiting for transfers between devices: none -> 4.37 us  [last_parts(): lax.ppermute(array, axis, [(i, i ^ k) for i in range(4)])]
  transfers between devices with their start and end apart: 27 -> 27, of which waited for: 11 -> 10; matrix products, arithmetic and copies ran while one was open for 3% -> 2% of each run, Pallas kernels for 23% -> 24%
where the time goes in v1:
time: 290 us; the launch traced here: 288 us
  Pallas kernels  180 us (62%)
  starting transfers between devices  63.9 us (22%)
  waiting for transfers between devices  30.6 us (11%)
  local copies, waits for them, and re-layouts  9.2 us (3%)
  other arithmetic  3.09 us (1%)
    pallas_call x2, Pallas kernels, hidden_again(): pl.pallas_call(hidden_kernel, grid=(slices,), in_specs=[a_slice(own.shape...  70.2 us
    pallas_call x1, Pallas kernels, conv_backward(): pl.pallas_call(backward_kernel, grid=(slices, parts), in_specs=[of_slice(...  44.8 us
    pallas_call x1, Pallas kernels, conv_forward(): pl.pallas_call(forward_kernel, grid=(slices,), in_specs=[a_slice(own.shap...  40.7 us
    pallas_call x1, Pallas kernels, kspace_step(): pl.pallas_call(functools.partial(kspace_kernel, frames_here, factor), gri...  13.7 us
    ppermute x3, starting transfers between devices, corners_along(): below = lax.ppermute(both[:, :, lanes - columns:], 'af', along('af', 1))  13.6 us
    ppermute x3, waiting for transfers between devices, corners_along(): above = lax.ppermute(both[:, :, :columns], 'af', along('af', -1))  11 us
    all_to_all x1, starting transfers between devices, middle_fast(): lax.all_to_all(hybrid.reshape(devices, 2 * lines, lanes), AXES, 0, 0, til...  9.07 us
    ppermute x2, starting transfers between devices, share_edges(): below = lax.ppermute(high, 'af', along('af', 1))  6.99 us
  transfers between devices with their start and end apart: 27, of which 10 were waited for; matrix products, arithmetic and copies ran while one was open for 2% of the time, Pallas kernels for 24%

profile of v1, /device:TPU:0, one launch (start us, length us, event | category | flops | bytes accessed | tf_op | source)
XLA Modules:
  0.0 288.5 jit_solution(11111598213995244307)
XLA Ops:
  2.3 2.4 collective-permute-start.2
  7.2 4.3 %collective-permute-start = (bf16[10,2,32,256]{3,2,1,0:T(8,128)(2,1)S(1)}, bf16[10,2,32,256]{3,2,1,0:T(8,128)(2,1)S(1)}, u32[]{:S(2)}, u32[]{:S(2)}) collective-permute-start(bf16[10,2,32,256]{3,2,1,0:T(8,128)(2,1)S(1)} %get-tuple-element.134), channel_id=1, source_target_pairs={{0,8},{8,16},{16,24},{1,9},{9,17},{17,25},{2,10},{10,18},{18,26},{... | collective-permute-start | bytes 983048 | tf_op jit(solution)/shard_map/ppermute | solution.py:505
  13.6 4.5 %collective-permute-start.4 = (bf16[10,4,256]{2,1,0:T(4,128)(2,1)S(1)}, bf16[10,4,256]{2,1,0:T(4,128)(2,1)S(1)}, u32[]{:S(2)}, u32[]{:S(2)}) collective-permute-start(bf16[10,4,256]{2,1,0:T(4,128)(2,1)S(1)} %get-tuple-element.140), channel_id=1, source_target_pairs={{0,8},{8,16},{16,24},{1,9},{9,17},{17,25},{2,10},{10,18},{18,26},{... | collective-permute-start | bytes 61448 | tf_op jit(solution)/shard_map/ppermute | solution.py:497
  21.7 2.4 collective-permute-done.5.refs_5_
  25.6 40.7 %conv_forward.1 = (f32[10,5,32,512]{3,2,1,0:T(8,128)}, bf16[10,2,32,256]{3,2,1,0:T(8,128)(2,1)}, bf16[10,2,32,256]{3,2,1,0:T(8,128)(2,1)}, bf16[10,2,1792]{2,1,0:T(2,128)(2,1)}, bf16[10,2,1792]{2,1,0:T(2,128)(2,1)}) custom-call(bf16[10,2,5,32,256]{4,3,2,1,0:T(8,128)(2,1)} %own.7, bf16[10,2,32,256]{3,2,1,0:T(8,128)(2,1)} %copy-done.1, ...), custom_call_target="tpu_custom_call" | custom-call | flops 69000003584 | tf_op jit(solution)/shard_map/conv_forward/pallas_call | solution.py:369
  66.4 2.0 collective-permute-start.8
  69.7 3.5 %collective-permute-start.6 = (bf16[10,2,32,256]{3,2,1,0:T(8,128)(2,1)}, bf16[10,2,32,256]{3,2,1,0:T(8,128)(2,1)S(1)}, u32[]{:S(2)}, u32[]{:S(2)}) collective-permute-start(bf16[10,2,32,256]{3,2,1,0:T(8,128)(2,1)} %get-tuple-element.81), channel_id=1, source_target_pairs={{0,8},{8,16},{16,24},{1,9},{9,17},{17,25},{2,10},{10,18},{18,26},{... | collective-permute-start | bytes 983048 | tf_op jit(solution)/shard_map/ppermute | solution.py:525
  75.2 4.5 %collective-permute-start.10 = (bf16[10,4,256]{2,1,0:T(4,128)(2,1)S(1)}, bf16[10,4,256]{2,1,0:T(4,128)(2,1)S(1)}, u32[]{:S(2)}, u32[]{:S(2)}) collective-permute-start(bf16[10,4,256]{2,1,0:T(4,128)(2,1)S(1)} %get-tuple-element.138), channel_id=1, source_target_pairs={{0,8},{8,16},{16,24},{1,9},{9,17},{17,25},{2,10},{10,18},{18,26},{... | collective-permute-start | bytes 61448 | tf_op jit(solution)/shard_map/ppermute | solution.py:497
  81.8 4.0 %collective-permute-done.11.corner_above = bf16[10,4,256]{2,1,0:T(4,128)(2,1)S(1)} collective-permute-done((bf16[10,4,256]{2,1,0:T(4,128)(2,1)S(1)}, bf16[10,4,256]{2,1,0:T(4,128)(2,1)S(1)}, u32[]{:S(2)}, u32[]{:S(2)}) %collective-permute-start.11) | collective-permute-done | bytes 20512 | tf_op jit(solution)/shard_map/ppermute | solution.py:498
  86.6 5.0 %image_to_hybrid.1 = bf16[512,1664]{1,0:T(8,128)(2,1)} custom-call(f32[10,5,32,512]{3,2,1,0:T(8,128)} %get-tuple-element.80.main, bf16[10,2,32,256]{3,2,1,0:T(8,128)(2,1)S(1)} %collective-permute-done.6.from_below, bf16[10,2,32,256]{3,2,1,0:T(8,128)(2,1)S(1)} %collective-permute-done.7.from_above, bf16[10,2,1792]{2,1,0:T(2,128)(2,1)S(1)} %collective-permute-done.8.upper, ...), custom_call_target="tpu_custom_call" | custom-call | flops 5750000128 | tf_op jit(solution)/shard_map/image_to_hybrid/pallas_call | solution.py:575
  91.6 9.1 %all-to-all-start = ((bf16[32,16,1664]{2,1,0:T(8,128)(2,1)}), bf16[32,16,1664]{2,1,0:T(8,128)(2,1)S(1)}, u32[]{:S(2)}, u32[]{:S(2)}) async-start(bf16[32,16,1664]{2,1,0:T(8,128)(2,1)} %bitcast.92), calls=%async_computation | async-start | bytes 3407872 | tf_op jit(solution)/shard_map/all_to_all | solution.py:910
  100.7 35.0 %hidden_again.2 = (bf16[10,8,1280,256]{3,2,1,0:T(8,128)(2,1)}, bf16[10,8,1280,256]{3,2,1,0:T(8,128)(2,1)}) custom-call(bf16[10,2,5,32,256]{4,3,2,1,0:T(8,128)(2,1)} %own.7, bf16[10,2,32,256]{3,2,1,0:T(8,128)(2,1)} %copy-done.1, bf16[10,2,32,256]{3,2,1,0:T(8,128)(2,1)} %copy-done.2, bf16[10,2,1280]{2,1,0:T(2,128)(2,1)} %copy-done.3, ...), custom_call_target="tpu_custom_call" | custom-call | flops 28750000128 | tf_op jit(solution)/shard_map/hidden_again/pallas_call | solution.py:396
  135.7 5.3 %all-to-all-done.received = bf16[32,16,1664]{2,1,0:T(8,128)(2,1)S(1)} async-done(((bf16[32,16,1664]{2,1,0:T(8,128)(2,1)}), bf16[32,16,1664]{2,1,0:T(8,128)(2,1)S(1)}, u32[]{:S(2)}, u32[]{:S(2)}) %all-to-all-start) | async-done | bytes 1703968 | tf_op jit(solution)/shard_map/all_to_all | solution.py:910
  141.0 13.7 %kspace.1 = (bf16[32,16,1664]{2,1,0:T(8,128)(2,1)}, f32[8,512]{1,0:T(8,128)}, f32[8,128]{1,0:T(8,128)}) custom-call(bf16[32,16,1664]{2,1,0:T(8,128)(2,1)S(1)} %all-to-all-done.received, f32[10,20,8,512]{3,2,1,0:T(8,128)} %measured.1, f32[10,20,8,512]{3,2,1,0:T(8,128)} %target.1, f32[20,8,512]{2,1,0:T(8,128)} %broadcast_in_dim.2.sampled, ...), custom_call_target="tpu_custom_call" | custom-call | flops 34500001792 | tf_op jit(solution)/shard_map/kspace/pallas_call | solution.py:776
  154.7 4.1 %all-to-all-start.1 = ((bf16[32,16,1664]{2,1,0:T(8,128)(2,1)}), bf16[32,16,1664]{2,1,0:T(8,128)(2,1)S(1)}, u32[]{:S(2)}, u32[]{:S(2)}) async-start(bf16[32,16,1664]{2,1,0:T(8,128)(2,1)} %get-tuple-element.97), calls=%async_computation.1 | async-start | bytes 3407872 | tf_op jit(solution)/shard_map/all_to_all | solution.py:919
  158.8 35.1 %hidden_again.3 = (bf16[10,8,1280,256]{3,2,1,0:T(8,128)(2,1)}, bf16[10,8,1280,256]{3,2,1,0:T(8,128)(2,1)}) custom-call(bf16[10,2,5,32,256]{4,3,2,1,0:T(8,128)(2,1)} %own.7, bf16[10,2,32,256]{3,2,1,0:T(8,128)(2,1)} %copy-done.1, bf16[10,2,32,256]{3,2,1,0:T(8,128)(2,1)} %copy-done.2, ...), custom_call_target="tpu_custom_call", output_to_operand_aliasing={{0}: (8, {}), {1}: (9, {})} | custom-call | flops 28750000128 | tf_op jit(solution)/shard_map/hidden_again/pallas_call | solution.py:396
  194.0 5.2 %all-to-all-done.1 = bf16[32,16,1664]{2,1,0:T(8,128)(2,1)S(1)} async-done(((bf16[32,16,1664]{2,1,0:T(8,128)(2,1)}), bf16[32,16,1664]{2,1,0:T(8,128)(2,1)S(1)}, u32[]{:S(2)}, u32[]{:S(2)}) %all-to-all-start.1) | async-done | bytes 1703968 | tf_op jit(solution)/shard_map/all_to_all | solution.py:919
  199.1 4.0 %hybrid_to_grad.1 = (bf16[10,2,5,32,256]{4,3,2,1,0:T(8,128)(2,1)}, bf16[10,2,32,256]{3,2,1,0:T(8,128)(2,1)}, bf16[10,2,32,256]{3,2,1,0:T(8,128)(2,1)}, f32[10,2,...) custom-call(bf16[512,1664]{1,0:T(8,128)(2,1)S(1)} %bitcast.91, bf16[512,512]{1,0:T(8,128)(2,1)} %constant.55.clone.table), custom_call_target="tpu_custom_call" | custom-call | flops 5750000128 | tf_op jit(solution)/shard_map/hybrid_to_grad/pallas_call | solution.py:619
  206.0 2.7 collective-permute-start.12
  210.2 4.5 %collective-permute-start.16 = (f32[10,4,256]{2,1,0:T(4,128)S(1)}, f32[10,4,256]{2,1,0:T(4,128)S(1)}, u32[]{:S(2)}, u32[]{:S(2)}) collective-permute-start(f32[10,4,256]{2,1,0:T(4,128)S(1)} %get-tuple-element.136), channel_id=1, source_target_pairs={{0,8},{8,16},{16,24},{1,9},{9,17},{17,25},{2,10},{10,18},{18,26},{... | collective-permute-start | bytes 122888 | tf_op jit(solution)/shard_map/ppermute | solution.py:497
  217.5 4.6 %collective-permute-done.17.refs_12_ = f32[10,4,256]{2,1,0:T(4,128)S(1)} collective-permute-done((f32[10,4,256]{2,1,0:T(4,128)S(1)}, f32[10,4,256]{2,1,0:T(4,128)S(1)}, u32[]{:S(2)}, u32[]{:S(2)}) %collective-permute-start.17) | collective-permute-done | bytes 40992 | tf_op jit(solution)/shard_map/ppermute | solution.py:498
  223.0 44.8 %conv_backward.1 = f32[72,128]{1,0:T(8,128)} custom-call(bf16[10,2,5,32,256]{4,3,2,1,0:T(8,128)(2,1)} %own.7, bf16[10,2,32,256]{3,2,1,0:T(8,128)(2,1)} %copy-done.1, bf16[10,2,32,256]{3,2,1,0:T(8,128)(2,1)} %copy-done.2, bf16[10,2,1280]{2,1,0:T(2,128)(2,1)} %copy-done.3, bf16[10,2,1280]{2,1,0:T(2,128)(2,1)} %copy-done.4, bf16[10,4,256]{2,1,0:T(4,128)(2,1)} %copy-done.9, ...), custom_call_target="tpu_custom_call" | custom-call | flops 57500000256 | tf_op jit(solution)/shard_map/conv_backward/pallas_call | solution.py:435
  282.1 2.0 collective-permute-done.23.refs_2_
  284.1 2.4 collective-permute-done.24.refs_3_
  (113 shorter events, 41.1 us)
Async XLA Ops:
  2.3 11.2 %collective-permute-start.2 = (bf16[10,2,1280]{2,1,0:T(2,128)(2,1)S(1)}, bf16[10,2,1280]{2,1,0:T(2,128)(2,1)S(1)}, u32[]{:S(2)}, u32[]{:S(2)}) collective-permute-start(bf16[10,2,1280]{2,1,0:T(2,128)(2,1)S(1)} %reshape_squeeze.6), channel_id=1, source_target_pairs={{0,1},{1,2},{2,3},{3,4},{4,5},{5,6},{6,7},{8,9},{9,10},{10,11},{11... | collective-permute-start | bytes 153608 | tf_op jit(solution)/shard_map/ppermute | solution.py:503
  4.8 8.8 %collective-permute-start.3 = (bf16[10,2,1280]{2,1,0:T(2,128)(2,1)S(1)}, bf16[10,2,1280]{2,1,0:T(2,128)(2,1)S(1)}, u32[]{:S(2)}, u32[]{:S(2)}) collective-permute-start(bf16[10,2,1280]{2,1,0:T(2,128)(2,1)S(1)} %reshape_squeeze.7), channel_id=1, source_target_pairs={{1,0},{2,1},{3,2},{4,3},{5,4},{6,5},{7,6},{9,8},{10,9},{11,10},{12... | collective-permute-start | bytes 153608 | tf_op jit(solution)/shard_map/ppermute | solution.py:504
  7.2 17.0 %collective-permute-start = (bf16[10,2,32,256]{3,2,1,0:T(8,128)(2,1)S(1)}, bf16[10,2,32,256]{3,2,1,0:T(8,128)(2,1)S(1)}, u32[]{:S(2)}, u32[]{:S(2)}) collective-permute-start(bf16[10,2,32,256]{3,2,1,0:T(8,128)(2,1)S(1)} %get-tuple-element.134), channel_id=1, source_target_pairs={{0,8},{8,16},{16,24},{1,9},{9,17},{17,25},{2,10},{10,18},{18,26},{... | collective-permute-start | bytes 983048 | tf_op jit(solution)/shard_map/ppermute | solution.py:505
  11.5 12.6 %collective-permute-start.1 = (bf16[10,2,32,256]{3,2,1,0:T(8,128)(2,1)S(1)}, bf16[10,2,32,256]{3,2,1,0:T(8,128)(2,1)S(1)}, u32[]{:S(2)}, u32[]{:S(2)}) collective-permute-start(bf16[10,2,32,256]{3,2,1,0:T(8,128)(2,1)S(1)} %get-tuple-element.133), channel_id=1, source_target_pairs={{8,0},{16,8},{24,16},{9,1},{17,9},{25,17},{10,2},{18,10},{26,18},{... | collective-permute-start | bytes 983048 | tf_op jit(solution)/shard_map/ppermute | solution.py:506
  13.6 8.1 %collective-permute-start.4 = (bf16[10,4,256]{2,1,0:T(4,128)(2,1)S(1)}, bf16[10,4,256]{2,1,0:T(4,128)(2,1)S(1)}, u32[]{:S(2)}, u32[]{:S(2)}) collective-permute-start(bf16[10,4,256]{2,1,0:T(4,128)(2,1)S(1)} %get-tuple-element.140), channel_id=1, source_target_pairs={{0,8},{8,16},{16,24},{1,9},{9,17},{17,25},{2,10},{10,18},{18,26},{... | collective-permute-start | bytes 61448 | tf_op jit(solution)/shard_map/ppermute | solution.py:497
  18.2 6.0 %collective-permute-start.5 = (bf16[10,4,256]{2,1,0:T(4,128)(2,1)S(1)}, bf16[10,4,256]{2,1,0:T(4,128)(2,1)S(1)}, u32[]{:S(2)}, u32[]{:S(2)}) collective-permute-start(bf16[10,4,256]{2,1,0:T(4,128)(2,1)S(1)} %get-tuple-element.139), channel_id=1, source_target_pairs={{8,0},{16,8},{24,16},{9,1},{17,9},{25,17},{10,2},{18,10},{26,18},{... | collective-permute-start | bytes 61448 | tf_op jit(solution)/shard_map/ppermute | solution.py:498
  66.4 8.8 %collective-permute-start.8 = (bf16[10,2,1792]{2,1,0:T(2,128)(2,1)}, bf16[10,2,1792]{2,1,0:T(2,128)(2,1)S(1)}, u32[]{:S(2)}, u32[]{:S(2)}) collective-permute-start(bf16[10,2,1792]{2,1,0:T(2,128)(2,1)} %get-tuple-element.83), channel_id=1, source_target_pairs={{0,1},{1,2},{2,3},{3,4},{4,5},{5,6},{6,7},{8,9},{9,10},{10,11},{11... | collective-permute-start | bytes 215048 | tf_op jit(solution)/shard_map/ppermute | solution.py:523
  68.4 6.8 %collective-permute-start.9 = (bf16[10,2,1792]{2,1,0:T(2,128)(2,1)}, bf16[10,2,1792]{2,1,0:T(2,128)(2,1)S(1)}, u32[]{:S(2)}, u32[]{:S(2)}) collective-permute-start(bf16[10,2,1792]{2,1,0:T(2,128)(2,1)} %get-tuple-element.84), channel_id=1, source_target_pairs={{1,0},{2,1},{3,2},{4,3},{5,4},{6,5},{7,6},{9,8},{10,9},{11,10},{12... | collective-permute-start | bytes 215048 | tf_op jit(solution)/shard_map/ppermute | solution.py:522
  69.7 16.0 %collective-permute-start.6 = (bf16[10,2,32,256]{3,2,1,0:T(8,128)(2,1)}, bf16[10,2,32,256]{3,2,1,0:T(8,128)(2,1)S(1)}, u32[]{:S(2)}, u32[]{:S(2)}) collective-permute-start(bf16[10,2,32,256]{3,2,1,0:T(8,128)(2,1)} %get-tuple-element.81), channel_id=1, source_target_pairs={{0,8},{8,16},{16,24},{1,9},{9,17},{17,25},{2,10},{10,18},{18,26},{... | collective-permute-start | bytes 983048 | tf_op jit(solution)/shard_map/ppermute | solution.py:525
  73.2 12.6 %collective-permute-start.7 = (bf16[10,2,32,256]{3,2,1,0:T(8,128)(2,1)}, bf16[10,2,32,256]{3,2,1,0:T(8,128)(2,1)S(1)}, u32[]{:S(2)}, u32[]{:S(2)}) collective-permute-start(bf16[10,2,32,256]{3,2,1,0:T(8,128)(2,1)} %get-tuple-element.82), channel_id=1, source_target_pairs={{8,0},{16,8},{24,16},{9,1},{17,9},{25,17},{10,2},{18,10},{26,18},{... | collective-permute-start | bytes 983048 | tf_op jit(solution)/shard_map/ppermute | solution.py:524
  75.2 6.6 %collective-permute-start.10 = (bf16[10,4,256]{2,1,0:T(4,128)(2,1)S(1)}, bf16[10,4,256]{2,1,0:T(4,128)(2,1)S(1)}, u32[]{:S(2)}, u32[]{:S(2)}) collective-permute-start(bf16[10,4,256]{2,1,0:T(4,128)(2,1)S(1)} %get-tuple-element.138), channel_id=1, source_target_pairs={{0,8},{8,16},{16,24},{1,9},{9,17},{17,25},{2,10},{10,18},{18,26},{... | collective-permute-start | bytes 61448 | tf_op jit(solution)/shard_map/ppermute | solution.py:497
  79.8 6.0 %collective-permute-start.11 = (bf16[10,4,256]{2,1,0:T(4,128)(2,1)S(1)}, bf16[10,4,256]{2,1,0:T(4,128)(2,1)S(1)}, u32[]{:S(2)}, u32[]{:S(2)}) collective-permute-start(bf16[10,4,256]{2,1,0:T(4,128)(2,1)S(1)} %get-tuple-element.137), channel_id=1, source_target_pairs={{8,0},{16,8},{24,16},{9,1},{17,9},{25,17},{10,2},{18,10},{26,18},{... | collective-permute-start | bytes 61448 | tf_op jit(solution)/shard_map/ppermute | solution.py:498
  91.6 49.4 %all-to-all-start = ((bf16[32,16,1664]{2,1,0:T(8,128)(2,1)}), bf16[32,16,1664]{2,1,0:T(8,128)(2,1)S(1)}, u32[]{:S(2)}, u32[]{:S(2)}) async-start(bf16[32,16,1664]{2,1,0:T(8,128)(2,1)} %bitcast.92), calls=%async_computation | async-start | bytes 3407872 | tf_op jit(solution)/shard_map/all_to_all | solution.py:910
  154.7 44.4 %all-to-all-start.1 = ((bf16[32,16,1664]{2,1,0:T(8,128)(2,1)}), bf16[32,16,1664]{2,1,0:T(8,128)(2,1)S(1)}, u32[]{:S(2)}, u32[]{:S(2)}) async-start(bf16[32,16,1664]{2,1,0:T(8,128)(2,1)} %get-tuple-element.97), calls=%async_computation.1 | async-start | bytes 3407872 | tf_op jit(solution)/shard_map/all_to_all | solution.py:919
  203.2 6.9 %collective-permute-start.14 = (f32[10,2,1280]{2,1,0:T(2,128)}, f32[10,2,1280]{2,1,0:T(2,128)S(1)}, u32[]{:S(2)}, u32[]{:S(2)}) collective-permute-start(f32[10,2,1280]{2,1,0:T(2,128)} %get-tuple-element.107), channel_id=1, source_target_pairs={{0,1},{1,2},{2,3},{3,4},{4,5},{5,6},{6,7},{8,9},{9,10},{10,11},{11... | collective-permute-start | bytes 307208 | tf_op jit(solution)/shard_map/ppermute | solution.py:503
  204.7 5.4 %collective-permute-start.15 = (f32[10,2,1280]{2,1,0:T(2,128)}, f32[10,2,1280]{2,1,0:T(2,128)S(1)}, u32[]{:S(2)}, u32[]{:S(2)}) collective-permute-start(f32[10,2,1280]{2,1,0:T(2,128)} %get-tuple-element.108), channel_id=1, source_target_pairs={{1,0},{2,1},{3,2},{4,3},{5,4},{6,5},{7,6},{9,8},{10,9},{11,10},{12... | collective-permute-start | bytes 307208 | tf_op jit(solution)/shard_map/ppermute | solution.py:504
  206.0 16.1 %collective-permute-start.12 = (bf16[10,2,32,256]{3,2,1,0:T(8,128)(2,1)}, bf16[10,2,32,256]{3,2,1,0:T(8,128)(2,1)S(1)}, u32[]{:S(2)}, u32[]{:S(2)}) collective-permute-start(bf16[10,2,32,256]{3,2,1,0:T(8,128)(2,1)} %get-tuple-element.105), channel_id=1, source_target_pairs={{0,8},{8,16},{16,24},{1,9},{9,17},{17,25},{2,10},{10,18},{18,26},{... | collective-permute-start | bytes 983048 | tf_op jit(solution)/shard_map/ppermute | solution.py:505
  208.7 13.4 %collective-permute-start.13 = (bf16[10,2,32,256]{3,2,1,0:T(8,128)(2,1)}, bf16[10,2,32,256]{3,2,1,0:T(8,128)(2,1)S(1)}, u32[]{:S(2)}, u32[]{:S(2)}) collective-permute-start(bf16[10,2,32,256]{3,2,1,0:T(8,128)(2,1)} %get-tuple-element.106), channel_id=1, source_target_pairs={{8,0},{16,8},{24,16},{9,1},{17,9},{25,17},{10,2},{18,10},{26,18},{... | collective-permute-start | bytes 983048 | tf_op jit(solution)/shard_map/ppermute | solution.py:506
  210.2 7.3 %collective-permute-start.16 = (f32[10,4,256]{2,1,0:T(4,128)S(1)}, f32[10,4,256]{2,1,0:T(4,128)S(1)}, u32[]{:S(2)}, u32[]{:S(2)}) collective-permute-start(f32[10,4,256]{2,1,0:T(4,128)S(1)} %get-tuple-element.136), channel_id=1, source_target_pairs={{0,8},{8,16},{16,24},{1,9},{9,17},{17,25},{2,10},{10,18},{18,26},{... | collective-permute-start | bytes 122888 | tf_op jit(solution)/shard_map/ppermute | solution.py:497
  214.7 7.3 %collective-permute-start.17 = (f32[10,4,256]{2,1,0:T(4,128)S(1)}, f32[10,4,256]{2,1,0:T(4,128)S(1)}, u32[]{:S(2)}, u32[]{:S(2)}) collective-permute-start(f32[10,4,256]{2,1,0:T(4,128)S(1)} %get-tuple-element.135), channel_id=1, source_target_pairs={{8,0},{16,8},{24,16},{9,1},{17,9},{25,17},{10,2},{18,10},{26,18},{... | collective-permute-start | bytes 122888 | tf_op jit(solution)/shard_map/ppermute | solution.py:498
  272.7 4.9 %collective-permute-start.21 = (f32[72,128]{1,0:T(8,128)S(1)}, f32[72,128]{1,0:T(8,128)S(1)}, u32[]{:S(2)}, u32[]{:S(2)}) collective-permute-start(f32[72,128]{1,0:T(8,128)S(1)} %add.38), channel_id=1, source_target_pairs={{0,6},{1,7},{2,4},{3,5},{4,2},{5,3},{6,0},{7,1},{8,14},{9,15},{10,... | collective-permute-start | bytes 110600 | tf_op jit(solution)/shard_map/ppermute | solution.py:481
  277.6 4.6 %collective-permute-start.22 = (f32[72,128]{1,0:T(8,128)S(1)}, f32[72,128]{1,0:T(8,128)S(1)}, u32[]{:S(2)}, u32[]{:S(2)}) collective-permute-start(f32[72,128]{1,0:T(8,128)S(1)} %add_add_fusion.refs_0_), channel_id=1, source_target_pairs={{0,8},{8,0},{16,24},{24,16},{1,9},{9,1},{17,25},{25,17},{2,10},{10... | collective-permute-start | bytes 110600 | tf_op jit(solution)/shard_map/ppermute | solution.py:461
  279.2 4.9 %collective-permute-start.23 = (f32[72,128]{1,0:T(8,128)S(1)}, f32[72,128]{1,0:T(8,128)S(1)}, u32[]{:S(2)}, u32[]{:S(2)}) collective-permute-start(f32[72,128]{1,0:T(8,128)S(1)} %add_add_fusion.refs_0_), channel_id=1, source_target_pairs={{0,16},{8,24},{16,0},{24,8},{1,17},{9,25},{17,1},{25,9},{2,18},{10... | collective-permute-start | bytes 110600 | tf_op jit(solution)/shard_map/ppermute | solution.py:461
  280.7 5.8 %collective-permute-start.24 = (f32[72,128]{1,0:T(8,128)S(1)}, f32[72,128]{1,0:T(8,128)S(1)}, u32[]{:S(2)}, u32[]{:S(2)}) collective-permute-start(f32[72,128]{1,0:T(8,128)S(1)} %add_add_fusion.refs_0_), channel_id=1, source_target_pairs={{0,24},{8,16},{16,8},{24,0},{1,25},{9,17},{17,9},{25,1},{2,26},{10... | collective-permute-start | bytes 110600 | tf_op jit(solution)/shard_map/ppermute | solution.py:461
  (21 other events, 221.9 us)

commit v2 on v1

--- a/solution.py
+++ b/solution.py
@@ -159,7 +159,7 @@
 def forward_kernel(
     own, *refs,
 ):
-    edges, refs = refs[:EDGES], refs[EDGES:]
+    edges, refs = of_step(refs[:EDGES], pl.program_id(0)), refs[EDGES:]
     (
     w_in, w_out, bias_out,
     main, part_below, part_above, part_left, part_right,
@@ -230,10 +230,10 @@
     )
 
 
-def hidden_kernel(own, *refs):
+def hidden_kernel(start, own, *refs):
     edges, (w_in, *_, hidden, slopes, volume, windows) = refs[:EDGES], refs[EDGES:]
     _, _, frames, rows, columns = own.shape
-    load_volume(volume, own, *edges)
+    load_volume(volume, own, *of_step(edges, start + pl.program_id(0)))
     build_windows(volume, windows, columns, True)
 
     def step(block, carry):
@@ -273,9 +273,9 @@
 
     @pl.when(part == 0)
     def _():
-        load_volume(volume, own, *edges)
+        load_volume(volume, own, *of_step(edges, pl.program_id(0)))
         build_windows(volume, windows, columns, True)
-        load_volume(volume, grad, *grad_edges)
+        load_volume(volume, grad, *of_step(grad_edges, pl.program_id(0)))
         build_windows(volume, grad_windows, columns, False)
 
     blocks = hidden.shape[1]
@@ -330,6 +330,10 @@
         out[width:, :] = row
 
 
+def of_step(refs, step):
+    return [ref.at[pl.ds(step, 1)] for ref in refs]
+
+
 def whole(shape):
     return pl.BlockSpec(tuple(shape), lambda s: (0,) * len(shape))
 
@@ -370,7 +374,7 @@
         forward_kernel,
         grid=(slices,),
         in_specs=[a_slice(own.shape, first)]
-        + [a_slice(one.shape) for one in edges]
+        + [pl.BlockSpec(memory_space=pltpu.VMEM)] * EDGES
         + [whole(w_in.shape), whole(w_out.shape), pl.BlockSpec(memory_space=pltpu.SMEM)],
         out_specs=[a_slice(one.shape) for one in out_shape],
         out_shape=out_shape,
@@ -385,7 +389,7 @@
         compiler_params=pltpu.CompilerParams(vmem_limit_bytes=VMEM),
         cost_estimate=expected(6 * slices),
         name="conv_forward",
-    )(own, *edges, w_in, w_out, bias_out)
+    )(own, *map(in_vmem, edges), w_in, w_out, bias_out)
 
 
 def hidden_again(own, edges, group, w_in, kept=()):
@@ -394,10 +398,10 @@
     volume, windows = conv_scratch(frames, rows, columns)
     shape = (own.shape[0], rows // BLOCK, frames * columns, w_in.shape[1])
     return pl.pallas_call(
-        hidden_kernel,
+        functools.partial(hidden_kernel, first),
         grid=(slices,),
         in_specs=[a_slice(own.shape, first)]
-        + [a_slice(one.shape, first) for one in edges]
+        + [pl.BlockSpec(memory_space=pltpu.VMEM)] * EDGES
         + [whole(w_in.shape)]
         + [pl.BlockSpec(memory_space=pl.ANY)] * len(kept),
         out_specs=[a_slice(shape, first)] * 2,
@@ -407,7 +411,7 @@
         compiler_params=pltpu.CompilerParams(vmem_limit_bytes=VMEM),
         cost_estimate=expected(5 * slices),
         name="hidden_again",
-    )(own, *edges, w_in, *kept)
+    )(own, *map(in_vmem, edges), w_in, *kept)
 
 
 def conv_backward(own, edges, grad, grad_edges, hidden, slopes, w_back, loss, sums):
@@ -417,7 +421,8 @@
     total = pltpu.VMEM((2 * 128, span), jnp.float32)
     fixed = (w_back, pick_table(), loss, sums)
     out_shape = jax.ShapeDtypeStruct((span // BLOCK + 8, PACKED), jnp.float32)
-    here = (own, *edges, grad, *grad_edges)
+    sides = [pl.BlockSpec(memory_space=pltpu.VMEM)] * EDGES
+    here = (own, *map(in_vmem, edges), grad, *map(in_vmem, grad_edges))
     blocks = rows // BLOCK
     parts = 1
 
@@ -435,7 +440,7 @@
     return pl.pallas_call(
         backward_kernel,
         grid=(slices, parts),
-        in_specs=[of_slice(one.shape) for one in here]
+        in_specs=[of_slice(own.shape), *sides, of_slice(grad.shape), *sides]
         + [part_of_slice(one.shape) for one in (hidden, slopes)]
         + [all_of(one.shape) for one in fixed],
         out_specs=all_of(out_shape.shape),
@@ -519,10 +524,10 @@
 
 
 def return_edges(part_below, part_above, part_left, part_right, columns):
+    from_above = lax.ppermute(part_below, "af", along("af", -1))
+    from_below = lax.ppermute(part_above, "af", along("af", 1))
     lower = lax.ppermute(part_left, "row", along("row", -1))
     upper = lax.ppermute(part_right, "row", along("row", 1))
-    from_above = lax.ppermute(part_below, "af", along("af", -1))
-    from_below = lax.ppermute(part_above, "af", along("af", 1))
     corner_below, corner_above = corners_along(upper, lower, columns)
     return from_below, from_above, upper, lower, corner_below, corner_above
 
@@ -641,44 +646,41 @@
     return jnp.concatenate(pieces, axis=1)
 
 
+def weighed(weights, arrays):
+    total = weights[0] * arrays[0]
+    for weight, array in zip(weights[1:], arrays[1:]):
+        total = total + weight * array
+    return total
+
+
 def kspace_slice(
-    k, index, frames_here, n_af, measured, target, sampled, share, scale, table,
-    spectrum, grads, loss_lanes,
+    k, frames_here, n_af, kspace, measured, target, sampled, share, scale, grads, loss_lanes
 ):
     frames = n_af * frames_here
-    twice = table.shape[0]
-    first = index * frames_here
-    size = frames * 8
-    here = spectrum[pl.ds(first, frames_here)].reshape(size, twice).astype(jnp.bfloat16)
-    kspace = jnp.dot(here, table[...], preferred_element_type=jnp.float32)
-
-    def place(t):
-        return (t % frames_here) * n_af + t // frames_here
-
-    filled = []
+    near = [range(max(t - 2, 0), min(t + 3, frames)) for t in range(frames)]
+
+    def rows_of(t):
+        start = (k * frames + (t % frames_here) * n_af + t // frames_here) * 8
+        return slice(start, start + 8)
+
+    factor = scale[...]
+    free = [1.0 - sampled[t] for t in range(frames)]
+    kept = [sampled[t] * measured[k, t] for t in range(frames)]
+    filled = [kept[t] + free[t] * kspace[rows_of(t)] for t in range(frames)]
+    slopes = []
+    terms = None
     for t in range(frames):
-        mask = sampled[t]
-        filled.append(mask * measured[k, t] + (1.0 - mask) * kspace[place(t) * 8 : place(t) * 8 + 8])
-    slopes = []
-    for t in range(frames):
-        mask = sampled[t]
-        near = range(max(t - 2, 0), min(t + 3, frames))
-        shared = sum(share[t, s] * filled[s] for s in near)
-        differ = mask * measured[k, t] + (1.0 - mask) * shared - target[k, t]
+        shared = weighed([share[t, s] for s in near[t]], [filled[s] for s in near[t]])
+        differ = kept[t] + free[t] * shared - target[k, t]
         square = differ * differ + 1.0
         inverse = lax.rsqrt(square)
-        loss_lanes[...] += (1.0 - mask) * (square * inverse - 1.0)
-        slopes.append((1.0 - mask) * differ * inverse * scale[...])
+        term = free[t] * (square * inverse - 1.0)
+        terms = term if terms is None else terms + term
+        slopes.append(free[t] * differ * inverse * factor)
+    loss_lanes[...] += terms
     for s in range(frames):
-        near = range(max(s - 2, 0), min(s + 3, frames))
-        grad = sum(share[t, s] * slopes[t] for t in near)
-        grads[k, place(s) * 8 : place(s) * 8 + 8, :] = (1.0 - sampled[s]) * grad
-    grad = grads[k]
-    high = grad.astype(jnp.bfloat16)
-    low = (grad - high.astype(jnp.float32)).astype(jnp.bfloat16)
-    back = lax.dot_general(high, table[...], NT, preferred_element_type=jnp.float32)
-    back += lax.dot_general(low, table[...], NT, preferred_element_type=jnp.float32)
-    spectrum[pl.ds(first, frames_here)] = back.reshape(frames_here, n_af, 8, twice)
+        grad = weighed([share[t, s] for t in near[s]], [slopes[t] for t in near[s]])
+        grads[rows_of(s), :] = free[s] * grad
 
 
 def kspace_kernel(
@@ -728,11 +730,17 @@
                         ]
 
     each = measured.shape[0]
+    here = pl.ds(step * each * frames_here, each * frames_here)
+    block = spectrum[here].reshape(grads.shape).astype(jnp.bfloat16)
+    kspace = jnp.dot(block, table[...], preferred_element_type=jnp.float32)
     for k in range(each):
         kspace_slice(
-            k, step * each + k, frames_here, n_af, measured, target, sampled, share, scale, table,
-            spectrum, grads, loss_lanes,
+            k, frames_here, n_af, kspace, measured, target, sampled, share, scale, grads, loss_lanes
         )
+    back = lax.dot_general(
+        grads[...].astype(jnp.bfloat16), table[...], NT, preferred_element_type=jnp.float32
+    )
+    spectrum[here] = back.reshape(each * frames_here, n_af, 8, twice)
 
     @pl.when(step == pl.num_programs(0) - 1)
     def _():
@@ -793,7 +801,7 @@
         ],
         scratch_shapes=[
             pltpu.VMEM((slices * frames_here, n_af, lines, twice), jnp.float32),
-            pltpu.VMEM((each, frames * lines, twice), jnp.float32),
+            pltpu.VMEM((each * frames * lines, twice), jnp.float32),
             pltpu.VMEM((lines, twice), jnp.float32),
             pltpu.VMEM((lines, twice), jnp.float32),
         ],
@@ -894,7 +902,7 @@
 
 
 def middle_fast(
-    main, added, measured, target, sampled, share, table_y, table_x, between, after
+    main, added, note, measured, target, sampled, window_half, table_y, table_x, between, after
 ):
     devices = lax.axis_size("af") * lax.axis_size("row")
     slices, frames_here, rows, twice = main.shape
@@ -903,7 +911,7 @@
     order = np.arange(twice).reshape(2, devices, lines).transpose(1, 0, 2).reshape(-1)
     permuted = jnp.asarray(np.ascontiguousarray(table_y[:, order].T), jnp.bfloat16)
     mask = jnp.broadcast_to(sampled[:, :, None], sampled.shape + (readout,))
-    note = jnp.sum(1.0 - sampled).reshape(1, 1)
+    share = share_matrix(window_half, measured.shape[1])
     mask, share, *added = lax.optimization_barrier((mask, share, *added))
     lanes = (size // 128 + 1) * 128
     hybrid = image_to_hybrid(main, added, permuted, note, lanes)
@@ -925,7 +933,7 @@
 
 
 def train_step(
-    image_in, measured, target, sampled, share, table_y, table_x, w_in, w_out, w_back, bias_out
+    image_in, measured, target, sampled, window_half, table_y, table_x, w_in, w_out, w_back, bias_out
 ):
     slices, _, frames_here, rows, columns = image_in.shape
     frames, lines = measured.shape[1:3]
@@ -933,6 +941,7 @@
     groups = [(0, cut), (cut, slices - cut)]
     edges = image_edges(image_in, (0, slices))
     main, *part = conv_forward(image_in, edges, (0, slices), w_in, w_out, bias_out)
+    note = jnp.sum(1.0 - sampled).reshape(1, 1)
     added = return_edges(*part, columns)
 
     def again(group, after, kept=()):
@@ -943,12 +952,13 @@
     fits = fits and frames * lines <= 256
     if fits:
         loss, count, grad, grad_edge, sums, kept = middle_fast(
-            main, added, measured, target, sampled, share, table_y, table_x,
+            main, added, note, measured, target, sampled, window_half, table_y, table_x,
             functools.partial(again, groups[0]), functools.partial(again, groups[1]),
         )
     else:
         loss, count, grad, sums = middle_plain(
-            main, added, measured, target, sampled, share, table_y, table_x
+            main, added, measured, target, sampled, share_matrix(window_half, frames),
+            table_y, table_x,
         )
         flat = (slices, 2, frames_here * columns)
         grad_edge = (
@@ -983,14 +993,13 @@
     rows = rows_here * lax.axis_size("row")
     table_y = dft_table(columns)
     table_x = dft_table(rows)
-    share = share_matrix(window_half, frames)
     sampled = line_mask.astype(jnp.float32)
     w_in = conv_in_weights(in_kernel, biases[:width])
     w_out = conv_out_weights(out_kernel)
     w_back = conv_back_weights(out_kernel)
 
     count, total = train_step(
-        image_in, measured, target, sampled, share, table_y, table_x,
+        image_in, measured, target, sampled, window_half, table_y, table_x,
         w_in, w_out, w_back, biases,
     )
     return update(

time: 290 us -> 284 us (0.979)
  Pallas kernels: 180 us -> 176 us
  transfers between devices with their start and end apart: 27 -> 27, of which waited for: 10 -> 10; matrix products, arithmetic and copies ran while one was open for 2% -> 2% of each run, Pallas kernels for 24% -> 25%
where the time goes in v2:
time: 284 us; the launch traced here: 283 us
  Pallas kernels  176 us (62%)
  starting transfers between devices  64.1 us (23%)
  waiting for transfers between devices  31.2 us (11%)
  local copies, waits for them, and re-layouts  6.93 us (2%)
  other arithmetic  3.09 us (1%)
    pallas_call x2, Pallas kernels, hidden_again(): pl.pallas_call(functools.partial(hidden_kernel, first), grid=(slices,), i...  69.5 us
    pallas_call x1, Pallas kernels, conv_backward(): pl.pallas_call(backward_kernel, grid=(slices, parts), in_specs=[of_slice(...  44.1 us
    pallas_call x1, Pallas kernels, conv_forward(): pl.pallas_call(forward_kernel, grid=(slices,), in_specs=[a_slice(own.shap...  40.3 us
    ppermute x3, starting transfers between devices, corners_along(): below = lax.ppermute(both[:, :, lanes - columns:], 'af', along('af', 1))  13.6 us
    pallas_call x1, Pallas kernels, kspace_step(): pl.pallas_call(functools.partial(kspace_kernel, frames_here, factor), gri...  11.3 us
    ppermute x3, waiting for transfers between devices, corners_along(): above = lax.ppermute(both[:, :, :columns], 'af', along('af', -1))  11 us
    all_to_all x1, starting transfers between devices, middle_fast(): lax.all_to_all(hybrid.reshape(devices, 2 * lines, lanes), AXES, 0, 0, til...  9.07 us
    ppermute x2, starting transfers between devices, share_edges(): below = lax.ppermute(high, 'af', along('af', 1))  6.98 us
  transfers between devices with their start and end apart: 27, of which 10 were waited for; matrix products, arithmetic and copies ran while one was open for 2% of the time, Pallas kernels for 25%

profile of v2, /device:TPU:0, one launch (start us, length us, event | category | flops | bytes accessed | tf_op | source)
XLA Modules:
  0.0 282.7 jit_solution(3771057524903812471)
XLA Ops:
  2.3 2.4 collective-permute-start.2
  7.2 4.3 %collective-permute-start = (bf16[10,2,32,256]{3,2,1,0:T(8,128)(2,1)S(1)}, bf16[10,2,32,256]{3,2,1,0:T(8,128)(2,1)S(1)}, u32[]{:S(2)}, u32[]{:S(2)}) collective-permute-start(bf16[10,2,32,256]{3,2,1,0:T(8,128)(2,1)S(1)} %get-tuple-element.134), channel_id=1, source_target_pairs={{0,8},{8,16},{16,24},{1,9},{9,17},{17,25},{2,10},{10,18},{18,26},{... | collective-permute-start | bytes 983048 | tf_op jit(solution)/shard_map/ppermute | solution.py:510
  13.6 4.5 %collective-permute-start.4 = (bf16[10,4,256]{2,1,0:T(4,128)(2,1)S(1)}, bf16[10,4,256]{2,1,0:T(4,128)(2,1)S(1)}, u32[]{:S(2)}, u32[]{:S(2)}) collective-permute-start(bf16[10,4,256]{2,1,0:T(4,128)(2,1)S(1)} %get-tuple-element.140), channel_id=1, source_target_pairs={{0,8},{8,16},{16,24},{1,9},{9,17},{17,25},{2,10},{10,18},{18,26},{... | collective-permute-start | bytes 61448 | tf_op jit(solution)/shard_map/ppermute | solution.py:502
  21.7 2.4 collective-permute-done.5.refs_5_
  24.2 40.3 %conv_forward.1 = (f32[10,5,32,512]{3,2,1,0:T(8,128)}, bf16[10,2,32,256]{3,2,1,0:T(8,128)(2,1)}, bf16[10,2,32,256]{3,2,1,0:T(8,128)(2,1)}, bf16[10,2,1792]{2,1,0:T(2,128)(2,1)}, bf16[10,2,1792]{2,1,0:T(2,128)(2,1)}) custom-call(bf16[10,2,5,32,256]{4,3,2,1,0:T(8,128)(2,1)} %own.7, bf16[10,2,32,256]{3,2,1,0:T(8,128)(2,1)S(1)} %collective-permute-done.refs_0_, ...), custom_call_target="tpu_custom_call" | custom-call | flops 69000003584 | tf_op jit(solution)/shard_map/conv_forward/pallas_call | solution.py:373
  64.4 2.0 collective-permute-start.8
  67.8 3.5 %collective-permute-start.6 = (bf16[10,2,32,256]{3,2,1,0:T(8,128)(2,1)}, bf16[10,2,32,256]{3,2,1,0:T(8,128)(2,1)S(1)}, u32[]{:S(2)}, u32[]{:S(2)}) collective-permute-start(bf16[10,2,32,256]{3,2,1,0:T(8,128)(2,1)} %get-tuple-element.81), channel_id=1, source_target_pairs={{0,8},{8,16},{16,24},{1,9},{9,17},{17,25},{2,10},{10,18},{18,26},{... | collective-permute-start | bytes 983048 | tf_op jit(solution)/shard_map/ppermute | solution.py:528
  73.3 4.5 %collective-permute-start.10 = (bf16[10,4,256]{2,1,0:T(4,128)(2,1)S(1)}, bf16[10,4,256]{2,1,0:T(4,128)(2,1)S(1)}, u32[]{:S(2)}, u32[]{:S(2)}) collective-permute-start(bf16[10,4,256]{2,1,0:T(4,128)(2,1)S(1)} %get-tuple-element.138), channel_id=1, source_target_pairs={{0,8},{8,16},{16,24},{1,9},{9,17},{17,25},{2,10},{10,18},{18,26},{... | collective-permute-start | bytes 61448 | tf_op jit(solution)/shard_map/ppermute | solution.py:502
  79.9 4.0 %collective-permute-done.11.corner_above = bf16[10,4,256]{2,1,0:T(4,128)(2,1)S(1)} collective-permute-done((bf16[10,4,256]{2,1,0:T(4,128)(2,1)S(1)}, bf16[10,4,256]{2,1,0:T(4,128)(2,1)S(1)}, u32[]{:S(2)}, u32[]{:S(2)}) %collective-permute-start.11) | collective-permute-done | bytes 20512 | tf_op jit(solution)/shard_map/ppermute | solution.py:503
  84.7 5.0 %image_to_hybrid.1 = bf16[512,1664]{1,0:T(8,128)(2,1)} custom-call(f32[10,5,32,512]{3,2,1,0:T(8,128)} %get-tuple-element.80.main, bf16[10,2,32,256]{3,2,1,0:T(8,128)(2,1)S(1)} %collective-permute-done.6.from_below, bf16[10,2,32,256]{3,2,1,0:T(8,128)(2,1)S(1)} %collective-permute-done.7.from_above, bf16[10,2,1792]{2,1,0:T(2,128)(2,1)S(1)} %collective-permute-done.8.upper, ...), custom_call_target="tpu_custom_call" | custom-call | flops 5750000128 | tf_op jit(solution)/shard_map/image_to_hybrid/pallas_call | solution.py:580
  89.7 9.1 %all-to-all-start = ((bf16[32,16,1664]{2,1,0:T(8,128)(2,1)}), bf16[32,16,1664]{2,1,0:T(8,128)(2,1)S(1)}, u32[]{:S(2)}, u32[]{:S(2)}) async-start(bf16[32,16,1664]{2,1,0:T(8,128)(2,1)} %bitcast.92), calls=%async_computation | async-start | bytes 3407872 | tf_op jit(solution)/shard_map/all_to_all | solution.py:918
  98.8 34.8 %hidden_again.2 = (bf16[10,8,1280,256]{3,2,1,0:T(8,128)(2,1)}, bf16[10,8,1280,256]{3,2,1,0:T(8,128)(2,1)}) custom-call(bf16[10,2,5,32,256]{4,3,2,1,0:T(8,128)(2,1)} %own.7, bf16[10,2,32,256]{3,2,1,0:T(8,128)(2,1)S(1)} %collective-permute-done.refs_0_, bf16[10,2,32,256]{3,2,1,0:T(8,128)(2,1)S(1)} %collective-permute-done.1.refs_1_, ...), custom_call_target="tpu_custom_call" | custom-call | flops 28750000128 | tf_op jit(solution)/shard_map/hidden_again/pallas_call | solution.py:400
  133.5 5.6 %all-to-all-done.received = bf16[32,16,1664]{2,1,0:T(8,128)(2,1)S(1)} async-done(((bf16[32,16,1664]{2,1,0:T(8,128)(2,1)}), bf16[32,16,1664]{2,1,0:T(8,128)(2,1)S(1)}, u32[]{:S(2)}, u32[]{:S(2)}) %all-to-all-start) | async-done | bytes 1703968 | tf_op jit(solution)/shard_map/all_to_all | solution.py:918
  139.1 11.3 %kspace.1 = (bf16[32,16,1664]{2,1,0:T(8,128)(2,1)}, f32[8,512]{1,0:T(8,128)}, f32[8,128]{1,0:T(8,128)}) custom-call(bf16[32,16,1664]{2,1,0:T(8,128)(2,1)S(1)} %all-to-all-done.received, f32[10,20,8,512]{3,2,1,0:T(8,128)} %measured.1, f32[10,20,8,512]{3,2,1,0:T(8,128)} %target.1, f32[20,8,512]{2,1,0:T(8,128)} %broadcast_in_dim.2.sampled, ...), custom_call_target="tpu_custom_call" | custom-call | flops 34500001792 | tf_op jit(solution)/shard_map/kspace/pallas_call | solution.py:784
  150.4 4.1 %all-to-all-start.1 = ((bf16[32,16,1664]{2,1,0:T(8,128)(2,1)}), bf16[32,16,1664]{2,1,0:T(8,128)(2,1)S(1)}, u32[]{:S(2)}, u32[]{:S(2)}) async-start(bf16[32,16,1664]{2,1,0:T(8,128)(2,1)} %get-tuple-element.97), calls=%async_computation.1 | async-start | bytes 3407872 | tf_op jit(solution)/shard_map/all_to_all | solution.py:927
  154.5 34.8 %hidden_again.3 = (bf16[10,8,1280,256]{3,2,1,0:T(8,128)(2,1)}, bf16[10,8,1280,256]{3,2,1,0:T(8,128)(2,1)}) custom-call(bf16[10,2,5,32,256]{4,3,2,1,0:T(8,128)(2,1)} %own.7, bf16[10,2,32,256]{3,2,1,0:T(8,128)(2,1)S(1)} %collective-permute-done.refs_0_, ...), custom_call_target="tpu_custom_call", output_to_operand_aliasing={{0}: (8, {}), {1}: (9, {})} | custom-call | flops 28750000128 | tf_op jit(solution)/shard_map/hidden_again/pallas_call | solution.py:400
  189.3 5.5 %all-to-all-done.1 = bf16[32,16,1664]{2,1,0:T(8,128)(2,1)S(1)} async-done(((bf16[32,16,1664]{2,1,0:T(8,128)(2,1)}), bf16[32,16,1664]{2,1,0:T(8,128)(2,1)S(1)}, u32[]{:S(2)}, u32[]{:S(2)}) %all-to-all-start.1) | async-done | bytes 1703968 | tf_op jit(solution)/shard_map/all_to_all | solution.py:927
  194.8 4.1 %hybrid_to_grad.1 = (bf16[10,2,5,32,256]{4,3,2,1,0:T(8,128)(2,1)}, bf16[10,2,32,256]{3,2,1,0:T(8,128)(2,1)}, bf16[10,2,32,256]{3,2,1,0:T(8,128)(2,1)}, f32[10,2,...) custom-call(bf16[512,1664]{1,0:T(8,128)(2,1)S(1)} %bitcast.91, bf16[512,512]{1,0:T(8,128)(2,1)} %constant.55.clone.table), custom_call_target="tpu_custom_call" | custom-call | flops 5750000128 | tf_op jit(solution)/shard_map/hybrid_to_grad/pallas_call | solution.py:624
  201.7 2.7 collective-permute-start.12
  205.8 4.5 %collective-permute-start.16 = (f32[10,4,256]{2,1,0:T(4,128)S(1)}, f32[10,4,256]{2,1,0:T(4,128)S(1)}, u32[]{:S(2)}, u32[]{:S(2)}) collective-permute-start(f32[10,4,256]{2,1,0:T(4,128)S(1)} %get-tuple-element.136), channel_id=1, source_target_pairs={{0,8},{8,16},{16,24},{1,9},{9,17},{17,25},{2,10},{10,18},{18,26},{... | collective-permute-start | bytes 122888 | tf_op jit(solution)/shard_map/ppermute | solution.py:502
  213.1 4.6 %collective-permute-done.17.refs_12_ = f32[10,4,256]{2,1,0:T(4,128)S(1)} collective-permute-done((f32[10,4,256]{2,1,0:T(4,128)S(1)}, f32[10,4,256]{2,1,0:T(4,128)S(1)}, u32[]{:S(2)}, u32[]{:S(2)}) %collective-permute-start.17) | collective-permute-done | bytes 40992 | tf_op jit(solution)/shard_map/ppermute | solution.py:503
  217.8 44.1 %conv_backward.1 = f32[72,128]{1,0:T(8,128)} custom-call(bf16[10,2,5,32,256]{4,3,2,1,0:T(8,128)(2,1)} %own.7, bf16[10,2,32,256]{3,2,1,0:T(8,128)(2,1)S(1)} %collective-permute-done.refs_0_, bf16[10,2,32,256]{3,2,1,0:T(8,128)(2,1)S(1)} %collective-permute-done.1.refs_1_, bf16[10,2,1280]{2,1,0:T(2,128)(2,1)S(1)} %collective-permute-done.2.refs_2_, ...), custom_call_target="tpu_custom_call" | custom-call | flops 57500000256 | tf_op jit(solution)/shard_map/conv_backward/pallas_call | solution.py:440
  276.3 2.0 collective-permute-done.23.refs_2_
  278.3 2.4 collective-permute-done.24.refs_3_
  (93 shorter events, 39.0 us)
Async XLA Ops:
  2.3 11.2 %collective-permute-start.2 = (bf16[10,2,1280]{2,1,0:T(2,128)(2,1)S(1)}, bf16[10,2,1280]{2,1,0:T(2,128)(2,1)S(1)}, u32[]{:S(2)}, u32[]{:S(2)}) collective-permute-start(bf16[10,2,1280]{2,1,0:T(2,128)(2,1)S(1)} %reshape_squeeze.6), channel_id=1, source_target_pairs={{0,1},{1,2},{2,3},{3,4},{4,5},{5,6},{6,7},{8,9},{9,10},{10,11},{11... | collective-permute-start | bytes 153608 | tf_op jit(solution)/shard_map/ppermute | solution.py:508
  4.8 8.8 %collective-permute-start.3 = (bf16[10,2,1280]{2,1,0:T(2,128)(2,1)S(1)}, bf16[10,2,1280]{2,1,0:T(2,128)(2,1)S(1)}, u32[]{:S(2)}, u32[]{:S(2)}) collective-permute-start(bf16[10,2,1280]{2,1,0:T(2,128)(2,1)S(1)} %reshape_squeeze.7), channel_id=1, source_target_pairs={{1,0},{2,1},{3,2},{4,3},{5,4},{6,5},{7,6},{9,8},{10,9},{11,10},{12... | collective-permute-start | bytes 153608 | tf_op jit(solution)/shard_map/ppermute | solution.py:509
  7.2 17.0 %collective-permute-start = (bf16[10,2,32,256]{3,2,1,0:T(8,128)(2,1)S(1)}, bf16[10,2,32,256]{3,2,1,0:T(8,128)(2,1)S(1)}, u32[]{:S(2)}, u32[]{:S(2)}) collective-permute-start(bf16[10,2,32,256]{3,2,1,0:T(8,128)(2,1)S(1)} %get-tuple-element.134), channel_id=1, source_target_pairs={{0,8},{8,16},{16,24},{1,9},{9,17},{17,25},{2,10},{10,18},{18,26},{... | collective-permute-start | bytes 983048 | tf_op jit(solution)/shard_map/ppermute | solution.py:510
  11.5 12.6 %collective-permute-start.1 = (bf16[10,2,32,256]{3,2,1,0:T(8,128)(2,1)S(1)}, bf16[10,2,32,256]{3,2,1,0:T(8,128)(2,1)S(1)}, u32[]{:S(2)}, u32[]{:S(2)}) collective-permute-start(bf16[10,2,32,256]{3,2,1,0:T(8,128)(2,1)S(1)} %get-tuple-element.133), channel_id=1, source_target_pairs={{8,0},{16,8},{24,16},{9,1},{17,9},{25,17},{10,2},{18,10},{26,18},{... | collective-permute-start | bytes 983048 | tf_op jit(solution)/shard_map/ppermute | solution.py:511
  13.6 8.1 %collective-permute-start.4 = (bf16[10,4,256]{2,1,0:T(4,128)(2,1)S(1)}, bf16[10,4,256]{2,1,0:T(4,128)(2,1)S(1)}, u32[]{:S(2)}, u32[]{:S(2)}) collective-permute-start(bf16[10,4,256]{2,1,0:T(4,128)(2,1)S(1)} %get-tuple-element.140), channel_id=1, source_target_pairs={{0,8},{8,16},{16,24},{1,9},{9,17},{17,25},{2,10},{10,18},{18,26},{... | collective-permute-start | bytes 61448 | tf_op jit(solution)/shard_map/ppermute | solution.py:502
  18.2 6.0 %collective-permute-start.5 = (bf16[10,4,256]{2,1,0:T(4,128)(2,1)S(1)}, bf16[10,4,256]{2,1,0:T(4,128)(2,1)S(1)}, u32[]{:S(2)}, u32[]{:S(2)}) collective-permute-start(bf16[10,4,256]{2,1,0:T(4,128)(2,1)S(1)} %get-tuple-element.139), channel_id=1, source_target_pairs={{8,0},{16,8},{24,16},{9,1},{17,9},{25,17},{10,2},{18,10},{26,18},{... | collective-permute-start | bytes 61448 | tf_op jit(solution)/shard_map/ppermute | solution.py:503
  64.4 8.8 %collective-permute-start.8 = (bf16[10,2,1792]{2,1,0:T(2,128)(2,1)}, bf16[10,2,1792]{2,1,0:T(2,128)(2,1)S(1)}, u32[]{:S(2)}, u32[]{:S(2)}) collective-permute-start(bf16[10,2,1792]{2,1,0:T(2,128)(2,1)} %get-tuple-element.83), channel_id=1, source_target_pairs={{0,1},{1,2},{2,3},{3,4},{4,5},{5,6},{6,7},{8,9},{9,10},{10,11},{11... | collective-permute-start | bytes 215048 | tf_op jit(solution)/shard_map/ppermute | solution.py:530
  66.5 6.8 %collective-permute-start.9 = (bf16[10,2,1792]{2,1,0:T(2,128)(2,1)}, bf16[10,2,1792]{2,1,0:T(2,128)(2,1)S(1)}, u32[]{:S(2)}, u32[]{:S(2)}) collective-permute-start(bf16[10,2,1792]{2,1,0:T(2,128)(2,1)} %get-tuple-element.84), channel_id=1, source_target_pairs={{1,0},{2,1},{3,2},{4,3},{5,4},{6,5},{7,6},{9,8},{10,9},{11,10},{12... | collective-permute-start | bytes 215048 | tf_op jit(solution)/shard_map/ppermute | solution.py:529
  67.8 16.1 %collective-permute-start.6 = (bf16[10,2,32,256]{3,2,1,0:T(8,128)(2,1)}, bf16[10,2,32,256]{3,2,1,0:T(8,128)(2,1)S(1)}, u32[]{:S(2)}, u32[]{:S(2)}) collective-permute-start(bf16[10,2,32,256]{3,2,1,0:T(8,128)(2,1)} %get-tuple-element.81), channel_id=1, source_target_pairs={{0,8},{8,16},{16,24},{1,9},{9,17},{17,25},{2,10},{10,18},{18,26},{... | collective-permute-start | bytes 983048 | tf_op jit(solution)/shard_map/ppermute | solution.py:528
  71.3 12.6 %collective-permute-start.7 = (bf16[10,2,32,256]{3,2,1,0:T(8,128)(2,1)}, bf16[10,2,32,256]{3,2,1,0:T(8,128)(2,1)S(1)}, u32[]{:S(2)}, u32[]{:S(2)}) collective-permute-start(bf16[10,2,32,256]{3,2,1,0:T(8,128)(2,1)} %get-tuple-element.82), channel_id=1, source_target_pairs={{8,0},{16,8},{24,16},{9,1},{17,9},{25,17},{10,2},{18,10},{26,18},{... | collective-permute-start | bytes 983048 | tf_op jit(solution)/shard_map/ppermute | solution.py:527
  73.3 6.6 %collective-permute-start.10 = (bf16[10,4,256]{2,1,0:T(4,128)(2,1)S(1)}, bf16[10,4,256]{2,1,0:T(4,128)(2,1)S(1)}, u32[]{:S(2)}, u32[]{:S(2)}) collective-permute-start(bf16[10,4,256]{2,1,0:T(4,128)(2,1)S(1)} %get-tuple-element.138), channel_id=1, source_target_pairs={{0,8},{8,16},{16,24},{1,9},{9,17},{17,25},{2,10},{10,18},{18,26},{... | collective-permute-start | bytes 61448 | tf_op jit(solution)/shard_map/ppermute | solution.py:502
  77.8 6.0 %collective-permute-start.11 = (bf16[10,4,256]{2,1,0:T(4,128)(2,1)S(1)}, bf16[10,4,256]{2,1,0:T(4,128)(2,1)S(1)}, u32[]{:S(2)}, u32[]{:S(2)}) collective-permute-start(bf16[10,4,256]{2,1,0:T(4,128)(2,1)S(1)} %get-tuple-element.137), channel_id=1, source_target_pairs={{8,0},{16,8},{24,16},{9,1},{17,9},{25,17},{10,2},{18,10},{26,18},{... | collective-permute-start | bytes 61448 | tf_op jit(solution)/shard_map/ppermute | solution.py:503
  89.7 49.4 %all-to-all-start = ((bf16[32,16,1664]{2,1,0:T(8,128)(2,1)}), bf16[32,16,1664]{2,1,0:T(8,128)(2,1)S(1)}, u32[]{:S(2)}, u32[]{:S(2)}) async-start(bf16[32,16,1664]{2,1,0:T(8,128)(2,1)} %bitcast.92), calls=%async_computation | async-start | bytes 3407872 | tf_op jit(solution)/shard_map/all_to_all | solution.py:918
  150.4 44.4 %all-to-all-start.1 = ((bf16[32,16,1664]{2,1,0:T(8,128)(2,1)}), bf16[32,16,1664]{2,1,0:T(8,128)(2,1)S(1)}, u32[]{:S(2)}, u32[]{:S(2)}) async-start(bf16[32,16,1664]{2,1,0:T(8,128)(2,1)} %get-tuple-element.97), calls=%async_computation.1 | async-start | bytes 3407872 | tf_op jit(solution)/shard_map/all_to_all | solution.py:927
  198.9 6.9 %collective-permute-start.14 = (f32[10,2,1280]{2,1,0:T(2,128)}, f32[10,2,1280]{2,1,0:T(2,128)S(1)}, u32[]{:S(2)}, u32[]{:S(2)}) collective-permute-start(f32[10,2,1280]{2,1,0:T(2,128)} %get-tuple-element.107), channel_id=1, source_target_pairs={{0,1},{1,2},{2,3},{3,4},{4,5},{5,6},{6,7},{8,9},{9,10},{10,11},{11... | collective-permute-start | bytes 307208 | tf_op jit(solution)/shard_map/ppermute | solution.py:508
  200.4 5.4 %collective-permute-start.15 = (f32[10,2,1280]{2,1,0:T(2,128)}, f32[10,2,1280]{2,1,0:T(2,128)S(1)}, u32[]{:S(2)}, u32[]{:S(2)}) collective-permute-start(f32[10,2,1280]{2,1,0:T(2,128)} %get-tuple-element.108), channel_id=1, source_target_pairs={{1,0},{2,1},{3,2},{4,3},{5,4},{6,5},{7,6},{9,8},{10,9},{11,10},{12... | collective-permute-start | bytes 307208 | tf_op jit(solution)/shard_map/ppermute | solution.py:509
  201.7 16.0 %collective-permute-start.12 = (bf16[10,2,32,256]{3,2,1,0:T(8,128)(2,1)}, bf16[10,2,32,256]{3,2,1,0:T(8,128)(2,1)S(1)}, u32[]{:S(2)}, u32[]{:S(2)}) collective-permute-start(bf16[10,2,32,256]{3,2,1,0:T(8,128)(2,1)} %get-tuple-element.105), channel_id=1, source_target_pairs={{0,8},{8,16},{16,24},{1,9},{9,17},{17,25},{2,10},{10,18},{18,26},{... | collective-permute-start | bytes 983048 | tf_op jit(solution)/shard_map/ppermute | solution.py:510
  204.4 13.4 %collective-permute-start.13 = (bf16[10,2,32,256]{3,2,1,0:T(8,128)(2,1)}, bf16[10,2,32,256]{3,2,1,0:T(8,128)(2,1)S(1)}, u32[]{:S(2)}, u32[]{:S(2)}) collective-permute-start(bf16[10,2,32,256]{3,2,1,0:T(8,128)(2,1)} %get-tuple-element.106), channel_id=1, source_target_pairs={{8,0},{16,8},{24,16},{9,1},{17,9},{25,17},{10,2},{18,10},{26,18},{... | collective-permute-start | bytes 983048 | tf_op jit(solution)/shard_map/ppermute | solution.py:511
  205.8 7.3 %collective-permute-start.16 = (f32[10,4,256]{2,1,0:T(4,128)S(1)}, f32[10,4,256]{2,1,0:T(4,128)S(1)}, u32[]{:S(2)}, u32[]{:S(2)}) collective-permute-start(f32[10,4,256]{2,1,0:T(4,128)S(1)} %get-tuple-element.136), channel_id=1, source_target_pairs={{0,8},{8,16},{16,24},{1,9},{9,17},{17,25},{2,10},{10,18},{18,26},{... | collective-permute-start | bytes 122888 | tf_op jit(solution)/shard_map/ppermute | solution.py:502
  210.4 7.4 %collective-permute-start.17 = (f32[10,4,256]{2,1,0:T(4,128)S(1)}, f32[10,4,256]{2,1,0:T(4,128)S(1)}, u32[]{:S(2)}, u32[]{:S(2)}) collective-permute-start(f32[10,4,256]{2,1,0:T(4,128)S(1)} %get-tuple-element.135), channel_id=1, source_target_pairs={{8,0},{16,8},{24,16},{9,1},{17,9},{25,17},{10,2},{18,10},{26,18},{... | collective-permute-start | bytes 122888 | tf_op jit(solution)/shard_map/ppermute | solution.py:503
  266.9 4.9 %collective-permute-start.21 = (f32[72,128]{1,0:T(8,128)S(1)}, f32[72,128]{1,0:T(8,128)S(1)}, u32[]{:S(2)}, u32[]{:S(2)}) collective-permute-start(f32[72,128]{1,0:T(8,128)S(1)} %add.38), channel_id=1, source_target_pairs={{0,6},{1,7},{2,4},{3,5},{4,2},{5,3},{6,0},{7,1},{8,14},{9,15},{10,... | collective-permute-start | bytes 110600 | tf_op jit(solution)/shard_map/ppermute | solution.py:486
  271.7 4.6 %collective-permute-start.22 = (f32[72,128]{1,0:T(8,128)S(1)}, f32[72,128]{1,0:T(8,128)S(1)}, u32[]{:S(2)}, u32[]{:S(2)}) collective-permute-start(f32[72,128]{1,0:T(8,128)S(1)} %add_add_fusion.refs_0_), channel_id=1, source_target_pairs={{0,8},{8,0},{16,24},{24,16},{1,9},{9,1},{17,25},{25,17},{2,10},{10... | collective-permute-start | bytes 110600 | tf_op jit(solution)/shard_map/ppermute | solution.py:466
  273.4 4.9 %collective-permute-start.23 = (f32[72,128]{1,0:T(8,128)S(1)}, f32[72,128]{1,0:T(8,128)S(1)}, u32[]{:S(2)}, u32[]{:S(2)}) collective-permute-start(f32[72,128]{1,0:T(8,128)S(1)} %add_add_fusion.refs_0_), channel_id=1, source_target_pairs={{0,16},{8,24},{16,0},{24,8},{1,17},{9,25},{17,1},{25,9},{2,18},{10... | collective-permute-start | bytes 110600 | tf_op jit(solution)/shard_map/ppermute | solution.py:466
  274.9 5.8 %collective-permute-start.24 = (f32[72,128]{1,0:T(8,128)S(1)}, f32[72,128]{1,0:T(8,128)S(1)}, u32[]{:S(2)}, u32[]{:S(2)}) collective-permute-start(f32[72,128]{1,0:T(8,128)S(1)} %add_add_fusion.refs_0_), channel_id=1, source_target_pairs={{0,24},{8,16},{16,8},{24,0},{1,25},{9,17},{17,9},{25,1},{2,26},{10... | collective-permute-start | bytes 110600 | tf_op jit(solution)/shard_map/ppermute | solution.py:466
  (11 other events, 325.3 us)

commit v3 on v2

--- a/solution.py
+++ b/solution.py
@@ -156,22 +156,40 @@
                 windows[block, e * SIDE : (e + 1) * SIDE, here] = shifted
 
 
-def forward_kernel(
-    own, *refs,
+def forward_kernel(own, *refs):
+    each = own.shape[0]
+    edges, fixed, rest = refs[:EDGES], refs[EDGES : EDGES + 3], refs[EDGES + 3 :]
+    slices = []
+    for k in range(each):
+        sides = of_step(edges, pl.program_id(0) * each + k)
+        outs = of_step(rest[:5], k)
+        slices.append(forward_slice(own.at[pl.ds(k, 1)], sides, *fixed, *outs, *(one.at[k] for one in rest[5:])))
+    blocks = own.shape[3] // BLOCK
+    slices[0][0]()
+    for k, (_, step, finish) in enumerate(slices):
+        for block in range(blocks):
+            step(block)
+            if block == blocks // 2 and k + 1 < each:
+                slices[k + 1][0]()
+            if block == 0 and k:
+                slices[k - 1][2]()
+    slices[-1][2]()
+
+
+def forward_slice(
+    own, edges, w_in, w_out, bias_out, main, part_below, part_above, part_left, part_right,
+    volume, windows, total, hidden, mixed, spread,
 ):
-    edges, refs = of_step(refs[:EDGES], pl.program_id(0)), refs[EDGES:]
-    (
-    w_in, w_out, bias_out,
-    main, part_below, part_above, part_left, part_right,
-    volume, windows, total, hidden, mixed, spread,
-    ) = refs
     _, _, frames, rows, columns = own.shape
     blocks = windows.shape[0]
-    load_volume(volume, own, *edges)
-    build_windows(volume, windows, columns, True)
+
+    def prepare():
+        load_volume(volume, own, *edges)
+        build_windows(volume, windows, columns, True)
+
     column = lax.broadcasted_iota(jnp.int32, (SIDE, columns), 1)
 
-    def step(block, carry):
+    def step(block):
         for f in range(frames):
             here = slice(f * columns, (f + 1) * columns)
             patch = jnp.concatenate(
@@ -199,29 +217,31 @@
                     summed = jnp.where(column == (0 if e == 0 else columns - 1), 0.0, summed)
                 window = summed if window is None else window + summed
             spread[block, :, t * columns : (t + 1) * columns] = window
-        return carry
-
-    lax.fori_loop(0, blocks, step, 0, unroll=True)
-    total[...] = jnp.zeros_like(total)
-    for block in range(blocks):
+
+    def finish():
+        total[...] = jnp.zeros_like(total)
+        for block in range(blocks):
+            for o in range(2):
+                start = 7 + BLOCK * block
+                total[o, start : start + WIN, :] = (
+                    total[o, start : start + WIN, :] + spread[block, o * WIN : (o + 1) * WIN, :]
+                )
         for o in range(2):
-            start = 7 + BLOCK * block
-            total[o, start : start + WIN, :] = (
-                total[o, start : start + WIN, :] + spread[block, o * WIN : (o + 1) * WIN, :]
-            )
-    for o in range(2):
-        for t in range(frames + 2):
-            here = total[o, 8 : 8 + rows, t * columns : (t + 1) * columns]
-            if t == 0:
-                part_below[0, o] = here.astype(jnp.bfloat16)
-            elif t == frames + 1:
-                part_above[0, o] = here.astype(jnp.bfloat16)
-            else:
-                base = volume[o, 8 : 8 + rows, t * columns : (t + 1) * columns] + bias_out[bias_out.shape[0] - 2 + o]
-                main[0, t - 1, :, o * columns : (o + 1) * columns] = base + here
-    for at, out in ((7, part_left), (8 + rows, part_right)):
-        both = [total[o, at : at + 1, :] for o in range(2)]
-        out[0] = jnp.concatenate(both, axis=0).astype(jnp.bfloat16)
+            for t in range(frames + 2):
+                here = total[o, 8 : 8 + rows, t * columns : (t + 1) * columns]
+                if t == 0:
+                    part_below[0, o] = here.astype(jnp.bfloat16)
+                elif t == frames + 1:
+                    part_above[0, o] = here.astype(jnp.bfloat16)
+                else:
+                    base = volume[o, 8 : 8 + rows, t * columns : (t + 1) * columns]
+                    base = base + bias_out[bias_out.shape[0] - 2 + o]
+                    main[0, t - 1, :, o * columns : (o + 1) * columns] = base + here
+        for at, out in ((7, part_left), (8 + rows, part_right)):
+            both = [total[o, at : at + 1, :] for o in range(2)]
+            out[0] = jnp.concatenate(both, axis=0).astype(jnp.bfloat16)
+
+    return prepare, step, finish
 
 
 def patches(source, block, frames, columns):
@@ -357,9 +377,15 @@
     )
 
 
-def conv_forward(own, edges, group, w_in, w_out, bias_out):
+def conv_forward(own, edges, w_in, w_out, bias_out):
     _, _, frames, rows, columns = own.shape
-    first, slices = group
+    slices = own.shape[0]
+    each = 2 if slices % 2 == 0 else 1
+
+    def some(shape):
+        rest = (0,) * (len(shape) - 1)
+        return pl.BlockSpec((each,) + tuple(shape[1:]), lambda s: (s,) + rest)
+
     lanes = (frames + 2) * columns
     span = w_in.shape[0]
     volume, windows = conv_scratch(frames, rows, columns)
@@ -372,19 +398,22 @@
     ]
     return pl.pallas_call(
         forward_kernel,
-        grid=(slices,),
-        in_specs=[a_slice(own.shape, first)]
+        grid=(slices // each,),
+        in_specs=[some(own.shape)]
         + [pl.BlockSpec(memory_space=pltpu.VMEM)] * EDGES
         + [whole(w_in.shape), whole(w_out.shape), pl.BlockSpec(memory_space=pltpu.SMEM)],
-        out_specs=[a_slice(one.shape) for one in out_shape],
+        out_specs=[some(one.shape) for one in out_shape],
         out_shape=out_shape,
         scratch_shapes=[
-            volume,
-            windows,
-            volume,
-            pltpu.VMEM((span, frames * columns), jnp.bfloat16),
-            pltpu.VMEM((frames, DEPTH, columns), jnp.float32),
-            pltpu.VMEM((rows // BLOCK, SIDE, lanes), jnp.float32),
+            pltpu.VMEM((each,) + tuple(shape), kind)
+            for shape, kind in (
+                (volume.shape, jnp.float32),
+                (windows.shape, jnp.bfloat16),
+                (volume.shape, jnp.float32),
+                ((span, frames * columns), jnp.bfloat16),
+                ((frames, DEPTH, columns), jnp.float32),
+                ((rows // BLOCK, SIDE, lanes), jnp.float32),
+            )
         ],
         compiler_params=pltpu.CompilerParams(vmem_limit_bytes=VMEM),
         cost_estimate=expected(6 * slices),
@@ -940,7 +969,7 @@
     cut = (slices + 1) // 2
     groups = [(0, cut), (cut, slices - cut)]
     edges = image_edges(image_in, (0, slices))
-    main, *part = conv_forward(image_in, edges, (0, slices), w_in, w_out, bias_out)
+    main, *part = conv_forward(image_in, edges, w_in, w_out, bias_out)
     note = jnp.sum(1.0 - sampled).reshape(1, 1)
     added = return_edges(*part, columns)
 

time: 284 us -> 281 us (0.989)
  no operation moved by 1% of the time
where the time goes in v3:
time: 281 us; the launch traced here: 280 us
  Pallas kernels  174 us (62%)
  starting transfers between devices  63.6 us (23%)
  waiting for transfers between devices  31.4 us (11%)
  local copies, waits for them, and re-layouts  6.93 us (2%)
  other arithmetic  3.09 us (1%)
    pallas_call x2, Pallas kernels, hidden_again(): pl.pallas_call(functools.partial(hidden_kernel, first), grid=(slices,), i...  69.5 us
    pallas_call x1, Pallas kernels, conv_backward(): pl.pallas_call(backward_kernel, grid=(slices, parts), in_specs=[of_slice(...  44.3 us
    pallas_call x1, Pallas kernels, conv_forward(): pl.pallas_call(forward_kernel, grid=(slices // each,), in_specs=[some(own...  37.9 us
    ppermute x3, starting transfers between devices, corners_along(): below = lax.ppermute(both[:, :, lanes - columns:], 'af', along('af', 1))  13.6 us
    pallas_call x1, Pallas kernels, kspace_step(): pl.pallas_call(functools.partial(kspace_kernel, frames_here, factor), gri...  11.3 us
    ppermute x3, waiting for transfers between devices, corners_along(): above = lax.ppermute(both[:, :, :columns], 'af', along('af', -1))  11 us
    all_to_all x1, starting transfers between devices, middle_fast(): lax.all_to_all(hybrid.reshape(devices, 2 * lines, lanes), AXES, 0, 0, til...  9.08 us
    ppermute x2, starting transfers between devices, share_edges(): below = lax.ppermute(high, 'af', along('af', 1))  6.99 us
  transfers between devices with their start and end apart: 27, of which 10 were waited for; matrix products, arithmetic and copies ran while one was open for 2% of the time, Pallas kernels for 25%

profile of v3, /device:TPU:0, one launch (start us, length us, event | category | flops | bytes accessed | tf_op | source)
XLA Modules:
  0.0 280.2 jit_solution(2823314893313124436)
XLA Ops:
  2.3 2.4 collective-permute-start.2
  7.2 4.3 %collective-permute-start = (bf16[10,2,32,256]{3,2,1,0:T(8,128)(2,1)S(1)}, bf16[10,2,32,256]{3,2,1,0:T(8,128)(2,1)S(1)}, u32[]{:S(2)}, u32[]{:S(2)}) collective-permute-start(bf16[10,2,32,256]{3,2,1,0:T(8,128)(2,1)S(1)} %get-tuple-element.134), channel_id=1, source_target_pairs={{0,8},{8,16},{16,24},{1,9},{9,17},{17,25},{2,10},{10,18},{18,26},{... | collective-permute-start | bytes 983048 | tf_op jit(solution)/shard_map/ppermute | solution.py:539
  13.6 4.5 %collective-permute-start.4 = (bf16[10,4,256]{2,1,0:T(4,128)(2,1)S(1)}, bf16[10,4,256]{2,1,0:T(4,128)(2,1)S(1)}, u32[]{:S(2)}, u32[]{:S(2)}) collective-permute-start(bf16[10,4,256]{2,1,0:T(4,128)(2,1)S(1)} %get-tuple-element.140), channel_id=1, source_target_pairs={{0,8},{8,16},{16,24},{1,9},{9,17},{17,25},{2,10},{10,18},{18,26},{... | collective-permute-start | bytes 61448 | tf_op jit(solution)/shard_map/ppermute | solution.py:531
  21.7 2.4 collective-permute-done.5.refs_5_
  24.2 37.9 %conv_forward.1 = (f32[10,5,32,512]{3,2,1,0:T(8,128)}, bf16[10,2,32,256]{3,2,1,0:T(8,128)(2,1)}, bf16[10,2,32,256]{3,2,1,0:T(8,128)(2,1)}, bf16[10,2,1792]{2,1,0:T(2,128)(2,1)}, bf16[10,2,1792]{2,1,0:T(2,128)(2,1)}) custom-call(bf16[10,2,5,32,256]{4,3,2,1,0:T(8,128)(2,1)} %own.7, bf16[10,2,32,256]{3,2,1,0:T(8,128)(2,1)S(1)} %collective-permute-done.refs_0_, ...), custom_call_target="tpu_custom_call" | custom-call | flops 69000003584 | tf_op jit(solution)/shard_map/conv_forward/pallas_call | solution.py:399
  62.1 2.0 collective-permute-start.8
  65.4 3.5 %collective-permute-start.6 = (bf16[10,2,32,256]{3,2,1,0:T(8,128)(2,1)}, bf16[10,2,32,256]{3,2,1,0:T(8,128)(2,1)S(1)}, u32[]{:S(2)}, u32[]{:S(2)}) collective-permute-start(bf16[10,2,32,256]{3,2,1,0:T(8,128)(2,1)} %get-tuple-element.81), channel_id=1, source_target_pairs={{0,8},{8,16},{16,24},{1,9},{9,17},{17,25},{2,10},{10,18},{18,26},{... | collective-permute-start | bytes 983048 | tf_op jit(solution)/shard_map/ppermute | solution.py:557
  70.9 4.5 %collective-permute-start.10 = (bf16[10,4,256]{2,1,0:T(4,128)(2,1)S(1)}, bf16[10,4,256]{2,1,0:T(4,128)(2,1)S(1)}, u32[]{:S(2)}, u32[]{:S(2)}) collective-permute-start(bf16[10,4,256]{2,1,0:T(4,128)(2,1)S(1)} %get-tuple-element.138), channel_id=1, source_target_pairs={{0,8},{8,16},{16,24},{1,9},{9,17},{17,25},{2,10},{10,18},{18,26},{... | collective-permute-start | bytes 61448 | tf_op jit(solution)/shard_map/ppermute | solution.py:531
  77.5 4.0 %collective-permute-done.11.corner_above = bf16[10,4,256]{2,1,0:T(4,128)(2,1)S(1)} collective-permute-done((bf16[10,4,256]{2,1,0:T(4,128)(2,1)S(1)}, bf16[10,4,256]{2,1,0:T(4,128)(2,1)S(1)}, u32[]{:S(2)}, u32[]{:S(2)}) %collective-permute-start.11) | collective-permute-done | bytes 20512 | tf_op jit(solution)/shard_map/ppermute | solution.py:532
  82.3 5.0 %image_to_hybrid.1 = bf16[512,1664]{1,0:T(8,128)(2,1)} custom-call(f32[10,5,32,512]{3,2,1,0:T(8,128)} %get-tuple-element.80.main, bf16[10,2,32,256]{3,2,1,0:T(8,128)(2,1)S(1)} %collective-permute-done.6.from_below, bf16[10,2,32,256]{3,2,1,0:T(8,128)(2,1)S(1)} %collective-permute-done.7.from_above, bf16[10,2,1792]{2,1,0:T(2,128)(2,1)S(1)} %collective-permute-done.8.upper, ...), custom_call_target="tpu_custom_call" | custom-call | flops 5750000128 | tf_op jit(solution)/shard_map/image_to_hybrid/pallas_call | solution.py:609
  87.3 9.1 %all-to-all-start = ((bf16[32,16,1664]{2,1,0:T(8,128)(2,1)}), bf16[32,16,1664]{2,1,0:T(8,128)(2,1)S(1)}, u32[]{:S(2)}, u32[]{:S(2)}) async-start(bf16[32,16,1664]{2,1,0:T(8,128)(2,1)} %bitcast.92), calls=%async_computation | async-start | bytes 3407872 | tf_op jit(solution)/shard_map/all_to_all | solution.py:947
  96.4 34.8 %hidden_again.2 = (bf16[10,8,1280,256]{3,2,1,0:T(8,128)(2,1)}, bf16[10,8,1280,256]{3,2,1,0:T(8,128)(2,1)}) custom-call(bf16[10,2,5,32,256]{4,3,2,1,0:T(8,128)(2,1)} %own.7, bf16[10,2,32,256]{3,2,1,0:T(8,128)(2,1)S(1)} %collective-permute-done.refs_0_, bf16[10,2,32,256]{3,2,1,0:T(8,128)(2,1)S(1)} %collective-permute-done.1.refs_1_, ...), custom_call_target="tpu_custom_call" | custom-call | flops 28750000128 | tf_op jit(solution)/shard_map/hidden_again/pallas_call | solution.py:429
  131.2 5.6 %all-to-all-done.received = bf16[32,16,1664]{2,1,0:T(8,128)(2,1)S(1)} async-done(((bf16[32,16,1664]{2,1,0:T(8,128)(2,1)}), bf16[32,16,1664]{2,1,0:T(8,128)(2,1)S(1)}, u32[]{:S(2)}, u32[]{:S(2)}) %all-to-all-start) | async-done | bytes 1703968 | tf_op jit(solution)/shard_map/all_to_all | solution.py:947
  136.7 11.3 %kspace.1 = (bf16[32,16,1664]{2,1,0:T(8,128)(2,1)}, f32[8,512]{1,0:T(8,128)}, f32[8,128]{1,0:T(8,128)}) custom-call(bf16[32,16,1664]{2,1,0:T(8,128)(2,1)S(1)} %all-to-all-done.received, f32[10,20,8,512]{3,2,1,0:T(8,128)} %measured.1, f32[10,20,8,512]{3,2,1,0:T(8,128)} %target.1, f32[20,8,512]{2,1,0:T(8,128)} %broadcast_in_dim.2.sampled, ...), custom_call_target="tpu_custom_call" | custom-call | flops 34500001792 | tf_op jit(solution)/shard_map/kspace/pallas_call | solution.py:813
  148.0 4.1 %all-to-all-start.1 = ((bf16[32,16,1664]{2,1,0:T(8,128)(2,1)}), bf16[32,16,1664]{2,1,0:T(8,128)(2,1)S(1)}, u32[]{:S(2)}, u32[]{:S(2)}) async-start(bf16[32,16,1664]{2,1,0:T(8,128)(2,1)} %get-tuple-element.97), calls=%async_computation.1 | async-start | bytes 3407872 | tf_op jit(solution)/shard_map/all_to_all | solution.py:956
  152.2 34.8 %hidden_again.3 = (bf16[10,8,1280,256]{3,2,1,0:T(8,128)(2,1)}, bf16[10,8,1280,256]{3,2,1,0:T(8,128)(2,1)}) custom-call(bf16[10,2,5,32,256]{4,3,2,1,0:T(8,128)(2,1)} %own.7, bf16[10,2,32,256]{3,2,1,0:T(8,128)(2,1)S(1)} %collective-permute-done.refs_0_, ...), custom_call_target="tpu_custom_call", output_to_operand_aliasing={{0}: (8, {}), {1}: (9, {})} | custom-call | flops 28750000128 | tf_op jit(solution)/shard_map/hidden_again/pallas_call | solution.py:429
  186.9 5.5 %all-to-all-done.1 = bf16[32,16,1664]{2,1,0:T(8,128)(2,1)S(1)} async-done(((bf16[32,16,1664]{2,1,0:T(8,128)(2,1)}), bf16[32,16,1664]{2,1,0:T(8,128)(2,1)S(1)}, u32[]{:S(2)}, u32[]{:S(2)}) %all-to-all-start.1) | async-done | bytes 1703968 | tf_op jit(solution)/shard_map/all_to_all | solution.py:956
  192.4 4.1 %hybrid_to_grad.1 = (bf16[10,2,5,32,256]{4,3,2,1,0:T(8,128)(2,1)}, bf16[10,2,32,256]{3,2,1,0:T(8,128)(2,1)}, bf16[10,2,32,256]{3,2,1,0:T(8,128)(2,1)}, f32[10,2,...) custom-call(bf16[512,1664]{1,0:T(8,128)(2,1)S(1)} %bitcast.91, bf16[512,512]{1,0:T(8,128)(2,1)} %constant.55.clone.table), custom_call_target="tpu_custom_call" | custom-call | flops 5750000128 | tf_op jit(solution)/shard_map/hybrid_to_grad/pallas_call | solution.py:653
  199.4 2.7 collective-permute-start.12
  203.5 4.5 %collective-permute-start.16 = (f32[10,4,256]{2,1,0:T(4,128)S(1)}, f32[10,4,256]{2,1,0:T(4,128)S(1)}, u32[]{:S(2)}, u32[]{:S(2)}) collective-permute-start(f32[10,4,256]{2,1,0:T(4,128)S(1)} %get-tuple-element.136), channel_id=1, source_target_pairs={{0,8},{8,16},{16,24},{1,9},{9,17},{17,25},{2,10},{10,18},{18,26},{... | collective-permute-start | bytes 122888 | tf_op jit(solution)/shard_map/ppermute | solution.py:531
  210.8 4.6 %collective-permute-done.17.refs_12_ = f32[10,4,256]{2,1,0:T(4,128)S(1)} collective-permute-done((f32[10,4,256]{2,1,0:T(4,128)S(1)}, f32[10,4,256]{2,1,0:T(4,128)S(1)}, u32[]{:S(2)}, u32[]{:S(2)}) %collective-permute-start.17) | collective-permute-done | bytes 40992 | tf_op jit(solution)/shard_map/ppermute | solution.py:532
  215.4 44.3 %conv_backward.1 = f32[72,128]{1,0:T(8,128)} custom-call(bf16[10,2,5,32,256]{4,3,2,1,0:T(8,128)(2,1)} %own.7, bf16[10,2,32,256]{3,2,1,0:T(8,128)(2,1)S(1)} %collective-permute-done.refs_0_, bf16[10,2,32,256]{3,2,1,0:T(8,128)(2,1)S(1)} %collective-permute-done.1.refs_1_, bf16[10,2,1280]{2,1,0:T(2,128)(2,1)S(1)} %collective-permute-done.2.refs_2_, ...), custom_call_target="tpu_custom_call" | custom-call | flops 57500000256 | tf_op jit(solution)/shard_map/conv_backward/pallas_call | solution.py:469
  273.8 2.5 collective-permute-done.23.refs_2_
  276.3 1.9 collective-permute-done.24.refs_3_
  (93 shorter events, 38.7 us)
Async XLA Ops:
  2.3 11.2 %collective-permute-start.2 = (bf16[10,2,1280]{2,1,0:T(2,128)(2,1)S(1)}, bf16[10,2,1280]{2,1,0:T(2,128)(2,1)S(1)}, u32[]{:S(2)}, u32[]{:S(2)}) collective-permute-start(bf16[10,2,1280]{2,1,0:T(2,128)(2,1)S(1)} %reshape_squeeze.6), channel_id=1, source_target_pairs={{0,1},{1,2},{2,3},{3,4},{4,5},{5,6},{6,7},{8,9},{9,10},{10,11},{11... | collective-permute-start | bytes 153608 | tf_op jit(solution)/shard_map/ppermute | solution.py:537
  4.8 8.8 %collective-permute-start.3 = (bf16[10,2,1280]{2,1,0:T(2,128)(2,1)S(1)}, bf16[10,2,1280]{2,1,0:T(2,128)(2,1)S(1)}, u32[]{:S(2)}, u32[]{:S(2)}) collective-permute-start(bf16[10,2,1280]{2,1,0:T(2,128)(2,1)S(1)} %reshape_squeeze.7), channel_id=1, source_target_pairs={{1,0},{2,1},{3,2},{4,3},{5,4},{6,5},{7,6},{9,8},{10,9},{11,10},{12... | collective-permute-start | bytes 153608 | tf_op jit(solution)/shard_map/ppermute | solution.py:538
  7.2 17.0 %collective-permute-start = (bf16[10,2,32,256]{3,2,1,0:T(8,128)(2,1)S(1)}, bf16[10,2,32,256]{3,2,1,0:T(8,128)(2,1)S(1)}, u32[]{:S(2)}, u32[]{:S(2)}) collective-permute-start(bf16[10,2,32,256]{3,2,1,0:T(8,128)(2,1)S(1)} %get-tuple-element.134), channel_id=1, source_target_pairs={{0,8},{8,16},{16,24},{1,9},{9,17},{17,25},{2,10},{10,18},{18,26},{... | collective-permute-start | bytes 983048 | tf_op jit(solution)/shard_map/ppermute | solution.py:539
  11.5 12.6 %collective-permute-start.1 = (bf16[10,2,32,256]{3,2,1,0:T(8,128)(2,1)S(1)}, bf16[10,2,32,256]{3,2,1,0:T(8,128)(2,1)S(1)}, u32[]{:S(2)}, u32[]{:S(2)}) collective-permute-start(bf16[10,2,32,256]{3,2,1,0:T(8,128)(2,1)S(1)} %get-tuple-element.133), channel_id=1, source_target_pairs={{8,0},{16,8},{24,16},{9,1},{17,9},{25,17},{10,2},{18,10},{26,18},{... | collective-permute-start | bytes 983048 | tf_op jit(solution)/shard_map/ppermute | solution.py:540
  13.6 8.1 %collective-permute-start.4 = (bf16[10,4,256]{2,1,0:T(4,128)(2,1)S(1)}, bf16[10,4,256]{2,1,0:T(4,128)(2,1)S(1)}, u32[]{:S(2)}, u32[]{:S(2)}) collective-permute-start(bf16[10,4,256]{2,1,0:T(4,128)(2,1)S(1)} %get-tuple-element.140), channel_id=1, source_target_pairs={{0,8},{8,16},{16,24},{1,9},{9,17},{17,25},{2,10},{10,18},{18,26},{... | collective-permute-start | bytes 61448 | tf_op jit(solution)/shard_map/ppermute | solution.py:531
  18.2 6.0 %collective-permute-start.5 = (bf16[10,4,256]{2,1,0:T(4,128)(2,1)S(1)}, bf16[10,4,256]{2,1,0:T(4,128)(2,1)S(1)}, u32[]{:S(2)}, u32[]{:S(2)}) collective-permute-start(bf16[10,4,256]{2,1,0:T(4,128)(2,1)S(1)} %get-tuple-element.139), channel_id=1, source_target_pairs={{8,0},{16,8},{24,16},{9,1},{17,9},{25,17},{10,2},{18,10},{26,18},{... | collective-permute-start | bytes 61448 | tf_op jit(solution)/shard_map/ppermute | solution.py:532
  62.1 8.8 %collective-permute-start.8 = (bf16[10,2,1792]{2,1,0:T(2,128)(2,1)}, bf16[10,2,1792]{2,1,0:T(2,128)(2,1)S(1)}, u32[]{:S(2)}, u32[]{:S(2)}) collective-permute-start(bf16[10,2,1792]{2,1,0:T(2,128)(2,1)} %get-tuple-element.83), channel_id=1, source_target_pairs={{0,1},{1,2},{2,3},{3,4},{4,5},{5,6},{6,7},{8,9},{9,10},{10,11},{11... | collective-permute-start | bytes 215048 | tf_op jit(solution)/shard_map/ppermute | solution.py:559
  64.1 6.8 %collective-permute-start.9 = (bf16[10,2,1792]{2,1,0:T(2,128)(2,1)}, bf16[10,2,1792]{2,1,0:T(2,128)(2,1)S(1)}, u32[]{:S(2)}, u32[]{:S(2)}) collective-permute-start(bf16[10,2,1792]{2,1,0:T(2,128)(2,1)} %get-tuple-element.84), channel_id=1, source_target_pairs={{1,0},{2,1},{3,2},{4,3},{5,4},{6,5},{7,6},{9,8},{10,9},{11,10},{12... | collective-permute-start | bytes 215048 | tf_op jit(solution)/shard_map/ppermute | solution.py:558
  65.4 16.0 %collective-permute-start.6 = (bf16[10,2,32,256]{3,2,1,0:T(8,128)(2,1)}, bf16[10,2,32,256]{3,2,1,0:T(8,128)(2,1)S(1)}, u32[]{:S(2)}, u32[]{:S(2)}) collective-permute-start(bf16[10,2,32,256]{3,2,1,0:T(8,128)(2,1)} %get-tuple-element.81), channel_id=1, source_target_pairs={{0,8},{8,16},{16,24},{1,9},{9,17},{17,25},{2,10},{10,18},{18,26},{... | collective-permute-start | bytes 983048 | tf_op jit(solution)/shard_map/ppermute | solution.py:557
  68.9 12.6 %collective-permute-start.7 = (bf16[10,2,32,256]{3,2,1,0:T(8,128)(2,1)}, bf16[10,2,32,256]{3,2,1,0:T(8,128)(2,1)S(1)}, u32[]{:S(2)}, u32[]{:S(2)}) collective-permute-start(bf16[10,2,32,256]{3,2,1,0:T(8,128)(2,1)} %get-tuple-element.82), channel_id=1, source_target_pairs={{8,0},{16,8},{24,16},{9,1},{17,9},{25,17},{10,2},{18,10},{26,18},{... | collective-permute-start | bytes 983048 | tf_op jit(solution)/shard_map/ppermute | solution.py:556
  70.9 6.6 %collective-permute-start.10 = (bf16[10,4,256]{2,1,0:T(4,128)(2,1)S(1)}, bf16[10,4,256]{2,1,0:T(4,128)(2,1)S(1)}, u32[]{:S(2)}, u32[]{:S(2)}) collective-permute-start(bf16[10,4,256]{2,1,0:T(4,128)(2,1)S(1)} %get-tuple-element.138), channel_id=1, source_target_pairs={{0,8},{8,16},{16,24},{1,9},{9,17},{17,25},{2,10},{10,18},{18,26},{... | collective-permute-start | bytes 61448 | tf_op jit(solution)/shard_map/ppermute | solution.py:531
  75.5 6.0 %collective-permute-start.11 = (bf16[10,4,256]{2,1,0:T(4,128)(2,1)S(1)}, bf16[10,4,256]{2,1,0:T(4,128)(2,1)S(1)}, u32[]{:S(2)}, u32[]{:S(2)}) collective-permute-start(bf16[10,4,256]{2,1,0:T(4,128)(2,1)S(1)} %get-tuple-element.137), channel_id=1, source_target_pairs={{8,0},{16,8},{24,16},{9,1},{17,9},{25,17},{10,2},{18,10},{26,18},{... | collective-permute-start | bytes 61448 | tf_op jit(solution)/shard_map/ppermute | solution.py:532
  87.3 49.4 %all-to-all-start = ((bf16[32,16,1664]{2,1,0:T(8,128)(2,1)}), bf16[32,16,1664]{2,1,0:T(8,128)(2,1)S(1)}, u32[]{:S(2)}, u32[]{:S(2)}) async-start(bf16[32,16,1664]{2,1,0:T(8,128)(2,1)} %bitcast.92), calls=%async_computation | async-start | bytes 3407872 | tf_op jit(solution)/shard_map/all_to_all | solution.py:947
  148.0 44.4 %all-to-all-start.1 = ((bf16[32,16,1664]{2,1,0:T(8,128)(2,1)}), bf16[32,16,1664]{2,1,0:T(8,128)(2,1)S(1)}, u32[]{:S(2)}, u32[]{:S(2)}) async-start(bf16[32,16,1664]{2,1,0:T(8,128)(2,1)} %get-tuple-element.97), calls=%async_computation.1 | async-start | bytes 3407872 | tf_op jit(solution)/shard_map/all_to_all | solution.py:956
  196.5 6.9 %collective-permute-start.14 = (f32[10,2,1280]{2,1,0:T(2,128)}, f32[10,2,1280]{2,1,0:T(2,128)S(1)}, u32[]{:S(2)}, u32[]{:S(2)}) collective-permute-start(f32[10,2,1280]{2,1,0:T(2,128)} %get-tuple-element.107), channel_id=1, source_target_pairs={{0,1},{1,2},{2,3},{3,4},{4,5},{5,6},{6,7},{8,9},{9,10},{10,11},{11... | collective-permute-start | bytes 307208 | tf_op jit(solution)/shard_map/ppermute | solution.py:537
  198.1 5.4 %collective-permute-start.15 = (f32[10,2,1280]{2,1,0:T(2,128)}, f32[10,2,1280]{2,1,0:T(2,128)S(1)}, u32[]{:S(2)}, u32[]{:S(2)}) collective-permute-start(f32[10,2,1280]{2,1,0:T(2,128)} %get-tuple-element.108), channel_id=1, source_target_pairs={{1,0},{2,1},{3,2},{4,3},{5,4},{6,5},{7,6},{9,8},{10,9},{11,10},{12... | collective-permute-start | bytes 307208 | tf_op jit(solution)/shard_map/ppermute | solution.py:538
  199.4 16.0 %collective-permute-start.12 = (bf16[10,2,32,256]{3,2,1,0:T(8,128)(2,1)}, bf16[10,2,32,256]{3,2,1,0:T(8,128)(2,1)S(1)}, u32[]{:S(2)}, u32[]{:S(2)}) collective-permute-start(bf16[10,2,32,256]{3,2,1,0:T(8,128)(2,1)} %get-tuple-element.105), channel_id=1, source_target_pairs={{0,8},{8,16},{16,24},{1,9},{9,17},{17,25},{2,10},{10,18},{18,26},{... | collective-permute-start | bytes 983048 | tf_op jit(solution)/shard_map/ppermute | solution.py:539
  202.0 13.4 %collective-permute-start.13 = (bf16[10,2,32,256]{3,2,1,0:T(8,128)(2,1)}, bf16[10,2,32,256]{3,2,1,0:T(8,128)(2,1)S(1)}, u32[]{:S(2)}, u32[]{:S(2)}) collective-permute-start(bf16[10,2,32,256]{3,2,1,0:T(8,128)(2,1)} %get-tuple-element.106), channel_id=1, source_target_pairs={{8,0},{16,8},{24,16},{9,1},{17,9},{25,17},{10,2},{18,10},{26,18},{... | collective-permute-start | bytes 983048 | tf_op jit(solution)/shard_map/ppermute | solution.py:540
  203.5 7.3 %collective-permute-start.16 = (f32[10,4,256]{2,1,0:T(4,128)S(1)}, f32[10,4,256]{2,1,0:T(4,128)S(1)}, u32[]{:S(2)}, u32[]{:S(2)}) collective-permute-start(f32[10,4,256]{2,1,0:T(4,128)S(1)} %get-tuple-element.136), channel_id=1, source_target_pairs={{0,8},{8,16},{16,24},{1,9},{9,17},{17,25},{2,10},{10,18},{18,26},{... | collective-permute-start | bytes 122888 | tf_op jit(solution)/shard_map/ppermute | solution.py:531
  208.0 7.4 %collective-permute-start.17 = (f32[10,4,256]{2,1,0:T(4,128)S(1)}, f32[10,4,256]{2,1,0:T(4,128)S(1)}, u32[]{:S(2)}, u32[]{:S(2)}) collective-permute-start(f32[10,4,256]{2,1,0:T(4,128)S(1)} %get-tuple-element.135), channel_id=1, source_target_pairs={{8,0},{16,8},{24,16},{9,1},{17,9},{25,17},{10,2},{18,10},{26,18},{... | collective-permute-start | bytes 122888 | tf_op jit(solution)/shard_map/ppermute | solution.py:532
  264.5 4.9 %collective-permute-start.21 = (f32[72,128]{1,0:T(8,128)S(1)}, f32[72,128]{1,0:T(8,128)S(1)}, u32[]{:S(2)}, u32[]{:S(2)}) collective-permute-start(f32[72,128]{1,0:T(8,128)S(1)} %add.38), channel_id=1, source_target_pairs={{0,6},{1,7},{2,4},{3,5},{4,2},{5,3},{6,0},{7,1},{8,14},{9,15},{10,... | collective-permute-start | bytes 110600 | tf_op jit(solution)/shard_map/ppermute | solution.py:515
  269.4 4.5 %collective-permute-start.22 = (f32[72,128]{1,0:T(8,128)S(1)}, f32[72,128]{1,0:T(8,128)S(1)}, u32[]{:S(2)}, u32[]{:S(2)}) collective-permute-start(f32[72,128]{1,0:T(8,128)S(1)} %add_add_fusion.refs_0_), channel_id=1, source_target_pairs={{0,8},{8,0},{16,24},{24,16},{1,9},{9,1},{17,25},{25,17},{2,10},{10... | collective-permute-start | bytes 110600 | tf_op jit(solution)/shard_map/ppermute | solution.py:495
  271.0 5.3 %collective-permute-start.23 = (f32[72,128]{1,0:T(8,128)S(1)}, f32[72,128]{1,0:T(8,128)S(1)}, u32[]{:S(2)}, u32[]{:S(2)}) collective-permute-start(f32[72,128]{1,0:T(8,128)S(1)} %add_add_fusion.refs_0_), channel_id=1, source_target_pairs={{0,16},{8,24},{16,0},{24,8},{1,17},{9,25},{17,1},{25,9},{2,18},{10... | collective-permute-start | bytes 110600 | tf_op jit(solution)/shard_map/ppermute | solution.py:495
  272.4 5.8 %collective-permute-start.24 = (f32[72,128]{1,0:T(8,128)S(1)}, f32[72,128]{1,0:T(8,128)S(1)}, u32[]{:S(2)}, u32[]{:S(2)}) collective-permute-start(f32[72,128]{1,0:T(8,128)S(1)} %add_add_fusion.refs_0_), channel_id=1, source_target_pairs={{0,24},{8,16},{16,8},{24,0},{1,25},{9,17},{17,9},{25,1},{2,26},{10... | collective-permute-start | bytes 110600 | tf_op jit(solution)/shard_map/ppermute | solution.py:495
  (11 other events, 318.1 us)

commit v4 on v3

--- a/solution.py
+++ b/solution.py
@@ -567,7 +567,7 @@
 ):
     slices, frames, rows, twice = main.shape
     columns = twice // 2
-    row = lax.broadcasted_iota(jnp.int32, (rows, columns), 0)
+    row = lax.broadcasted_iota(jnp.int32, (8, columns), 0)
     for s in range(slices):
         tops = upper[s].astype(jnp.float32)
         ends = lower[s].astype(jnp.float32)
@@ -588,8 +588,12 @@
                 if f in corners:
                     top = top + corners[f][o : o + 1]
                     end = end + corners[f][2 + o : 3 + o]
-                value = value + jnp.where(row == 0, top, 0.0)
-                value = value + jnp.where(row == rows - 1, end, 0.0)
+                parts = (
+                    value[0:8] + jnp.where(row == 0, top, 0.0),
+                    value[8 : rows - 8],
+                    value[rows - 8 :] + jnp.where(row == 7, end, 0.0),
+                )
+                value = jnp.concatenate(parts, axis=0)
                 start = (s * frames + f) * rows
                 image[start : start + rows, here] = value.astype(jnp.bfloat16)
     size = slices * frames * rows
@@ -620,7 +624,7 @@
 
 def grad_image_kernel(hybrid, table, out, low, high, first, last, sums):
     slices, _, frames, rows, columns = out.shape
-    sums[...] = jnp.zeros_like(sums)
+    partial = [jnp.zeros((8, columns), jnp.float32)] * 2
     for s in range(slices):
         size = frames * rows
         start = s * size // 128 * 128
@@ -639,11 +643,14 @@
                 if f == frames - 1:
                     high[s, c] = piece
                 wide = piece.astype(jnp.float32)
-                sums[c : c + 1, :] += jnp.sum(wide, axis=0, keepdims=True)
+                for at in range(0, rows, 8):
+                    partial[c] = partial[c] + wide[at : at + 8]
                 tops.append(wide[0:1])
                 ends.append(wide[rows - 1 :])
             first[s, c : c + 1, :] = jnp.concatenate(tops, axis=1)
             last[s, c : c + 1, :] = jnp.concatenate(ends, axis=1)
+    for c in range(2):
+        sums[c : c + 1, :] = jnp.sum(partial[c], axis=0, keepdims=True)
 
 
 def hybrid_to_grad(hybrid, table, shape):
@@ -804,7 +811,7 @@
     _, frames, lines, twice = measured.shape
     slices = measured.shape[0]
     n_af = frames // frames_here
-    each = 2 if slices % 2 == 0 else 1
+    each = next(n for n in (5, 2, 1) if slices % n == 0)
     chunks = chunk_table()
 
     def some(shape):

time: 281 us -> 281 us (level)
  transfers between devices with their start and end apart: 27 -> 27, of which waited for: 10 -> 11; matrix products, arithmetic and copies ran while one was open for 2% -> 2% of each run, Pallas kernels for 25% -> 25%
where the time goes in v4:
time: 281 us; the launch traced here: 280 us
  Pallas kernels  174 us (62%)
  starting transfers between devices  63.6 us (23%)
  waiting for transfers between devices  31.3 us (11%)
  local copies, waits for them, and re-layouts  6.93 us (2%)
  other arithmetic  3.09 us (1%)
    pallas_call x2, Pallas kernels, hidden_again(): pl.pallas_call(functools.partial(hidden_kernel, first), grid=(slices,), i...  69.5 us
    pallas_call x1, Pallas kernels, conv_backward(): pl.pallas_call(backward_kernel, grid=(slices, parts), in_specs=[of_slice(...  44.3 us
    pallas_call x1, Pallas kernels, conv_forward(): pl.pallas_call(forward_kernel, grid=(slices // each,), in_specs=[some(own...  37.9 us
    ppermute x3, starting transfers between devices, corners_along(): below = lax.ppermute(both[:, :, lanes - columns:], 'af', along('af', 1))  13.6 us
    pallas_call x1, Pallas kernels, kspace_step(): pl.pallas_call(functools.partial(kspace_kernel, frames_here, factor), gri...  11 us
    ppermute x3, waiting for transfers between devices, corners_along(): above = lax.ppermute(both[:, :, :columns], 'af', along('af', -1))  11 us
    all_to_all x1, starting transfers between devices, middle_fast(): lax.all_to_all(hybrid.reshape(devices, 2 * lines, lanes), AXES, 0, 0, til...  9.08 us
    ppermute x2, starting transfers between devices, share_edges(): below = lax.ppermute(high, 'af', along('af', 1))  6.99 us
  transfers between devices with their start and end apart: 27, of which 11 were waited for; matrix products, arithmetic and copies ran while one was open for 2% of the time, Pallas kernels for 25%

profile of v4, /device:TPU:0, one launch (start us, length us, event | category | flops | bytes accessed | tf_op | source)
XLA Modules:
  0.0 279.8 jit_solution(11846552478439019364)
XLA Ops:
  2.3 2.4 collective-permute-start.2
  7.2 4.3 %collective-permute-start = (bf16[10,2,32,256]{3,2,1,0:T(8,128)(2,1)S(1)}, bf16[10,2,32,256]{3,2,1,0:T(8,128)(2,1)S(1)}, u32[]{:S(2)}, u32[]{:S(2)}) collective-permute-start(bf16[10,2,32,256]{3,2,1,0:T(8,128)(2,1)S(1)} %get-tuple-element.134), channel_id=1, source_target_pairs={{0,8},{8,16},{16,24},{1,9},{9,17},{17,25},{2,10},{10,18},{18,26},{... | collective-permute-start | bytes 983048 | tf_op jit(solution)/shard_map/ppermute | solution.py:539
  13.6 4.5 %collective-permute-start.4 = (bf16[10,4,256]{2,1,0:T(4,128)(2,1)S(1)}, bf16[10,4,256]{2,1,0:T(4,128)(2,1)S(1)}, u32[]{:S(2)}, u32[]{:S(2)}) collective-permute-start(bf16[10,4,256]{2,1,0:T(4,128)(2,1)S(1)} %get-tuple-element.140), channel_id=1, source_target_pairs={{0,8},{8,16},{16,24},{1,9},{9,17},{17,25},{2,10},{10,18},{18,26},{... | collective-permute-start | bytes 61448 | tf_op jit(solution)/shard_map/ppermute | solution.py:531
  21.7 2.4 collective-permute-done.5.refs_5_
  24.2 37.9 %conv_forward.1 = (f32[10,5,32,512]{3,2,1,0:T(8,128)}, bf16[10,2,32,256]{3,2,1,0:T(8,128)(2,1)}, bf16[10,2,32,256]{3,2,1,0:T(8,128)(2,1)}, bf16[10,2,1792]{2,1,0:T(2,128)(2,1)}, bf16[10,2,1792]{2,1,0:T(2,128)(2,1)}) custom-call(bf16[10,2,5,32,256]{4,3,2,1,0:T(8,128)(2,1)} %own.7, bf16[10,2,32,256]{3,2,1,0:T(8,128)(2,1)S(1)} %collective-permute-done.refs_0_, ...), custom_call_target="tpu_custom_call" | custom-call | flops 69000003584 | tf_op jit(solution)/shard_map/conv_forward/pallas_call | solution.py:399
  62.1 2.0 collective-permute-start.8
  65.4 3.5 %collective-permute-start.6 = (bf16[10,2,32,256]{3,2,1,0:T(8,128)(2,1)}, bf16[10,2,32,256]{3,2,1,0:T(8,128)(2,1)S(1)}, u32[]{:S(2)}, u32[]{:S(2)}) collective-permute-start(bf16[10,2,32,256]{3,2,1,0:T(8,128)(2,1)} %get-tuple-element.81), channel_id=1, source_target_pairs={{0,8},{8,16},{16,24},{1,9},{9,17},{17,25},{2,10},{10,18},{18,26},{... | collective-permute-start | bytes 983048 | tf_op jit(solution)/shard_map/ppermute | solution.py:557
  70.9 4.5 %collective-permute-start.10 = (bf16[10,4,256]{2,1,0:T(4,128)(2,1)S(1)}, bf16[10,4,256]{2,1,0:T(4,128)(2,1)S(1)}, u32[]{:S(2)}, u32[]{:S(2)}) collective-permute-start(bf16[10,4,256]{2,1,0:T(4,128)(2,1)S(1)} %get-tuple-element.138), channel_id=1, source_target_pairs={{0,8},{8,16},{16,24},{1,9},{9,17},{17,25},{2,10},{10,18},{18,26},{... | collective-permute-start | bytes 61448 | tf_op jit(solution)/shard_map/ppermute | solution.py:531
  77.5 4.0 %collective-permute-done.11.corner_above = bf16[10,4,256]{2,1,0:T(4,128)(2,1)S(1)} collective-permute-done((bf16[10,4,256]{2,1,0:T(4,128)(2,1)S(1)}, bf16[10,4,256]{2,1,0:T(4,128)(2,1)S(1)}, u32[]{:S(2)}, u32[]{:S(2)}) %collective-permute-start.11) | collective-permute-done | bytes 20512 | tf_op jit(solution)/shard_map/ppermute | solution.py:532
  82.3 5.0 %image_to_hybrid.1 = bf16[512,1664]{1,0:T(8,128)(2,1)} custom-call(f32[10,5,32,512]{3,2,1,0:T(8,128)} %get-tuple-element.80.main, bf16[10,2,32,256]{3,2,1,0:T(8,128)(2,1)S(1)} %collective-permute-done.6.from_below, bf16[10,2,32,256]{3,2,1,0:T(8,128)(2,1)S(1)} %collective-permute-done.7.from_above, bf16[10,2,1792]{2,1,0:T(2,128)(2,1)S(1)} %collective-permute-done.8.upper, ...), custom_call_target="tpu_custom_call" | custom-call | flops 5750000128 | tf_op jit(solution)/shard_map/image_to_hybrid/pallas_call | solution.py:613
  87.3 9.1 %all-to-all-start = ((bf16[32,16,1664]{2,1,0:T(8,128)(2,1)}), bf16[32,16,1664]{2,1,0:T(8,128)(2,1)S(1)}, u32[]{:S(2)}, u32[]{:S(2)}) async-start(bf16[32,16,1664]{2,1,0:T(8,128)(2,1)} %bitcast.92), calls=%async_computation | async-start | bytes 3407872 | tf_op jit(solution)/shard_map/all_to_all | solution.py:954
  96.4 34.8 %hidden_again.2 = (bf16[10,8,1280,256]{3,2,1,0:T(8,128)(2,1)}, bf16[10,8,1280,256]{3,2,1,0:T(8,128)(2,1)}) custom-call(bf16[10,2,5,32,256]{4,3,2,1,0:T(8,128)(2,1)} %own.7, bf16[10,2,32,256]{3,2,1,0:T(8,128)(2,1)S(1)} %collective-permute-done.refs_0_, bf16[10,2,32,256]{3,2,1,0:T(8,128)(2,1)S(1)} %collective-permute-done.1.refs_1_, ...), custom_call_target="tpu_custom_call" | custom-call | flops 28750000128 | tf_op jit(solution)/shard_map/hidden_again/pallas_call | solution.py:429
  131.2 5.6 %all-to-all-done.received = bf16[32,16,1664]{2,1,0:T(8,128)(2,1)S(1)} async-done(((bf16[32,16,1664]{2,1,0:T(8,128)(2,1)}), bf16[32,16,1664]{2,1,0:T(8,128)(2,1)S(1)}, u32[]{:S(2)}, u32[]{:S(2)}) %all-to-all-start) | async-done | bytes 1703968 | tf_op jit(solution)/shard_map/all_to_all | solution.py:954
  136.7 11.0 %kspace.1 = (bf16[32,16,1664]{2,1,0:T(8,128)(2,1)}, f32[8,512]{1,0:T(8,128)}, f32[8,128]{1,0:T(8,128)}) custom-call(bf16[32,16,1664]{2,1,0:T(8,128)(2,1)S(1)} %all-to-all-done.received, f32[10,20,8,512]{3,2,1,0:T(8,128)} %measured.1, f32[10,20,8,512]{3,2,1,0:T(8,128)} %target.1, f32[20,8,512]{2,1,0:T(8,128)} %broadcast_in_dim.2.sampled, ...), custom_call_target="tpu_custom_call" | custom-call | flops 34500001792 | tf_op jit(solution)/shard_map/kspace/pallas_call | solution.py:820
  147.8 4.1 %all-to-all-start.1 = ((bf16[32,16,1664]{2,1,0:T(8,128)(2,1)}), bf16[32,16,1664]{2,1,0:T(8,128)(2,1)S(1)}, u32[]{:S(2)}, u32[]{:S(2)}) async-start(bf16[32,16,1664]{2,1,0:T(8,128)(2,1)} %get-tuple-element.97), calls=%async_computation.1 | async-start | bytes 3407872 | tf_op jit(solution)/shard_map/all_to_all | solution.py:963
  151.9 34.8 %hidden_again.3 = (bf16[10,8,1280,256]{3,2,1,0:T(8,128)(2,1)}, bf16[10,8,1280,256]{3,2,1,0:T(8,128)(2,1)}) custom-call(bf16[10,2,5,32,256]{4,3,2,1,0:T(8,128)(2,1)} %own.7, bf16[10,2,32,256]{3,2,1,0:T(8,128)(2,1)S(1)} %collective-permute-done.refs_0_, ...), custom_call_target="tpu_custom_call", output_to_operand_aliasing={{0}: (8, {}), {1}: (9, {})} | custom-call | flops 28750000128 | tf_op jit(solution)/shard_map/hidden_again/pallas_call | solution.py:429
  186.6 5.5 %all-to-all-done.1 = bf16[32,16,1664]{2,1,0:T(8,128)(2,1)S(1)} async-done(((bf16[32,16,1664]{2,1,0:T(8,128)(2,1)}), bf16[32,16,1664]{2,1,0:T(8,128)(2,1)S(1)}, u32[]{:S(2)}, u32[]{:S(2)}) %all-to-all-start.1) | async-done | bytes 1703968 | tf_op jit(solution)/shard_map/all_to_all | solution.py:963
  192.2 4.1 %hybrid_to_grad.1 = (bf16[10,2,5,32,256]{4,3,2,1,0:T(8,128)(2,1)}, bf16[10,2,32,256]{3,2,1,0:T(8,128)(2,1)}, bf16[10,2,32,256]{3,2,1,0:T(8,128)(2,1)}, f32[10,2,...) custom-call(bf16[512,1664]{1,0:T(8,128)(2,1)S(1)} %bitcast.91, bf16[512,512]{1,0:T(8,128)(2,1)} %constant.55.clone.table), custom_call_target="tpu_custom_call" | custom-call | flops 5750000128 | tf_op jit(solution)/shard_map/hybrid_to_grad/pallas_call | solution.py:660
  199.1 2.7 collective-permute-start.12
  203.2 4.5 %collective-permute-start.16 = (f32[10,4,256]{2,1,0:T(4,128)S(1)}, f32[10,4,256]{2,1,0:T(4,128)S(1)}, u32[]{:S(2)}, u32[]{:S(2)}) collective-permute-start(f32[10,4,256]{2,1,0:T(4,128)S(1)} %get-tuple-element.136), channel_id=1, source_target_pairs={{0,8},{8,16},{16,24},{1,9},{9,17},{17,25},{2,10},{10,18},{18,26},{... | collective-permute-start | bytes 122888 | tf_op jit(solution)/shard_map/ppermute | solution.py:531
  210.5 4.6 %collective-permute-done.17.refs_12_ = f32[10,4,256]{2,1,0:T(4,128)S(1)} collective-permute-done((f32[10,4,256]{2,1,0:T(4,128)S(1)}, f32[10,4,256]{2,1,0:T(4,128)S(1)}, u32[]{:S(2)}, u32[]{:S(2)}) %collective-permute-start.17) | collective-permute-done | bytes 40992 | tf_op jit(solution)/shard_map/ppermute | solution.py:532
  215.1 44.3 %conv_backward.1 = f32[72,128]{1,0:T(8,128)} custom-call(bf16[10,2,5,32,256]{4,3,2,1,0:T(8,128)(2,1)} %own.7, bf16[10,2,32,256]{3,2,1,0:T(8,128)(2,1)S(1)} %collective-permute-done.refs_0_, bf16[10,2,32,256]{3,2,1,0:T(8,128)(2,1)S(1)} %collective-permute-done.1.refs_1_, bf16[10,2,1280]{2,1,0:T(2,128)(2,1)S(1)} %collective-permute-done.2.refs_2_, ...), custom_call_target="tpu_custom_call" | custom-call | flops 57500000256 | tf_op jit(solution)/shard_map/conv_backward/pallas_call | solution.py:469
  273.5 2.0 collective-permute-done.23.refs_2_
  275.5 2.3 collective-permute-done.24.refs_3_
  (93 shorter events, 38.6 us)
Async XLA Ops:
  2.3 11.2 %collective-permute-start.2 = (bf16[10,2,1280]{2,1,0:T(2,128)(2,1)S(1)}, bf16[10,2,1280]{2,1,0:T(2,128)(2,1)S(1)}, u32[]{:S(2)}, u32[]{:S(2)}) collective-permute-start(bf16[10,2,1280]{2,1,0:T(2,128)(2,1)S(1)} %reshape_squeeze.6), channel_id=1, source_target_pairs={{0,1},{1,2},{2,3},{3,4},{4,5},{5,6},{6,7},{8,9},{9,10},{10,11},{11... | collective-permute-start | bytes 153608 | tf_op jit(solution)/shard_map/ppermute | solution.py:537
  4.8 8.8 %collective-permute-start.3 = (bf16[10,2,1280]{2,1,0:T(2,128)(2,1)S(1)}, bf16[10,2,1280]{2,1,0:T(2,128)(2,1)S(1)}, u32[]{:S(2)}, u32[]{:S(2)}) collective-permute-start(bf16[10,2,1280]{2,1,0:T(2,128)(2,1)S(1)} %reshape_squeeze.7), channel_id=1, source_target_pairs={{1,0},{2,1},{3,2},{4,3},{5,4},{6,5},{7,6},{9,8},{10,9},{11,10},{12... | collective-permute-start | bytes 153608 | tf_op jit(solution)/shard_map/ppermute | solution.py:538
  7.2 17.0 %collective-permute-start = (bf16[10,2,32,256]{3,2,1,0:T(8,128)(2,1)S(1)}, bf16[10,2,32,256]{3,2,1,0:T(8,128)(2,1)S(1)}, u32[]{:S(2)}, u32[]{:S(2)}) collective-permute-start(bf16[10,2,32,256]{3,2,1,0:T(8,128)(2,1)S(1)} %get-tuple-element.134), channel_id=1, source_target_pairs={{0,8},{8,16},{16,24},{1,9},{9,17},{17,25},{2,10},{10,18},{18,26},{... | collective-permute-start | bytes 983048 | tf_op jit(solution)/shard_map/ppermute | solution.py:539
  11.5 12.6 %collective-permute-start.1 = (bf16[10,2,32,256]{3,2,1,0:T(8,128)(2,1)S(1)}, bf16[10,2,32,256]{3,2,1,0:T(8,128)(2,1)S(1)}, u32[]{:S(2)}, u32[]{:S(2)}) collective-permute-start(bf16[10,2,32,256]{3,2,1,0:T(8,128)(2,1)S(1)} %get-tuple-element.133), channel_id=1, source_target_pairs={{8,0},{16,8},{24,16},{9,1},{17,9},{25,17},{10,2},{18,10},{26,18},{... | collective-permute-start | bytes 983048 | tf_op jit(solution)/shard_map/ppermute | solution.py:540
  13.6 8.1 %collective-permute-start.4 = (bf16[10,4,256]{2,1,0:T(4,128)(2,1)S(1)}, bf16[10,4,256]{2,1,0:T(4,128)(2,1)S(1)}, u32[]{:S(2)}, u32[]{:S(2)}) collective-permute-start(bf16[10,4,256]{2,1,0:T(4,128)(2,1)S(1)} %get-tuple-element.140), channel_id=1, source_target_pairs={{0,8},{8,16},{16,24},{1,9},{9,17},{17,25},{2,10},{10,18},{18,26},{... | collective-permute-start | bytes 61448 | tf_op jit(solution)/shard_map/ppermute | solution.py:531
  18.2 6.0 %collective-permute-start.5 = (bf16[10,4,256]{2,1,0:T(4,128)(2,1)S(1)}, bf16[10,4,256]{2,1,0:T(4,128)(2,1)S(1)}, u32[]{:S(2)}, u32[]{:S(2)}) collective-permute-start(bf16[10,4,256]{2,1,0:T(4,128)(2,1)S(1)} %get-tuple-element.139), channel_id=1, source_target_pairs={{8,0},{16,8},{24,16},{9,1},{17,9},{25,17},{10,2},{18,10},{26,18},{... | collective-permute-start | bytes 61448 | tf_op jit(solution)/shard_map/ppermute | solution.py:532
  62.1 8.8 %collective-permute-start.8 = (bf16[10,2,1792]{2,1,0:T(2,128)(2,1)}, bf16[10,2,1792]{2,1,0:T(2,128)(2,1)S(1)}, u32[]{:S(2)}, u32[]{:S(2)}) collective-permute-start(bf16[10,2,1792]{2,1,0:T(2,128)(2,1)} %get-tuple-element.83), channel_id=1, source_target_pairs={{0,1},{1,2},{2,3},{3,4},{4,5},{5,6},{6,7},{8,9},{9,10},{10,11},{11... | collective-permute-start | bytes 215048 | tf_op jit(solution)/shard_map/ppermute | solution.py:559
  64.1 6.8 %collective-permute-start.9 = (bf16[10,2,1792]{2,1,0:T(2,128)(2,1)}, bf16[10,2,1792]{2,1,0:T(2,128)(2,1)S(1)}, u32[]{:S(2)}, u32[]{:S(2)}) collective-permute-start(bf16[10,2,1792]{2,1,0:T(2,128)(2,1)} %get-tuple-element.84), channel_id=1, source_target_pairs={{1,0},{2,1},{3,2},{4,3},{5,4},{6,5},{7,6},{9,8},{10,9},{11,10},{12... | collective-permute-start | bytes 215048 | tf_op jit(solution)/shard_map/ppermute | solution.py:558
  65.4 16.0 %collective-permute-start.6 = (bf16[10,2,32,256]{3,2,1,0:T(8,128)(2,1)}, bf16[10,2,32,256]{3,2,1,0:T(8,128)(2,1)S(1)}, u32[]{:S(2)}, u32[]{:S(2)}) collective-permute-start(bf16[10,2,32,256]{3,2,1,0:T(8,128)(2,1)} %get-tuple-element.81), channel_id=1, source_target_pairs={{0,8},{8,16},{16,24},{1,9},{9,17},{17,25},{2,10},{10,18},{18,26},{... | collective-permute-start | bytes 983048 | tf_op jit(solution)/shard_map/ppermute | solution.py:557
  68.9 12.6 %collective-permute-start.7 = (bf16[10,2,32,256]{3,2,1,0:T(8,128)(2,1)}, bf16[10,2,32,256]{3,2,1,0:T(8,128)(2,1)S(1)}, u32[]{:S(2)}, u32[]{:S(2)}) collective-permute-start(bf16[10,2,32,256]{3,2,1,0:T(8,128)(2,1)} %get-tuple-element.82), channel_id=1, source_target_pairs={{8,0},{16,8},{24,16},{9,1},{17,9},{25,17},{10,2},{18,10},{26,18},{... | collective-permute-start | bytes 983048 | tf_op jit(solution)/shard_map/ppermute | solution.py:556
  70.9 6.6 %collective-permute-start.10 = (bf16[10,4,256]{2,1,0:T(4,128)(2,1)S(1)}, bf16[10,4,256]{2,1,0:T(4,128)(2,1)S(1)}, u32[]{:S(2)}, u32[]{:S(2)}) collective-permute-start(bf16[10,4,256]{2,1,0:T(4,128)(2,1)S(1)} %get-tuple-element.138), channel_id=1, source_target_pairs={{0,8},{8,16},{16,24},{1,9},{9,17},{17,25},{2,10},{10,18},{18,26},{... | collective-permute-start | bytes 61448 | tf_op jit(solution)/shard_map/ppermute | solution.py:531
  75.5 6.0 %collective-permute-start.11 = (bf16[10,4,256]{2,1,0:T(4,128)(2,1)S(1)}, bf16[10,4,256]{2,1,0:T(4,128)(2,1)S(1)}, u32[]{:S(2)}, u32[]{:S(2)}) collective-permute-start(bf16[10,4,256]{2,1,0:T(4,128)(2,1)S(1)} %get-tuple-element.137), channel_id=1, source_target_pairs={{8,0},{16,8},{24,16},{9,1},{17,9},{25,17},{10,2},{18,10},{26,18},{... | collective-permute-start | bytes 61448 | tf_op jit(solution)/shard_map/ppermute | solution.py:532
  87.3 49.4 %all-to-all-start = ((bf16[32,16,1664]{2,1,0:T(8,128)(2,1)}), bf16[32,16,1664]{2,1,0:T(8,128)(2,1)S(1)}, u32[]{:S(2)}, u32[]{:S(2)}) async-start(bf16[32,16,1664]{2,1,0:T(8,128)(2,1)} %bitcast.92), calls=%async_computation | async-start | bytes 3407872 | tf_op jit(solution)/shard_map/all_to_all | solution.py:954
  147.8 44.4 %all-to-all-start.1 = ((bf16[32,16,1664]{2,1,0:T(8,128)(2,1)}), bf16[32,16,1664]{2,1,0:T(8,128)(2,1)S(1)}, u32[]{:S(2)}, u32[]{:S(2)}) async-start(bf16[32,16,1664]{2,1,0:T(8,128)(2,1)} %get-tuple-element.97), calls=%async_computation.1 | async-start | bytes 3407872 | tf_op jit(solution)/shard_map/all_to_all | solution.py:963
  196.2 6.9 %collective-permute-start.14 = (f32[10,2,1280]{2,1,0:T(2,128)}, f32[10,2,1280]{2,1,0:T(2,128)S(1)}, u32[]{:S(2)}, u32[]{:S(2)}) collective-permute-start(f32[10,2,1280]{2,1,0:T(2,128)} %get-tuple-element.107), channel_id=1, source_target_pairs={{0,1},{1,2},{2,3},{3,4},{4,5},{5,6},{6,7},{8,9},{9,10},{10,11},{11... | collective-permute-start | bytes 307208 | tf_op jit(solution)/shard_map/ppermute | solution.py:537
  197.8 5.4 %collective-permute-start.15 = (f32[10,2,1280]{2,1,0:T(2,128)}, f32[10,2,1280]{2,1,0:T(2,128)S(1)}, u32[]{:S(2)}, u32[]{:S(2)}) collective-permute-start(f32[10,2,1280]{2,1,0:T(2,128)} %get-tuple-element.108), channel_id=1, source_target_pairs={{1,0},{2,1},{3,2},{4,3},{5,4},{6,5},{7,6},{9,8},{10,9},{11,10},{12... | collective-permute-start | bytes 307208 | tf_op jit(solution)/shard_map/ppermute | solution.py:538
  199.1 16.1 %collective-permute-start.12 = (bf16[10,2,32,256]{3,2,1,0:T(8,128)(2,1)}, bf16[10,2,32,256]{3,2,1,0:T(8,128)(2,1)S(1)}, u32[]{:S(2)}, u32[]{:S(2)}) collective-permute-start(bf16[10,2,32,256]{3,2,1,0:T(8,128)(2,1)} %get-tuple-element.105), channel_id=1, source_target_pairs={{0,8},{8,16},{16,24},{1,9},{9,17},{17,25},{2,10},{10,18},{18,26},{... | collective-permute-start | bytes 983048 | tf_op jit(solution)/shard_map/ppermute | solution.py:539
  201.7 13.4 %collective-permute-start.13 = (bf16[10,2,32,256]{3,2,1,0:T(8,128)(2,1)}, bf16[10,2,32,256]{3,2,1,0:T(8,128)(2,1)S(1)}, u32[]{:S(2)}, u32[]{:S(2)}) collective-permute-start(bf16[10,2,32,256]{3,2,1,0:T(8,128)(2,1)} %get-tuple-element.106), channel_id=1, source_target_pairs={{8,0},{16,8},{24,16},{9,1},{17,9},{25,17},{10,2},{18,10},{26,18},{... | collective-permute-start | bytes 983048 | tf_op jit(solution)/shard_map/ppermute | solution.py:540
  203.2 7.3 %collective-permute-start.16 = (f32[10,4,256]{2,1,0:T(4,128)S(1)}, f32[10,4,256]{2,1,0:T(4,128)S(1)}, u32[]{:S(2)}, u32[]{:S(2)}) collective-permute-start(f32[10,4,256]{2,1,0:T(4,128)S(1)} %get-tuple-element.136), channel_id=1, source_target_pairs={{0,8},{8,16},{16,24},{1,9},{9,17},{17,25},{2,10},{10,18},{18,26},{... | collective-permute-start | bytes 122888 | tf_op jit(solution)/shard_map/ppermute | solution.py:531
  207.7 7.4 %collective-permute-start.17 = (f32[10,4,256]{2,1,0:T(4,128)S(1)}, f32[10,4,256]{2,1,0:T(4,128)S(1)}, u32[]{:S(2)}, u32[]{:S(2)}) collective-permute-start(f32[10,4,256]{2,1,0:T(4,128)S(1)} %get-tuple-element.135), channel_id=1, source_target_pairs={{8,0},{16,8},{24,16},{9,1},{17,9},{25,17},{10,2},{18,10},{26,18},{... | collective-permute-start | bytes 122888 | tf_op jit(solution)/shard_map/ppermute | solution.py:532
  264.0 4.9 %collective-permute-start.21 = (f32[72,128]{1,0:T(8,128)S(1)}, f32[72,128]{1,0:T(8,128)S(1)}, u32[]{:S(2)}, u32[]{:S(2)}) collective-permute-start(f32[72,128]{1,0:T(8,128)S(1)} %add.38), channel_id=1, source_target_pairs={{0,6},{1,7},{2,4},{3,5},{4,2},{5,3},{6,0},{7,1},{8,14},{9,15},{10,... | collective-permute-start | bytes 110600 | tf_op jit(solution)/shard_map/ppermute | solution.py:515
  268.9 4.6 %collective-permute-start.22 = (f32[72,128]{1,0:T(8,128)S(1)}, f32[72,128]{1,0:T(8,128)S(1)}, u32[]{:S(2)}, u32[]{:S(2)}) collective-permute-start(f32[72,128]{1,0:T(8,128)S(1)} %add_add_fusion.refs_0_), channel_id=1, source_target_pairs={{0,8},{8,0},{16,24},{24,16},{1,9},{9,1},{17,25},{25,17},{2,10},{10... | collective-permute-start | bytes 110600 | tf_op jit(solution)/shard_map/ppermute | solution.py:495
  270.6 4.9 %collective-permute-start.23 = (f32[72,128]{1,0:T(8,128)S(1)}, f32[72,128]{1,0:T(8,128)S(1)}, u32[]{:S(2)}, u32[]{:S(2)}) collective-permute-start(f32[72,128]{1,0:T(8,128)S(1)} %add_add_fusion.refs_0_), channel_id=1, source_target_pairs={{0,16},{8,24},{16,0},{24,8},{1,17},{9,25},{17,1},{25,9},{2,18},{10... | collective-permute-start | bytes 110600 | tf_op jit(solution)/shard_map/ppermute | solution.py:495
  272.1 5.8 %collective-permute-start.24 = (f32[72,128]{1,0:T(8,128)S(1)}, f32[72,128]{1,0:T(8,128)S(1)}, u32[]{:S(2)}, u32[]{:S(2)}) collective-permute-start(f32[72,128]{1,0:T(8,128)S(1)} %add_add_fusion.refs_0_), channel_id=1, source_target_pairs={{0,24},{8,16},{16,8},{24,0},{1,25},{9,17},{17,9},{25,1},{2,26},{10... | collective-permute-start | bytes 110600 | tf_op jit(solution)/shard_map/ppermute | solution.py:495
  (11 other events, 317.7 us)
